TPU v7x, 32 devices: a whole 2x2x4 slice. The times are simulated.
32 devices in a mesh: group: 4 (over x, core), replica: 8 (over z, y).
Axes of the slice: x: 2, y: 2, z: 4, core: 2. Of those that a mesh axis runs over, the one named last changes fastest.
Arguments:
- tokens: bfloat16 [8, 512, 768], P('replica', 'group'), may hold values from -6 to 6
- segment_ids: int32 [8, 512], P('replica'), may hold values from 0 to 3, as said below
- cotangent: bfloat16 [8, 512, 768], P('replica', 'group'), may hold values from -6 to 6
- qkv_weight: bfloat16 [768, 2304], P('group'), may hold values from -0.21875 to 0.21875
- qv_bias: bfloat16 [1536], P('group'), may hold values from -3 to 3
- out_weight: bfloat16 [768, 768], P('group'), may hold values from -0.625 to 0.625
- out_bias: bfloat16 [768], P('group'), may hold values from -3 to 3
- norm1_gain: bfloat16 [768], P('group'), may hold values from 0.099609375 to 1.8984375
- norm1_shift: bfloat16 [768], P('group'), may hold values from -3 to 3
- up_weight: bfloat16 [768, 3072], P('group'), may hold values from -0.21875 to 0.21875
- up_bias: bfloat16 [3072], P('group'), may hold values from -3 to 3
- down_weight: bfloat16 [3072, 768], P('group'), may hold values from -0.15625 to 0.15625
- down_bias: bfloat16 [768], P('group'), may hold values from -3 to 3
- norm2_gain: bfloat16 [768], P('group'), may hold values from 0.099609375 to 1.8984375
- norm2_shift: bfloat16 [768], P('group'), may hold values from -3 to 3
Outputs:
- output: bfloat16 [8, 512, 768], P('replica', 'group')
- grad_tokens: bfloat16 [8, 512, 768], P('replica', 'group')
- grad_qkv_weight: float32 [768, 2304], P('group')
- grad_qv_bias: float32 [1536], P('group')
- grad_out_weight: float32 [768, 768], P('group')
- grad_out_bias: float32 [768], P('group')
- grad_norm1_gain: float32 [768], P('group')
- grad_norm1_shift: float32 [768], P('group')
- grad_up_weight: float32 [768, 3072], P('group')
- grad_up_bias: float32 [3072], P('group')
- grad_down_weight: float32 [3072, 768], P('group')
- grad_down_bias: float32 [768], P('group')
- grad_norm2_gain: float32 [768], P('group')
- grad_norm2_shift: float32 [768], P('group')
Inputs may be any that keep to these rules, and one draw needn't show every extreme that they name: `segment_ids`: within each sequence the numbers never fall; in every sequence one document starts within the first 64 positions and ends within the last 64.
All inputs are finite; a program needn't handle non-finite values.
Results may differ from a plain program's by a relative error of at most 0.018.
Values may be sent and summed in bfloat16 or wider, within the bound.
No kernel may reach another device: no remote copies, remote signals or barrier semaphores. Data moves between devices by JAX's collectives and lax.ppermute only.
A program may use at most 128 MiB of HBM per device.

v0:
```python
from functools import partial

import jax
import jax.numpy as jnp
from jax import lax
from jax.sharding import PartitionSpec as P

H = 12
HD = 64


EPS = 1e-05


def norm_apply(value, gain, shift):
    centre = value - jnp.mean(value, axis=-1, keepdims=True)
    spread = jnp.mean(centre * centre, axis=-1, keepdims=True)
    return centre * lax.rsqrt(spread + EPS) * gain + shift


def on_device(
    tokens,
    segment_ids,
    cotangent,
    qkv_weight,
    qv_bias,
    out_weight,
    out_bias,
    norm1_gain,
    norm1_shift,
    up_weight,
    up_bias,
    down_weight,
    down_bias,
    norm2_gain,
    norm2_shift,
):
    gathered = (
        lax.all_gather(qkv_weight, "group", axis=0, tiled=True),
        lax.all_gather(qv_bias, "group", axis=0, tiled=True),
        lax.all_gather(out_weight, "group", axis=0, tiled=True),
        lax.all_gather(out_bias, "group", axis=0, tiled=True),
        lax.all_gather(norm1_gain, "group", axis=0, tiled=True),
        lax.all_gather(norm1_shift, "group", axis=0, tiled=True),
        lax.all_gather(up_weight, "group", axis=0, tiled=True),
        lax.all_gather(up_bias, "group", axis=0, tiled=True),
        lax.all_gather(down_weight, "group", axis=0, tiled=True),
        lax.all_gather(down_bias, "group", axis=0, tiled=True),
        lax.all_gather(norm2_gain, "group", axis=0, tiled=True),
        lax.all_gather(norm2_shift, "group", axis=0, tiled=True),
    )
    (
        whole_qkv,
        whole_qv,
        whole_out,
        whole_outb,
        whole_gone,
        whole_sone,
        whole_up,
        whole_upb,
        whole_down,
        whole_downb,
        whole_gtwo,
        whole_stwo,
    ) = gathered
    seqcount = tokens.shape[0]
    rowcount = tokens.shape[1]
    width = tokens.shape[2]
    length = segment_ids.shape[1]
    place = lax.axis_index("group")
    my_segments = lax.dynamic_slice_in_dim(segment_ids, place * rowcount, rowcount, 1)
    flat_in = tokens.reshape(seqcount * rowcount, width)
    bias_full = jnp.concatenate(
        [
            whole_qv[:width].astype(jnp.float32),
            jnp.zeros((width,), jnp.float32),
            whole_qv[width:].astype(jnp.float32),
        ]
    )
    projected = (
        jnp.dot(flat_in, whole_qkv, preferred_element_type=jnp.float32) + bias_full
    ).astype(jnp.bfloat16)
    queries = projected[:, :width].reshape(seqcount, rowcount, width)
    keys = projected[:, width : 2 * width].reshape(seqcount, rowcount, width)
    values = projected[:, 2 * width :].reshape(seqcount, rowcount, width)
    all_keys, all_values = (
        lax.all_gather(keys, "group", axis=1, tiled=True),
        lax.all_gather(values, "group", axis=1, tiled=True),
    )
    scale = HD ** (-0.5)
    query_heads = queries.reshape(seqcount, rowcount, H, HD)
    key_heads = all_keys.reshape(seqcount, length, H, HD)
    value_heads = all_values.reshape(seqcount, length, H, HD)
    same = my_segments[:, None, :, None] == segment_ids[:, None, None, :]

    def make_scores():
        raw = (
            jnp.einsum(
                "sqhd,skhd->shqk", query_heads, key_heads, preferred_element_type=jnp.float32
            )
            * scale
        )
        return jnp.where(same, raw, jnp.float32(-1e30))

    scores = make_scores()
    peak = jnp.max(scores, axis=-1, keepdims=True)
    expo = jnp.exp(scores - peak)
    total = jnp.sum(expo, axis=-1, keepdims=True)
    probs = expo / total
    log_total = peak + jnp.log(total)
    probs_low = probs.astype(jnp.bfloat16)
    attended = jnp.einsum(
        "shqk,skhd->sqhd", probs_low, value_heads, preferred_element_type=jnp.float32
    )
    attended_low = attended.reshape(seqcount * rowcount, width).astype(jnp.bfloat16)
    branch = jnp.dot(
        attended_low, whole_out, preferred_element_type=jnp.float32
    ) + whole_outb.astype(jnp.float32)
    first_in = flat_in.astype(jnp.float32) + branch
    normed, norm_one_pull = jax.vjp(
        norm_apply, first_in, whole_gone.astype(jnp.float32), whole_sone.astype(jnp.float32)
    )
    normed_low = normed.astype(jnp.bfloat16)
    pre_act = jnp.dot(normed_low, whole_up, preferred_element_type=jnp.float32) + whole_upb.astype(
        jnp.float32
    )
    activated, gelu_pull = jax.vjp(partial(jax.nn.gelu, approximate=False), pre_act)
    act_low = activated.astype(jnp.bfloat16)
    second = jnp.dot(act_low, whole_down, preferred_element_type=jnp.float32) + whole_downb.astype(
        jnp.float32
    )
    result, norm_two_pull = jax.vjp(
        norm_apply, normed + second, whole_gtwo.astype(jnp.float32), whole_stwo.astype(jnp.float32)
    )
    output = result.astype(jnp.bfloat16).reshape(seqcount, rowcount, width)
    back_qkv, back_out, back_up, back_down = (
        lax.all_gather(qkv_weight, "group", axis=0, tiled=True),
        lax.all_gather(out_weight, "group", axis=0, tiled=True),
        lax.all_gather(up_weight, "group", axis=0, tiled=True),
        lax.all_gather(down_weight, "group", axis=0, tiled=True),
    )
    upstream = cotangent.reshape(seqcount * rowcount, width).astype(jnp.float32)
    d_sum_two, grad_gain_two, grad_shift_two = norm_two_pull(upstream)
    d_second = d_sum_two.astype(jnp.bfloat16)
    grad_downb = jnp.sum(d_second.astype(jnp.float32), axis=0)
    grad_down = jnp.einsum("nf,nd->fd", act_low, d_second, preferred_element_type=jnp.float32)
    d_act = jnp.einsum("nd,fd->nf", d_second, back_down, preferred_element_type=jnp.float32)
    (d_pre,) = gelu_pull(d_act)
    d_pre_low = d_pre.astype(jnp.bfloat16)
    grad_upb = jnp.sum(d_pre_low.astype(jnp.float32), axis=0)
    grad_up = jnp.einsum("nd,nf->df", normed_low, d_pre_low, preferred_element_type=jnp.float32)
    d_normed = d_sum_two + jnp.einsum(
        "nf,df->nd", d_pre_low, back_up, preferred_element_type=jnp.float32
    )
    d_first, grad_gain_one, grad_shift_one = norm_one_pull(d_normed)
    d_branch = d_first.astype(jnp.bfloat16)
    grad_outb = jnp.sum(d_branch.astype(jnp.float32), axis=0)
    grad_out = jnp.einsum("nd,ne->de", attended_low, d_branch, preferred_element_type=jnp.float32)
    d_attended = jnp.einsum("ne,de->nd", d_branch, back_out, preferred_element_type=jnp.float32)
    d_att_heads = d_attended.astype(jnp.bfloat16).reshape(seqcount, rowcount, H, HD)
    again_probs = jnp.exp(make_scores() - log_total)
    d_probs = jnp.einsum(
        "sqhd,skhd->shqk", d_att_heads, value_heads, preferred_element_type=jnp.float32
    )
    inner = jnp.sum(again_probs * d_probs, axis=-1, keepdims=True)
    d_scores = (again_probs * (d_probs - inner)).astype(jnp.bfloat16)
    d_queries = (
        jnp.einsum("shqk,skhd->sqhd", d_scores, key_heads, preferred_element_type=jnp.float32)
        * scale
    )
    d_keys_all = (
        jnp.einsum("shqk,sqhd->skhd", d_scores, query_heads, preferred_element_type=jnp.float32)
        * scale
    )
    d_values_all = jnp.einsum(
        "shqk,sqhd->skhd", probs_low, d_att_heads, preferred_element_type=jnp.float32
    )
    d_keys, d_values = (
        lax.psum_scatter(
            d_keys_all.reshape(seqcount, length, width).astype(jnp.bfloat16),
            "group",
            scatter_dimension=1,
            tiled=True,
        ).astype(jnp.float32),
        lax.psum_scatter(
            d_values_all.reshape(seqcount, length, width).astype(jnp.bfloat16),
            "group",
            scatter_dimension=1,
            tiled=True,
        ).astype(jnp.float32),
    )
    d_proj = jnp.concatenate(
        [
            d_queries.reshape(seqcount * rowcount, width),
            d_keys.reshape(seqcount * rowcount, width),
            d_values.reshape(seqcount * rowcount, width),
        ],
        axis=1,
    ).astype(jnp.bfloat16)
    proj_sums = jnp.sum(d_proj.astype(jnp.float32), axis=0)
    grad_qvb = jnp.concatenate([proj_sums[:width], proj_sums[2 * width :]])
    grad_qkv = jnp.einsum("nd,ne->de", flat_in, d_proj, preferred_element_type=jnp.float32)
    d_input = d_first + jnp.einsum(
        "ne,de->nd", d_proj, back_qkv, preferred_element_type=jnp.float32
    )
    grad_input = d_input.astype(jnp.bfloat16).reshape(seqcount, rowcount, width)
    shared = (
        lax.psum_scatter(
            grad_qkv.astype(jnp.bfloat16), "group", scatter_dimension=0, tiled=True
        ).astype(jnp.float32),
        lax.psum_scatter(
            grad_qvb.astype(jnp.bfloat16), "group", scatter_dimension=0, tiled=True
        ).astype(jnp.float32),
        lax.psum_scatter(
            grad_out.astype(jnp.bfloat16), "group", scatter_dimension=0, tiled=True
        ).astype(jnp.float32),
        lax.psum_scatter(
            grad_outb.astype(jnp.bfloat16), "group", scatter_dimension=0, tiled=True
        ).astype(jnp.float32),
        lax.psum_scatter(
            grad_gain_one.astype(jnp.bfloat16), "group", scatter_dimension=0, tiled=True
        ).astype(jnp.float32),
        lax.psum_scatter(
            grad_shift_one.astype(jnp.bfloat16), "group", scatter_dimension=0, tiled=True
        ).astype(jnp.float32),
        lax.psum_scatter(
            grad_up.astype(jnp.bfloat16), "group", scatter_dimension=0, tiled=True
        ).astype(jnp.float32),
        lax.psum_scatter(
            grad_upb.astype(jnp.bfloat16), "group", scatter_dimension=0, tiled=True
        ).astype(jnp.float32),
        lax.psum_scatter(
            grad_down.astype(jnp.bfloat16), "group", scatter_dimension=0, tiled=True
        ).astype(jnp.float32),
        lax.psum_scatter(
            grad_downb.astype(jnp.bfloat16), "group", scatter_dimension=0, tiled=True
        ).astype(jnp.float32),
        lax.psum_scatter(
            grad_gain_two.astype(jnp.bfloat16), "group", scatter_dimension=0, tiled=True
        ).astype(jnp.float32),
        lax.psum_scatter(
            grad_shift_two.astype(jnp.bfloat16), "group", scatter_dimension=0, tiled=True
        ).astype(jnp.float32),
    )
    summed = lax.psum(
        (
            shared[0],
            shared[1],
            shared[2],
            shared[3],
            shared[4],
            shared[5],
            shared[6],
            shared[7],
            shared[8],
            shared[9],
            shared[10],
            shared[11],
        ),
        "replica",
    )
    return (output, grad_input) + tuple(summed)


def solution(mesh):
    in_specs = (
        P("replica", "group", None),
        P("replica", None),
        P("replica", "group", None),
        P("group", None),
        P("group"),
        P("group", None),
        P("group"),
        P("group"),
        P("group"),
        P("group", None),
        P("group"),
        P("group", None),
        P("group"),
        P("group"),
        P("group"),
    )
    out_specs = (
        P("replica", "group", None),
        P("replica", "group", None),
        P("group", None),
        P("group"),
        P("group", None),
        P("group"),
        P("group"),
        P("group"),
        P("group", None),
        P("group"),
        P("group", None),
        P("group"),
        P("group"),
        P("group"),
    )
    return jax.shard_map(
        on_device, mesh=mesh, in_specs=in_specs, out_specs=out_specs, check_vma=False
    )
```

profile of v0, /device:TPU:0, one launch (start us, length us, event | category | flops | bytes accessed | tf_op | source)
XLA Modules:
  0.0 700.4 jit_solution(16442214825439429237)
XLA Ops:
  12.6 13.1 %all-reduce.16 = (bf16[768]{0:T(1024)(128)(2,1)S(1)}, bf16[768]{0:T(1024)(128)(2,1)S(1)}, bf16[768]{0:T(1024)(128)(2,1)S(1)}, bf16[768]{0:T(1024)(128)(2,1)S(1)}, bf16[768]{0:T(1024)(128)(2,1)S(1)}) all-reduce(bf16[768]{0:T(1024)(128)(2,1)S(1)} %dynamic-update-slice, ...), channel_id=1, replica_groups=mesh['group'=4,'replica'=8] {'group'}, use_global_device_ids=true, to_apply=%add | all-reduce | flops 3840 | bytes 15360
  27.5 5.1 all-gather.2
  32.7 5.2 all-gather.3
  39.3 4.0 all-gather.9.cloned.1.call-done
  43.3 2.6 fusion.1
  46.2 8.6 %all-gather.1 = bf16[512,768]{1,0:T(8,128)(2,1)S(1)} all-gather(bf16[128,768]{1,0:T(8,128)(2,1)S(1)} %get-tuple-element.101), channel_id=3, replica_groups=mesh['group'=4,'replica'=8] {'group'}, dimensions={0}, use_global_device_ids=true | all-gather | bytes 983040 | tf_op jit(solution)/shard_map/all_gather | solution.py:87
  54.8 1.2 copy.45
  55.9 10.0 %all-gather = bf16[512,768]{1,0:T(8,128)(2,1)S(1)} all-gather(bf16[128,768]{1,0:T(8,128)(2,1)S(1)} %get-tuple-element.103), channel_id=2, replica_groups=mesh['group'=4,'replica'=8] {'group'}, dimensions={0}, use_global_device_ids=true | all-gather | bytes 983040 | tf_op jit(solution)/shard_map/all_gather | solution.py:88
  65.9 1.2 copy.43
  67.1 1.9 fusion.38
  69.0 0.8 fusion.2
  70.7 1.1 copy-done
  71.9 1.3 convolution_convert_fusion.6
  73.2 2.2 fusion.39
  77.1 25.3 %all-gather.13.cloned.1.call-done = bf16[768,3072]{1,0:T(8,128)(2,1)} async-done(((bf16[192,3072]{1,0:T(8,128)(2,1)}), bf16[768,3072]{1,0:T(8,128)(2,1)}) %all-gather.13.cloned.1.call-update) | async-done | bytes 4718608 | tf_op jit(solution)/shard_map/all_gather | solution.py:45
  102.4 8.5 %multiply_convert_fusion.2 = (bf16[128,3072]{1,0:T(8,128)(2,1)}, f32[128,3072]{1,0:T(8,128)}, f32[128,3072]{1,0:T(8,128)}) fusion(f32[3072]{0:T(1024)} %bitcast.124, bf16[768,3072]{1,0:T(8,128)(2,1)} %all-gather.13.cloned.1.call-done, f32[128,768]{1,0:T(8,128)S(1)} %get-tuple-element.111, f32[768]{0:T(1024)S(1)} %convert_element_type.208, ...), kind=kOutput, calls=%fused_computation.18 | convolution fusion | flops 630423552 | bytes 9063424 | tf_op jit(solution)/shard_map/dot_general | solution.py:124
  111.0 30.4 %all-gather.15.cloned.1.call-done = bf16[3072,768]{1,0:T(8,128)(2,1)} async-done(((bf16[768,768]{1,0:T(8,128)(2,1)}), bf16[3072,768]{1,0:T(8,128)(2,1)}) %all-gather.15.cloned.1.call-update) | async-done | bytes 4718608 | tf_op jit(solution)/shard_map/all_gather | solution.py:47
  141.4 3.6 fusion.40
  147.0 2.5 fusion.30
  149.6 2.4 multiply_reduce_fusion.1
  154.4 1.2 convolution_convert_fusion.5
  155.6 1.7 copy.46
  157.3 2.8 convolution_convert_fusion.4
  160.1 4.7 copy.50
  164.8 2.4 copy.58
  168.2 2.3 multiply_reduce_fusion
  171.3 1.1 copy-done.1
  172.9 1.6 copy.48
  174.5 1.0 copy.59
  175.7 1.5 convolution_convert_fusion.3
  178.0 12.6 %reduce-scatter.21.cloned.1.call-done = bf16[128,768]{1,0:T(8,128)(2,1)} async-done(((bf16[512,768]{1,0:T(8,128)(2,1)}), bf16[128,768]{1,0:T(8,128)(2,1)}) %reduce-scatter.21.cloned.1.call-update) | async-done | bytes 196624
  190.6 1.1 reshape_bitcast_fusion
  192.2 24.3 %reduce-scatter.19.cloned.1.call-done = bf16[128,768]{1,0:T(8,128)(2,1)} async-done(((bf16[512,768]{1,0:T(8,128)(2,1)}), bf16[128,768]{1,0:T(8,128)(2,1)}) %reduce-scatter.19.cloned.1.call-update) | async-done | bytes 196624
  216.5 1.1 reshape_bitcast_fusion.1
  218.0 2.8 fusion
  220.9 5.9 copy.52
  226.8 1.1 copy-done.10
  227.9 3.7 convolution_convert_fusion.1
  231.6 1.1 copy-done.7
  232.7 3.6 convolution_convert_fusion
  239.2 10.8 %all-reduce.15 = (bf16[768]{0:T(1024)(128)(2,1)S(1)}, bf16[1536]{0:T(1024)(128)(2,1)S(1)}, bf16[768]{0:T(1024)(128)(2,1)S(1)}, bf16[768]{0:T(1024)(128)(2,1)S(1)...) all-reduce(bf16[768]{0:T(1024)(128)(2,1)S(1)} %dynamic-update-slice, ...), channel_id=1, replica_groups=mesh['group'=4,'replica'=8] {'group'}, use_global_device_ids=true, to_apply=%add.5 | all-reduce | flops 9984 | bytes 39936
  251.3 4.0 fusion.13
  255.2 33.5 %reduce-scatter.23.cloned.1.call-done = bf16[192,2304]{1,0:T(8,128)(2,1)} async-done(((bf16[768,2304]{1,0:T(8,128)(2,1)}), bf16[192,2304]{1,0:T(8,128)(2,1)}) %reduce-scatter.23.cloned.1.call-update) | async-done | bytes 884752
  288.8 1.5 copy.53
  290.3 48.9 %reduce-scatter.15.cloned.1.call-done = bf16[192,3072]{1,0:T(8,128)(2,1)} async-done(((bf16[768,3072]{1,0:T(8,128)(2,1)}), bf16[192,3072]{1,0:T(8,128)(2,1)}) %reduce-scatter.15.cloned.1.call-update) | async-done | bytes 1179664 | tf_op jit(solution)/shard_map/reduce_scatter | solution.py:226
  339.2 50.4 %reduce-scatter.17.cloned.1.call-done = bf16[768,768]{1,0:T(8,128)(2,1)} async-done(((bf16[3072,768]{1,0:T(8,128)(2,1)}), bf16[768,768]{1,0:T(8,128)(2,1)}) %reduce-scatter.17.cloned.1.call-update) | async-done | bytes 1179664 | tf_op jit(solution)/shard_map/reduce_scatter | solution.py:232
  389.6 301.1 %all-reduce.18 = (f32[192,2304]{0,1:T(8,128)}, f32[384]{0:T(512)}, f32[192,768]{1,0:T(8,128)}, f32[192]{0:T(256)}, f32[192]{0:T(256)}, /*index=5*/f32[192]{0:T(2...) all-reduce(bf16[192,2304]{0,1:T(8,128)(2,1)S(1)} %copy.53, ...), channel_id=1, replica_groups=mesh['group'=4,'replica'=8] {'replica'}, use_global_device_ids=true, to_apply=%region_14.15 | all-reduce | flops 1771776 | bytes 10635264 | tf_op jit(solution)/shard_map/psum | solution.py:245
  690.6 2.9 copy.47
  (211 shorter events, 20.9 us)
Async XLA Ops:
  7.2 3.0 copy-start.45
  7.2 3.0 copy-start.47
  7.2 36.1 %all-gather.9.cloned.1.call-start = ((), (), s32[]{:S(2)}) async-start(), calls=%async_computation.6 | async-start | bytes 4423680 | tf_op jit(solution)/shard_map/all_gather | solution.py:39
  7.9 3.5 copy-start.52
  7.9 3.7 copy-start.53
  8.0 4.0 copy-start.54
  8.0 4.2 copy-start.55
  8.0 4.4 copy-start.56
  8.0 18.3 %copy-start.46 = (bf16[768]{0:T(1024)(128)(2,1)S(1)}, bf16[768]{0:T(1024)(128)(2,1)}, u32[]{:S(2)}) copy-start(bf16[768]{0:T(1024)(128)(2,1)} %param.25) | copy-start | bytes 4612
  8.0 30.5 %copy-start.44 = (s32[1,512]{1,0:T(1,128)S(1)}, s32[1,512]{1,0:T(1,128)}, u32[]{:S(2)}) copy-start(s32[1,512]{1,0:T(1,128)} %param.16) | copy-start | bytes 6148
  8.0 35.3 %copy-start.11 = (bf16[1,128,768]{2,1,0:T(8,128)(2,1)S(1)}, bf16[1,128,768]{2,1,0:T(8,128)(2,1)}, u32[]{:S(2)}) copy-start(bf16[1,128,768]{2,1,0:T(8,128)(2,1)} %param.15) | copy-start | bytes 589828
  8.0 65.2 %all-gather.11.cloned.1.call-start = ((), (), s32[]{:S(2)}) async-start(), calls=%async_computation.7 | async-start | bytes 1474560 | tf_op jit(solution)/shard_map/all_gather | solution.py:41
  8.8 93.6 %all-gather.13.cloned.1.call-start = ((), (), s32[]{:S(2)}) async-start(), calls=%async_computation.8 | async-start | bytes 5898240 | tf_op jit(solution)/shard_map/all_gather | solution.py:45
  9.5 131.8 %all-gather.15.cloned.1.call-start = ((), (), s32[]{:S(2)}) async-start(), calls=%async_computation.9 | async-start | bytes 5898240 | tf_op jit(solution)/shard_map/all_gather | solution.py:47
  10.1 180.5 %reduce-scatter.21.cloned.1.call-start = ((), (), s32[]{:S(2)}) async-start(), calls=%async_computation.14 | async-start | bytes 983040
  46.1 21.0 %copy-start.13 = (bf16[128,768]{0,1:T(8,128)(2,1)}, bf16[128,768]{0,1:T(8,128)(2,1)S(1)}, u32[]{:S(2)}) copy-start(bf16[128,768]{0,1:T(8,128)(2,1)S(1)} %copy.44) | copy-start | bytes 589828
  55.9 11.2 %copy-start.25 = (pred[128,512]{1,0:T(8,128)(4,1)S(1)}, pred[128,512]{1,0:T(8,128)(4,1)}, u32[]{:S(2)}) copy-start(pred[128,512]{1,0:T(8,128)(4,1)} %broadcast_compare_fusion) | copy-start | bytes 196612
  141.4 5.6 slice-start.2
  141.4 3.9 copy-start.18
  141.4 3.9 copy-start.27
  141.4 5.6 slice-start.3
  141.4 5.6 copy-start.59
  146.3 3.3 slice-start
  147.0 2.6 copy-start.22
  147.0 2.5 slice-start.1
  147.0 2.5 copy-start.30
  147.0 2.5 copy-start.32
  149.5 2.4 copy-start.9
  152.0 2.4 copy-start.8
  167.2 49.2 %reduce-scatter.19.cloned.1.call-start = ((), (), s32[]{:S(2)}) async-start(), calls=%async_computation.13 | async-start | bytes 983040
  175.5 79.7 %reduce-scatter.13.cloned.1.call-start = ((), (), s32[]{:S(2)}) async-start(), calls=%async_computation.10 | async-start | bytes 1474560 | tf_op jit(solution)/shard_map/reduce_scatter | solution.py:214
  177.2 111.6 %reduce-scatter.23.cloned.1.call-start = ((), (), s32[]{:S(2)}) async-start(), calls=%async_computation.15 | async-start | bytes 4423680
  178.0 40.0 %copy-start.12 = (bf16[1,128,768]{2,1,0:T(8,128)(2,1)S(1)}, bf16[1,128,768]{2,1,0:T(8,128)(2,1)}, u32[]{:S(2)}) copy-start(bf16[1,128,768]{2,1,0:T(8,128)(2,1)} %param.15) | copy-start | bytes 589828
  226.8 112.4 %reduce-scatter.15.cloned.1.call-start = ((), (), s32[]{:S(2)}) async-start(), calls=%async_computation.11 | async-start | bytes 5898240 | tf_op jit(solution)/shard_map/reduce_scatter | solution.py:226
  231.6 158.0 %reduce-scatter.17.cloned.1.call-start = ((), (), s32[]{:S(2)}) async-start(), calls=%async_computation.12 | async-start | bytes 5898240 | tf_op jit(solution)/shard_map/reduce_scatter | solution.py:232
  236.3 2.8 copy-start.34
  236.3 2.8 copy-start.35
  236.3 2.8 copy-start.36
  236.3 2.8 copy-start.37
  236.4 2.8 copy-start.38
  236.4 2.8 copy-start.41
  236.4 14.1 %copy-start.4 = (f32[128,768]{1,0:T(8,128)S(1)}, f32[128,768]{1,0:T(8,128)}, u32[]{:S(2)}) copy-start(f32[128,768]{1,0:T(8,128)} %copy-done.3) | copy-start | bytes 1179652
  236.4 14.0 %copy-start.28 = (f32[768]{0:T(1024)S(1)}, f32[768]{0:T(1024)}, u32[]{:S(2)}) copy-start(f32[768]{0:T(1024)} %convert_element_type.213) | copy-start | bytes 9220
  236.4 14.0 %copy-start.40 = (f32[128]{0:T(128)S(1)}, f32[128]{0:T(128)}, u32[]{:S(2)}) copy-start(f32[128]{0:T(128)} %copy-done.39) | copy-start | bytes 1540
  236.4 14.0 %copy-start.43 = (f32[128]{0:T(128)S(1)}, f32[128]{0:T(128)}, u32[]{:S(2)}) copy-start(f32[128]{0:T(128)} %copy-done.42) | copy-start | bytes 1540
  236.4 14.8 %copy-start.21 = (f32[128,768]{1,0:T(8,128)S(1)}, f32[128,768]{1,0:T(8,128)}, u32[]{:S(2)}) copy-start(f32[128,768]{1,0:T(8,128)} %copy-done.20) | copy-start | bytes 1179652
  236.4 14.8 %copy-start.51 = (f32[128]{0:T(128)S(1)}, f32[128]{0:T(128)}, u32[]{:S(2)}) copy-start(f32[128]{0:T(128)} %copy-done.50) | copy-start | bytes 1540
  255.2 134.3 %copy-start.24 = (bf16[192,768]{1,0:T(8,128)(2,1)S(1)}, bf16[192,768]{1,0:T(8,128)(2,1)}, u32[]{:S(2)}) copy-start(bf16[192,768]{1,0:T(8,128)(2,1)} %reduce-scatter.13.cloned.1.call-done) | copy-start | bytes 884740
  (26 other events, 36.5 us)
Sparse Core Ops, SparseCore 0:
  9.6 33.6 all-gather.8
  44.8 18.4 all-gather.10
  64.9 37.4 all-gather.12
  103.8 37.4 all-gather.14
  167.4 23.2 reduce-scatter.20
  193.2 23.2 reduce-scatter.18
  219.6 25.8 reduce-scatter.12
  248.3 40.4 reduce-scatter.22
  291.3 47.8 reduce-scatter.14
  341.7 47.8 reduce-scatter.16
where the time goes:
time: 701 us; the launch traced here: 700 us
  blocking collectives  354 us (50%)
  waiting for transfers between devices  232 us (33%)
  matrix products  47.8 us (7%)
  local copies, waits for them, and re-layouts  36.8 us (5%)
  between operations  17.8 us (3%)
  other arithmetic  11.4 us (2%)
    psum x1, blocking collectives, on_device(): lax.psum((shared[0], shared[1], shared[2], shared[3], shared[4], shared[5...  301 us
    unnamed x13, waiting for transfers between devices  73.1 us
    reduce_scatter x1, waiting for transfers between devices, on_device(): lax.psum_scatter(grad_down.astype(jnp.bfloat16), 'group', scatter_dimensi...  50.4 us
    reduce_scatter x1, waiting for transfers between devices, on_device(): lax.psum_scatter(grad_up.astype(jnp.bfloat16), 'group', scatter_dimension...  48.9 us
    unnamed x154, local copies, waits for them, and re-layouts  32.5 us
    all_gather x1, waiting for transfers between devices, on_device(): lax.all_gather(down_weight, 'group', axis=0, tiled=True)  30.4 us
    all_gather x1, waiting for transfers between devices, on_device(): lax.all_gather(up_weight, 'group', axis=0, tiled=True)  25.3 us
    unnamed x2, blocking collectives  23.9 us
  transfers between devices with their start and end apart: 10, of which 8 were waited for; matrix products, arithmetic and copies ran while one was open for 9% of the time, Pallas kernels for 0%

commit v1 on v0

v1 whole, which is shorter than its diff:
```python
from functools import partial

import jax
import jax.numpy as jnp
from jax import lax
from jax.sharding import PartitionSpec as P

HD = 64
G = 4
EPS = 1e-05
BF = jnp.bfloat16
F32 = jnp.float32


def gx(value, bits):
    return lax.ppermute(value, "group", [(i, i ^ bits) for i in range(G)])


def rx(value, bits, count):
    return lax.ppermute(value, "replica", [(i, i ^ bits) for i in range(count)])


def dot(a, b):
    return jnp.dot(a, b, preferred_element_type=F32)


def dot_t(a, b):
    return lax.dot_general(a, b, (((1,), (1,)), ((), ())), preferred_element_type=F32)


def t_dot(a, b):
    return lax.dot_general(a, b, (((0,), (0,)), ((), ())), preferred_element_type=F32)


def xor_order(items, place):
    count = len(items)
    bit = 1
    while bit < count:
        on = (place & bit) != 0
        items = [jnp.where(on, items[i ^ bit], items[i]) for i in range(count)]
        bit *= 2
    return items


def gather_rows(own):
    far = gx(own, 2)
    near = gx(own, 1)
    return own, near, far, gx(far, 1)


def scatter_rows(parts):
    far = parts[2] + gx(parts[3].astype(BF), 1).astype(F32)
    far = gx(far.astype(BF), 2)
    near = gx(parts[1].astype(BF), 1)
    return parts[0] + near.astype(F32) + far.astype(F32)


def replica_scatter(value, order, me, count):
    top = count.bit_length() - 1
    rest = value.shape[1:]
    value = value.reshape((2,) * top + rest)
    left = list(range(top - 1, -1, -1))
    for bit in order:
        axis = left.index(bit)
        mine = (me >> bit) & 1
        other = lax.dynamic_index_in_dim(value, 1 - mine, axis, keepdims=False)
        keep = lax.dynamic_index_in_dim(value, mine, axis, keepdims=False)
        got = rx(other, 1 << bit, count)
        value = (keep.astype(F32) + got.astype(F32)).astype(BF)
        left.remove(bit)
    return value


def replica_gather(value, order, me, count):
    top = count.bit_length() - 1
    rest = value.shape
    left = []
    for bit in reversed(order):
        got = rx(value, 1 << bit, count)
        on = ((me >> bit) & 1) != 0
        left = sorted(left + [bit], reverse=True)
        axis = left.index(bit)
        value = jnp.stack([jnp.where(on, got, value), jnp.where(on, value, got)], axis=axis)
    return value.reshape((count,) + rest)


def norm_parts(value):
    centre = value - jnp.mean(value, axis=-1, keepdims=True)
    spread = jnp.mean(centre * centre, axis=-1, keepdims=True)
    scale = lax.rsqrt(spread + EPS)
    return centre * scale, scale


def norm_back(upstream, hat, scale, gain):
    scaled = upstream * gain
    first = jnp.mean(scaled, axis=-1, keepdims=True)
    second = jnp.mean(scaled * hat, axis=-1, keepdims=True)
    return scale * (scaled - first - hat * second)


def on_device(
    replicas,
    tokens,
    segment_ids,
    cotangent,
    qkv_weight,
    qv_bias,
    out_weight,
    out_bias,
    norm1_gain,
    norm1_shift,
    up_weight,
    up_bias,
    down_weight,
    down_bias,
    norm2_gain,
    norm2_shift,
):
    place = lax.axis_index("group")
    me = lax.axis_index("replica")
    rows, width = tokens.shape[1], tokens.shape[2]
    part = width // G
    hidden = up_weight.shape[1] // G
    heads = part // HD
    bits = list(range(replicas.bit_length() - 1))
    order_a = bits
    order_b = bits[1:] + bits[:1]

    own_x = tokens[0]
    x_blocks = gather_rows(own_x)
    qkv_by_dest = qkv_weight.reshape(part, 3, G, part)
    qkv_rows = [
        lax.dynamic_index_in_dim(qkv_by_dest, place ^ k, 2, keepdims=False).reshape(part, 3 * part)
        for k in range(G)
    ]
    qkv_rows = [qkv_rows[0]] + [gx(qkv_rows[k], k) for k in range(1, G)]
    small = jnp.concatenate(
        [qv_bias, out_bias, norm1_gain, norm1_shift, down_bias, norm2_gain, norm2_shift]
    ).reshape(1, -1)
    small = jnp.concatenate(xor_order(list(gather_rows(small)), place), axis=0).astype(F32)
    qv = small[:, : 2 * part].reshape(2, width)
    vectors = small[:, 2 * part :].reshape(G, 6, part).transpose(1, 0, 2).reshape(6, width)
    out_b, gain1, shift1, down_b, gain2, shift2 = [vectors[i] for i in range(6)]
    up_rows = [
        lax.dynamic_slice_in_dim(up_weight, (place ^ k) * hidden, hidden, 1) for k in range(G)
    ]
    up_rows = [up_rows[0]] + [gx(up_rows[k], k) for k in range(1, G)]
    up_bias = up_bias.astype(F32)

    qkv_local = jnp.concatenate(xor_order(qkv_rows, place), axis=0)
    up_local = jnp.concatenate(xor_order(up_rows, place), axis=0)
    own_qv = lax.dynamic_slice_in_dim(qv, place * part, part, 1)
    bias = jnp.concatenate([own_qv[0], jnp.zeros((part,), F32), own_qv[1]])
    segs = segment_ids.reshape(G, rows)
    segs = jnp.concatenate(
        [lax.dynamic_index_in_dim(segs, place ^ k, 0, keepdims=False) for k in range(G)]
    )
    same = segs[:, None] == segs[None, :]

    x_all = jnp.concatenate(x_blocks, axis=0)
    proj = (dot(x_all, qkv_local) + bias).astype(BF)
    scale = HD**-0.5
    attended, kept = [], []
    for h in range(heads):
        q = proj[:, h * HD : (h + 1) * HD]
        k = proj[:, part + h * HD : part + (h + 1) * HD]
        v = proj[:, 2 * part + h * HD : 2 * part + (h + 1) * HD]
        scores = jnp.where(same, dot_t(q, k) * scale, jnp.float32(-1e30))
        peak = jnp.max(scores, axis=-1, keepdims=True)
        expo = jnp.exp(scores - peak)
        probs = expo / jnp.sum(expo, axis=-1, keepdims=True)
        low = probs.astype(BF)
        attended.append(dot(low, v).astype(BF))
        kept.append((q, k, v, probs, low))
    attended = jnp.concatenate(attended, axis=1)
    branch = dot(attended, out_weight)
    branch = scatter_rows([branch[k * rows : (k + 1) * rows] for k in range(G)])
    first = own_x.astype(F32) + branch + out_b
    hat1, scale1 = norm_parts(first)
    normed = hat1 * gain1 + shift1
    normed_low = jnp.concatenate(gather_rows(normed.astype(BF)), axis=0)
    pre = dot(normed_low, up_local) + up_bias
    cdf = 0.5 * (1.0 + lax.erf(pre * (0.5**0.5)))
    act = (pre * cdf).astype(BF)
    slope = cdf + pre * jnp.exp(-0.5 * pre * pre) * ((2 * jnp.pi) ** -0.5)
    second = dot(act, down_weight)
    second = scatter_rows([second[k * rows : (k + 1) * rows] for k in range(G)])
    hat2, scale2 = norm_parts(normed + second + down_b)
    output = (hat2 * gain2 + shift2).astype(BF)

    up_stream = cotangent[0].astype(F32)
    d_sum = norm_back(up_stream, hat2, scale2, gain2)
    d_second = d_sum.astype(BF)
    vec_gain2 = jnp.sum(up_stream * hat2, axis=0)
    vec_shift2 = jnp.sum(up_stream, axis=0)
    vec_down = jnp.sum(d_second.astype(F32), axis=0)
    d_second_all = jnp.concatenate(gather_rows(d_second), axis=0)
    grad_down = t_dot(act, d_second_all).astype(BF)
    d_pre = (dot_t(d_second_all, down_weight) * slope).astype(BF)
    vec_up = jnp.sum(d_pre.astype(F32), axis=0)
    grad_up = t_dot(normed_low, d_pre).astype(BF)
    d_normed = dot_t(d_pre, up_local)
    d_normed = d_sum + scatter_rows([d_normed[k * rows : (k + 1) * rows] for k in range(G)])

    down_piece = replica_scatter(grad_down.reshape(replicas, -1, width), order_a, me, replicas)
    grad_down = replica_gather(down_piece, order_a, me, replicas).reshape(hidden, width)
    cut = part // replicas

    def column_grad(value, order):
        columns = value.shape[1]
        pieces = value.reshape(G, replicas, cut, columns).transpose(1, 0, 2, 3)
        mine = replica_scatter(pieces, order, me, replicas)
        mine = [lax.dynamic_index_in_dim(mine, place ^ k, 0, keepdims=False) for k in range(G)]
        mine = [mine[0]] + [gx(mine[k], k) for k in range(1, G)]
        whole = replica_gather(jnp.stack(mine), order, me, replicas)
        whole = xor_order([whole[:, k].reshape(part, columns).astype(F32) for k in range(G)], place)
        return jnp.stack(whole, axis=1)

    grad_up = column_grad(grad_up, order_b).reshape(part, G * hidden)

    d_first = norm_back(d_normed, hat1, scale1, gain1)
    vec_gain1 = jnp.sum(d_normed * hat1, axis=0)
    vec_shift1 = jnp.sum(d_normed, axis=0)
    d_branch = d_first.astype(BF)
    vec_out = jnp.sum(d_branch.astype(F32), axis=0)
    d_branch_all = jnp.concatenate(gather_rows(d_branch), axis=0)
    grad_out = t_dot(attended, d_branch_all).astype(BF)
    out_piece = replica_scatter(grad_out.reshape(replicas, -1, width), order_a, me, replicas)
    grad_out = replica_gather(out_piece, order_a, me, replicas).reshape(part, width)
    d_att = dot_t(d_branch_all, out_weight).astype(BF)
    d_q, d_k, d_v = [], [], []
    for h in range(heads):
        q, k, v, probs, low = kept[h]
        d_o = d_att[:, h * HD : (h + 1) * HD]
        d_probs = dot_t(d_o, v)
        inner = jnp.sum(probs * d_probs, axis=-1, keepdims=True)
        d_scores = (probs * (d_probs - inner)).astype(BF)
        d_q.append((dot(d_scores, k) * scale).astype(BF))
        d_k.append((t_dot(d_scores, q) * scale).astype(BF))
        d_v.append(t_dot(low, d_o).astype(BF))
    d_proj = jnp.concatenate(d_q + d_k + d_v, axis=1)
    sums = jnp.sum(d_proj.astype(F32), axis=0)
    grad_qkv = t_dot(x_all, d_proj).astype(BF)
    half = 3 * part // 2
    grad_qkv = jnp.concatenate(
        [
            column_grad(grad_qkv[:, :half], order_a),
            column_grad(grad_qkv[:, half:], order_b),
        ],
        axis=2,
    )
    grad_qkv = grad_qkv.reshape(part, G, 3, part).transpose(0, 2, 1, 3).reshape(part, 3 * width)
    d_in = dot_t(d_proj, qkv_local)
    d_in = d_first + scatter_rows([d_in[k * rows : (k + 1) * rows] for k in range(G)])
    grad_tokens = d_in.astype(BF)

    vecs = jnp.concatenate(
        [
            jnp.stack([vec_out, vec_gain1, vec_shift1, vec_down, vec_gain2, vec_shift2]).reshape(-1),
            lax.dynamic_update_slice_in_dim(jnp.zeros((G * hidden,), F32), vec_up, place * hidden, 0),
            lax.dynamic_update_slice_in_dim(
                jnp.zeros((3, width), F32), sums.reshape(3, part), place * part, 1
            ).reshape(-1),
        ]
    ).reshape(-1, width)
    for bit in range(2):
        vecs = vecs + gx(vecs, 1 << bit)
    for bit in bits:
        vecs = vecs + rx(vecs, 1 << bit, replicas)
    six = lax.dynamic_slice_in_dim(vecs[:6], place * part, part, 1)
    vec_up = lax.dynamic_slice_in_dim(vecs[6 : 6 + G].reshape(-1), place * hidden, hidden, 0)
    qvs = jnp.concatenate([vecs[6 + G], vecs[8 + G]])
    vec_qv = lax.dynamic_slice_in_dim(qvs, place * 2 * part, 2 * part, 0)
    return (
        output[None],
        grad_tokens[None],
        grad_qkv,
        vec_qv,
        grad_out.astype(F32),
        six[0],
        six[1],
        six[2],
        grad_up,
        vec_up,
        grad_down.astype(F32),
        six[3],
        six[4],
        six[5],
    )


def solution(mesh):
    rows = P("replica", "group", None)
    flat = P("group")
    matrix = P("group", None)
    in_specs = (
        rows,
        P("replica", None),
        rows,
        matrix,
        flat,
        matrix,
        flat,
        flat,
        flat,
        matrix,
        flat,
        matrix,
        flat,
        flat,
        flat,
    )
    out_specs = (
        rows,
        rows,
        matrix,
        flat,
        matrix,
        flat,
        flat,
        flat,
        matrix,
        flat,
        matrix,
        flat,
        flat,
        flat,
    )
    return jax.shard_map(
        partial(on_device, mesh.shape["replica"]),
        mesh=mesh,
        in_specs=in_specs,
        out_specs=out_specs,
        check_vma=False,
    )
```

time: 701 us -> 309 us (0.44)
  blocking collectives: 354 us -> 0 us
  waiting for transfers between devices: 232 us -> 111 us
  starting transfers between devices: 0.62 us -> 60.3 us
  local copies, waits for them, and re-layouts: 36.8 us -> 66.6 us
  other arithmetic: 11.4 us -> 35.3 us
  matrix products: 47.8 us -> 30.8 us
  between operations: 17.8 us -> 2.51 us
    psum x1 -> x0, blocking collectives: 301 us -> none  [on_device(): lax.psum((shared[0], shared[1], shared[2], shared[3], shared[4], shared[5...]
    ppermute x0 -> x77, waiting for transfers between devices: none -> 111 us  [the longest x33 61.1 us: rx(): return lax.ppermute(value, 'replica', [(i, i ^ bits) for i in range(count)])]
    reduce_scatter x3 -> x0, waiting for transfers between devices: 99.3 us -> none  [the longest x1 50.4 us: on_device(): lax.psum_scatter(grad_down.astype(jnp.bfloat16), 'group', scatter_dimensi...]
    unnamed x13 -> x0, waiting for transfers between devices: 73.1 us -> none
    ppermute x0 -> x77, starting transfers between devices: none -> 60.3 us  [the longest x33 35.9 us: rx(): return lax.ppermute(value, 'replica', [(i, i ^ bits) for i in range(count)])]
    all_gather x4 -> x0, waiting for transfers between devices: 59.7 us -> none  [the longest x1 30.4 us: on_device(): lax.all_gather(down_weight, 'group', axis=0, tiled=True)]
    all_gather x4 -> x0, blocking collectives: 29 us -> none  [the longest x1 10 us: on_device(): lax.all_gather(values, 'group', axis=1, tiled=True)]
    unnamed x2 -> x0, blocking collectives: 23.9 us -> none
  transfers between devices with their start and end apart: 10 -> 77, of which waited for: 8 -> 28; matrix products, arithmetic and copies ran while one was open for 9% -> 31% of each run, Pallas kernels for 0% -> 0%
where the time goes in v1:
time: 309 us; the launch traced here: 306 us
  waiting for transfers between devices  111 us (36%)
  local copies, waits for them, and re-layouts  66.6 us (22%)
  starting transfers between devices  60.3 us (20%)
  other arithmetic  35.3 us (11%)
  matrix products  30.8 us (10%)
    ppermute x33, waiting for transfers between devices, rx(): return lax.ppermute(value, 'replica', [(i, i ^ bits) for i in range(count)])  61.1 us
    ppermute x44, waiting for transfers between devices, gx(): return lax.ppermute(value, 'group', [(i, i ^ bits) for i in range(G)])  49.6 us
    ppermute x33, starting transfers between devices, rx(): return lax.ppermute(value, 'replica', [(i, i ^ bits) for i in range(count)])  35.9 us
    ppermute x44, starting transfers between devices, gx(): return lax.ppermute(value, 'group', [(i, i ^ bits) for i in range(G)])  24.4 us
    dynamic_update_slice x1, local copies, waits for them, and re-layouts, on_device(): lax.dynamic_update_slice_in_dim(jnp.zeros((G * hidden,), F32), vec_up, pl...  13.1 us
    dot_general x10, matrix products, dot_t(): lax.dot_general(a, b, (((1,), (1,)), ((), ())), preferred_element_type=F32)  11.9 us
    unnamed x149, local copies, waits for them, and re-layouts  11.8 us
    dot_general x10, matrix products, dot(): return jnp.dot(a, b, preferred_element_type=F32)  9.46 us
  transfers between devices with their start and end apart: 77, of which 28 were waited for; matrix products, arithmetic and copies ran while one was open for 31% of the time, Pallas kernels for 0%

profile of v1, /device:TPU:0, one launch (start us, length us, event | category | flops | bytes accessed | tf_op | source)
XLA Modules:
  0.0 306.2 jit_solution(18327568884617517982)
XLA Ops:
  0.7 4.9 %concatenate.48 = bf16[1536]{0:T(1024)(128)(2,1)S(1)} concatenate(bf16[384]{0:T(512)(128)(2,1)} %param.19, bf16[192]{0:T(256)(128)(2,1)} %param.21, bf16[192]{0:T(256)(128)(2,1)} %param.22, bf16[192]{0:T(256)(128)(2,1)} %param.23, bf16[192]{0:T(256)(128)(2,1)} %param.27, bf16[192]{0:T(256)(128)(2,1)} %param.28, bf16[192]{0:T(256)(128)(2,1)} %param.29), dimensions={0} | concatenate | bytes 6144 | tf_op jit(solution)/shard_map/concatenate | solution.py:137
  6.6 2.5 collective-permute-start.6
  9.3 2.9 reshape.608
  12.3 3.4 %constant_dynamic-slice_fusion.12 = (bf16[192,3,1,192]{3,2,1,0:T(2,128)(2,1)}, bf16[192,3,1,192]{3,2,1,0:T(2,128)(2,1)S(1)}, bf16[192,3,1,192]{3,2,1,0:T(2,128)(2,1)S(1)}, bf16[192,3,1,192]{3,2,1,0:T(2,128)(2,1)}) fusion(bf16[192,3,4,192]{3,2,1,0:T(4,128)(2,1)S(1)} %reshape.608, s32[]{:T(128)S(6)} %select_n.780, s32[]{:T(128)S(6)} %select_n.781, ...), kind=kLoop, calls=%fused_computation.317 | loop fusion | bytes 1769488 | tf_op jit(solution)/shard_map/jit(dynamic_index_in_dim)/dynamic_slice | solution.py:133
  17.1 1.9 collective-permute-start.3
  24.5 1.9 collective-permute-done.3
  26.4 6.5 %collective-permute-done.4 = bf16[192,576]{0,1:T(8,128)(2,1)S(1)} collective-permute-done((bf16[192,576]{0,1:T(8,128)(2,1)S(1)}, bf16[192,576]{0,1:T(8,128)(2,1)S(1)}, u32[]{:S(2)}, u32[]{:S(2)}) %collective-permute-start.4) | collective-permute-done | bytes 221216 | tf_op jit(solution)/shard_map/ppermute | solution.py:16
  34.1 2.1 fusion.6
  48.9 1.7 collective-permute-start.11
  51.0 14.4 %collective-permute-done.11 = bf16[128,768]{1,0:T(8,128)(2,1)} collective-permute-done((bf16[128,768]{1,0:T(8,128)(2,1)S(1)}, bf16[128,768]{1,0:T(8,128)(2,1)}, u32[]{:S(2)}, u32[]{:S(2)}) %collective-permute-start.11) | collective-permute-done | bytes 196640 | tf_op jit(solution)/shard_map/ppermute | solution.py:16
  69.4 4.7 %collective-permute-done.13 = bf16[128,768]{1,0:T(8,128)(2,1)} collective-permute-done((bf16[128,768]{1,0:T(8,128)(2,1)}, bf16[128,768]{1,0:T(8,128)(2,1)}, u32[]{:S(2)}, u32[]{:S(2)}) %collective-permute-start.13) | collective-permute-done | bytes 196640 | tf_op jit(solution)/shard_map/ppermute | solution.py:16
  77.1 3.4 %multiply_convert_fusion = (bf16[512,768]{1,0:T(8,128)(2,1)S(1)}, f32[512,768]{1,0:T(8,128)}) fusion(f32[768]{0:T(1024)S(1)} %convert_element_type.658, bf16[192,768]{1,0:T(8,128)(2,1)S(1)} %get-tuple-element.42, bf16[192,768]{1,0:T(8,128)(2,1)S(1)} %get-tuple-element.41, bf16[192,768]{1,0:T(8,128)(2,1)S(1)} %get-tuple-element.40, ...), kind=kOutput, calls=%fused_computation.13 | convolution fusion | flops 614203392 | bytes 4328448 | tf_op jit(solution)/shard_map/dot_general | solution.py:24
  86.4 5.0 %collective-permute-done.20 = bf16[128,768]{1,0:T(8,128)(2,1)} collective-permute-done((bf16[128,768]{1,0:T(8,128)(2,1)}, bf16[128,768]{1,0:T(8,128)(2,1)}, u32[]{:S(2)}, u32[]{:S(2)}) %collective-permute-start.20) | collective-permute-done | bytes 196640 | tf_op jit(solution)/shard_map/ppermute | solution.py:16
  96.3 5.1 %collective-permute-done.22 = bf16[128,768]{1,0:T(8,128)(2,1)} collective-permute-done((bf16[128,768]{1,0:T(8,128)(2,1)}, bf16[128,768]{1,0:T(8,128)(2,1)}, u32[]{:S(2)}, u32[]{:S(2)}) %collective-permute-start.22) | collective-permute-done | bytes 196640 | tf_op jit(solution)/shard_map/ppermute | solution.py:16
  103.2 3.5 %convert_reduce_fusion = (f32[768]{0:T(1024)}, bf16[512,768]{1,0:T(8,128)(2,1)S(1)}) fusion(f32[512,768]{1,0:T(8,128)} %get-tuple-element.148, bf16[768,768]{1,0:T(8,128)(2,1)S(1)} %copy-done, bf16[128,768]{1,0:T(8,128)(2,1)} %collective-permute-done.23, bf16[128,768]{1,0:T(8,128)(2,1)} %collective-permute-done.22, ...), kind=kOutput, calls=%fused_computation.12 | convolution fusion | flops 611843328 | bytes 4328448 | tf_op jit(solution)/shard_map/dot_general | solution.py:28
  107.7 2.3 convolution_convert_fusion.1
  111.3 2.0 convolution_convert_fusion
  120.6 13.1 %dynamic_update_slice.6 = f32[3072]{0:T(1024)S(1)} dynamic-update-slice(f32[3072]{0:T(1024)S(1)} %broadcast_in_dim.20, f32[768]{0:T(1024)S(1)} %copy-done.62, s32[]{:T(128)S(6)} %select_n.814) | dynamic-update-slice | bytes 6148 | tf_op jit(solution)/shard_map/dynamic_update_slice | solution.py:260
  133.7 2.2 multiply_reduce_fusion.3
  140.1 3.2 %collective-permute-done.28 = bf16[128,768]{1,0:T(8,128)(2,1)} collective-permute-done((bf16[128,768]{1,0:T(8,128)(2,1)}, bf16[128,768]{1,0:T(8,128)(2,1)}, u32[]{:S(2)}, u32[]{:S(2)}) %collective-permute-start.28) | collective-permute-done | bytes 196640 | tf_op jit(solution)/shard_map/ppermute | solution.py:16
  145.3 2.6 collective-permute-start.63
  156.5 2.3 fusion.160
  162.1 1.8 convolution_convert_fusion.2
  166.0 1.8 fusion.149
  169.5 2.8 collective-permute-done.52
  175.6 2.5 collective-permute-done.53
  180.7 1.7 collective-permute-done.54
  182.8 2.6 collective-permute-start.55
  186.4 7.6 %collective-permute-done.55 = f32[13,768]{1,0:T(8,128)S(1)} collective-permute-done((f32[13,768]{1,0:T(8,128)S(1)}, f32[13,768]{1,0:T(8,128)S(1)}, u32[]{:S(2)}, u32[]{:S(2)}) %collective-permute-start.55) | collective-permute-done | bytes 39968 | tf_op jit(solution)/shard_map/ppermute | solution.py:20
  196.1 2.3 collective-permute-done.57
  209.1 1.7 collective-permute-start.59
  210.8 8.4 %collective-permute-done.59 = bf16[24,768]{1,0:T(8,128)(2,1)S(1)} collective-permute-done((bf16[24,768]{1,0:T(8,128)(2,1)S(1)}, bf16[24,768]{1,0:T(8,128)(2,1)S(1)}, u32[]{:S(2)}, u32[]{:S(2)}) %collective-permute-start.59) | collective-permute-done | bytes 36896 | tf_op jit(solution)/shard_map/ppermute | solution.py:20
  221.0 2.7 collective-permute-start.60
  223.7 5.3 %collective-permute-done.60 = bf16[2,24,768]{2,1,0:T(8,128)(2,1)S(1)} collective-permute-done((bf16[2,24,768]{2,1,0:T(8,128)(2,1)S(1)}, bf16[2,24,768]{2,1,0:T(8,128)(2,1)S(1)}, u32[]{:S(2)}, u32[]{:S(2)}) %collective-permute-start.60) | collective-permute-done | bytes 73760 | tf_op jit(solution)/shard_map/ppermute | solution.py:20
  229.1 5.2 %collective-permute-done.35 = bf16[4,24,288]{2,1,0:T(8,128)(2,1)S(1)} collective-permute-done((bf16[4,24,288]{2,1,0:T(8,128)(2,1)S(1)}, bf16[4,24,288]{2,1,0:T(8,128)(2,1)S(1)}, u32[]{:S(2)}, u32[]{:S(2)}) %collective-permute-start.35) | collective-permute-done | bytes 55328 | tf_op jit(solution)/shard_map/ppermute | solution.py:20
  234.4 4.3 %collective-permute-done.44 = bf16[4,24,288]{2,1,0:T(8,128)(2,1)S(1)} collective-permute-done((bf16[4,24,288]{2,1,0:T(8,128)(2,1)S(1)}, bf16[4,24,288]{2,1,0:T(8,128)(2,1)S(1)}, u32[]{:S(2)}, u32[]{:S(2)}) %collective-permute-start.44) | collective-permute-done | bytes 55328 | tf_op jit(solution)/shard_map/ppermute | solution.py:20
  240.9 1.9 fusion.84
  248.2 2.1 collective-permute-start.48
  252.0 3.3 %collective-permute-done.39 = bf16[4,24,288]{2,1,0:T(8,128)(2,1)S(1)} collective-permute-done((bf16[4,24,288]{2,1,0:T(8,128)(2,1)S(1)}, bf16[4,24,288]{2,1,0:T(8,128)(2,1)S(1)}, u32[]{:S(2)}, u32[]{:S(2)}) %collective-permute-start.39) | collective-permute-done | bytes 55328 | tf_op jit(solution)/shard_map/ppermute | solution.py:20
  255.3 3.0 collective-permute-start.40
  259.9 4.8 %collective-permute-done.40 = bf16[2,4,24,288]{3,2,1,0:T(8,128)(2,1)S(1)} collective-permute-done((bf16[2,4,24,288]{3,2,1,0:T(8,128)(2,1)S(1)}, bf16[2,4,24,288]{3,2,1,0:T(8,128)(2,1)S(1)}, u32[]{:S(2)}, u32[]{:S(2)}) %collective-permute-start.40) | collective-permute-done | bytes 110624 | tf_op jit(solution)/shard_map/ppermute | solution.py:20
  264.8 1.7 collective-permute-start.41
  266.6 7.3 %collective-permute-done.49 = bf16[2,4,24,288]{3,2,1,0:T(8,128)(2,1)S(1)} collective-permute-done((bf16[2,4,24,288]{3,2,1,0:T(8,128)(2,1)S(1)}, bf16[2,4,24,288]{3,2,1,0:T(8,128)(2,1)S(1)}, u32[]{:S(2)}, u32[]{:S(2)}) %collective-permute-start.49) | collective-permute-done | bytes 110624 | tf_op jit(solution)/shard_map/ppermute | solution.py:20
  276.7 2.0 collective-permute-start.70
  278.7 5.3 %collective-permute-done.50 = bf16[2,2,4,24,288]{4,3,2,1,0:T(8,128)(2,1)S(1)} collective-permute-done((bf16[2,2,4,24,288]{4,3,2,1,0:T(8,128)(2,1)S(1)}, bf16[2,2,4,24,288]{4,3,2,1,0:T(8,128)(2,1)S(1)}, u32[]{:S(2)}, u32[]{:S(2)}) %collective-permute-start.50) | collective-permute-done | bytes 221216 | tf_op jit(solution)/shard_map/ppermute | solution.py:20
  291.7 1.8 maximum_maximum_fusion
  293.4 2.5 copy.75
  296.0 3.7 %reshape.623 = f32[192,2304]{1,0:T(8,128)} reshape(f32[192,3,4,192]{3,2,1,0:T(4,128)} %copy.75) | data formatting | bytes 3538944 | tf_op jit(solution)/shard_map/reshape | solution.py:252
  (463 shorter events, 122.0 us)
Async XLA Ops:
  6.1 16.5 %collective-permute-start.8 = (bf16[1,1536]{1,0:T(2,128)(2,1)}, bf16[1,1536]{1,0:T(2,128)(2,1)S(1)}, u32[]{:S(2)}, u32[]{:S(2)}) collective-permute-start(bf16[1,1536]{1,0:T(2,128)(2,1)} %reshape.613), channel_id=1, source_target_pairs={{0,8},{8,0},{16,24},{24,16},{1,9},{9,1},{17,25},{25,17},{2,10},{10... | collective-permute-start | bytes 9224 | tf_op jit(solution)/shard_map/ppermute | solution.py:16
  6.6 12.5 %collective-permute-start.6 = (bf16[1,1536]{1,0:T(2,128)(2,1)}, bf16[1,1536]{1,0:T(2,128)(2,1)}, u32[]{:S(2)}, u32[]{:S(2)}) collective-permute-start(bf16[1,1536]{1,0:T(2,128)(2,1)} %reshape.613), channel_id=1, source_target_pairs={{0,16},{8,24},{16,0},{24,8},{1,17},{9,25},{17,1},{25,9},{2,18},{10... | collective-permute-start | bytes 9224 | tf_op jit(solution)/shard_map/ppermute | solution.py:16
  9.1 15.1 %collective-permute-start.1 = (bf16[128,768]{1,0:T(8,128)(2,1)}, bf16[128,768]{1,0:T(8,128)(2,1)}, u32[]{:S(2)}, u32[]{:S(2)}) collective-permute-start(bf16[128,768]{1,0:T(8,128)(2,1)} %bitcast.320), channel_id=1, source_target_pairs={{0,16},{8,24},{16,0},{24,8},{1,17},{9,25},{17,1},{25,9},{2,18},{10... | collective-permute-start | bytes 589832 | tf_op jit(solution)/shard_map/ppermute | solution.py:16
  9.1 24.9 %collective-permute-start = (bf16[128,768]{1,0:T(8,128)(2,1)}, bf16[128,768]{1,0:T(8,128)(2,1)}, u32[]{:S(2)}, u32[]{:S(2)}) collective-permute-start(bf16[128,768]{1,0:T(8,128)(2,1)} %bitcast.321), channel_id=1, source_target_pairs={{0,8},{8,0},{16,24},{24,16},{1,9},{9,1},{17,25},{25,17},{2,10},{10... | collective-permute-start | bytes 589832 | tf_op jit(solution)/shard_map/ppermute | solution.py:16
  17.1 9.3 %collective-permute-start.3 = (bf16[192,576]{0,1:T(8,128)(2,1)S(1)}, bf16[192,576]{0,1:T(8,128)(2,1)}, u32[]{:S(2)}, u32[]{:S(2)}) collective-permute-start(bf16[192,576]{0,1:T(8,128)(2,1)S(1)} %bitcast.314), channel_id=1, source_target_pairs={{0,24},{8,16},{16,8},{24,0},{1,25},{9,17},{17,9},{25,1},{2,26},{10... | collective-permute-start | bytes 663560 | tf_op jit(solution)/shard_map/ppermute | solution.py:16
  22.6 10.3 %collective-permute-start.4 = (bf16[192,576]{0,1:T(8,128)(2,1)S(1)}, bf16[192,576]{0,1:T(8,128)(2,1)S(1)}, u32[]{:S(2)}, u32[]{:S(2)}) collective-permute-start(bf16[192,576]{0,1:T(8,128)(2,1)S(1)} %bitcast.316), channel_id=1, source_target_pairs={{0,16},{8,24},{16,0},{24,8},{1,17},{9,25},{17,1},{25,9},{2,18},{10... | collective-permute-start | bytes 663560 | tf_op jit(solution)/shard_map/ppermute | solution.py:16
  23.1 9.9 %collective-permute-start.5 = (bf16[192,576]{0,1:T(8,128)(2,1)S(1)}, bf16[192,576]{0,1:T(8,128)(2,1)S(1)}, u32[]{:S(2)}, u32[]{:S(2)}) collective-permute-start(bf16[192,576]{0,1:T(8,128)(2,1)S(1)} %bitcast.315), channel_id=1, source_target_pairs={{0,8},{8,0},{16,24},{24,16},{1,9},{9,1},{17,25},{25,17},{2,10},{10... | collective-permute-start | bytes 663560 | tf_op jit(solution)/shard_map/ppermute | solution.py:16
  24.2 9.9 %collective-permute-start.2 = (bf16[128,768]{1,0:T(8,128)(2,1)}, bf16[128,768]{1,0:T(8,128)(2,1)S(1)}, u32[]{:S(2)}, u32[]{:S(2)}) collective-permute-start(bf16[128,768]{1,0:T(8,128)(2,1)} %collective-permute-done.1), channel_id=1, source_target_pairs={{0,8},{8,0},{16,24},{24,16},{1,9},{9,1},{17,25},{25,17},{2,10},{10... | collective-permute-start | bytes 589832 | tf_op jit(solution)/shard_map/ppermute | solution.py:16
  45.2 28.9 %collective-permute-start.17 = (bf16[192,768]{1,0:T(8,128)(2,1)}, bf16[192,768]{1,0:T(8,128)(2,1)S(1)}, u32[]{:S(2)}, u32[]{:S(2)}) collective-permute-start(bf16[192,768]{1,0:T(8,128)(2,1)} %get-tuple-element.59), channel_id=1, source_target_pairs={{0,8},{8,0},{16,24},{24,16},{1,9},{9,1},{17,25},{25,17},{2,10},{10... | collective-permute-start | bytes 884744 | tf_op jit(solution)/shard_map/ppermute | solution.py:16
  45.7 28.4 %collective-permute-start.16 = (bf16[192,768]{1,0:T(8,128)(2,1)}, bf16[192,768]{1,0:T(8,128)(2,1)S(1)}, u32[]{:S(2)}, u32[]{:S(2)}) collective-permute-start(bf16[192,768]{1,0:T(8,128)(2,1)} %get-tuple-element.60), channel_id=1, source_target_pairs={{0,16},{8,24},{16,0},{24,8},{1,17},{9,25},{17,1},{25,9},{2,18},{10... | collective-permute-start | bytes 884744 | tf_op jit(solution)/shard_map/ppermute | solution.py:16
  47.3 28.2 %collective-permute-start.15 = (bf16[192,768]{1,0:T(8,128)(2,1)}, bf16[192,768]{1,0:T(8,128)(2,1)}, u32[]{:S(2)}, u32[]{:S(2)}) collective-permute-start(bf16[192,768]{1,0:T(8,128)(2,1)} %get-tuple-element.61), channel_id=1, source_target_pairs={{0,24},{8,16},{16,8},{24,0},{1,25},{9,17},{17,9},{25,1},{2,26},{10... | collective-permute-start | bytes 884744 | tf_op jit(solution)/shard_map/ppermute | solution.py:16
  48.9 16.5 %collective-permute-start.11 = (bf16[128,768]{1,0:T(8,128)(2,1)S(1)}, bf16[128,768]{1,0:T(8,128)(2,1)}, u32[]{:S(2)}, u32[]{:S(2)}) collective-permute-start(bf16[128,768]{1,0:T(8,128)(2,1)S(1)} %fusion.58), channel_id=1, source_target_pairs={{0,16},{8,24},{16,0},{24,8},{1,17},{9,25},{17,1},{25,9},{2,18},{10... | collective-permute-start | bytes 589832 | tf_op jit(solution)/shard_map/ppermute | solution.py:16
  67.8 6.3 %collective-permute-start.13 = (bf16[128,768]{1,0:T(8,128)(2,1)}, bf16[128,768]{1,0:T(8,128)(2,1)}, u32[]{:S(2)}, u32[]{:S(2)}) collective-permute-start(bf16[128,768]{1,0:T(8,128)(2,1)} %fusion.62), channel_id=1, source_target_pairs={{0,16},{8,24},{16,0},{24,8},{1,17},{9,25},{17,1},{25,9},{2,18},{10... | collective-permute-start | bytes 589832 | tf_op jit(solution)/shard_map/ppermute | solution.py:16
  69.4 7.7 %collective-permute-start.12 = (bf16[128,768]{1,0:T(8,128)(2,1)}, bf16[128,768]{1,0:T(8,128)(2,1)S(1)}, u32[]{:S(2)}, u32[]{:S(2)}) collective-permute-start(bf16[128,768]{1,0:T(8,128)(2,1)} %fusion.62), channel_id=1, source_target_pairs={{0,8},{8,0},{16,24},{24,16},{1,9},{9,1},{17,25},{25,17},{2,10},{10... | collective-permute-start | bytes 589832 | tf_op jit(solution)/shard_map/ppermute | solution.py:16
  83.9 7.5 %collective-permute-start.20 = (bf16[128,768]{1,0:T(8,128)(2,1)}, bf16[128,768]{1,0:T(8,128)(2,1)}, u32[]{:S(2)}, u32[]{:S(2)}) collective-permute-start(bf16[128,768]{1,0:T(8,128)(2,1)} %fusion.54), channel_id=1, source_target_pairs={{0,16},{8,24},{16,0},{24,8},{1,17},{9,25},{17,1},{25,9},{2,18},{10... | collective-permute-start | bytes 589832 | tf_op jit(solution)/shard_map/ppermute | solution.py:16
  94.7 6.7 %collective-permute-start.22 = (bf16[128,768]{1,0:T(8,128)(2,1)}, bf16[128,768]{1,0:T(8,128)(2,1)}, u32[]{:S(2)}, u32[]{:S(2)}) collective-permute-start(bf16[128,768]{1,0:T(8,128)(2,1)} %get-tuple-element.30), channel_id=1, source_target_pairs={{0,16},{8,24},{16,0},{24,8},{1,17},{9,25},{17,1},{25,9},{2,18},{10... | collective-permute-start | bytes 589832 | tf_op jit(solution)/shard_map/ppermute | solution.py:16
  110.8 22.9 %collective-permute-start.24 = (bf16[128,768]{1,0:T(8,128)(2,1)}, bf16[128,768]{1,0:T(8,128)(2,1)S(1)}, u32[]{:S(2)}, u32[]{:S(2)}) collective-permute-start(bf16[128,768]{1,0:T(8,128)(2,1)} %get-tuple-element.66), channel_id=1, source_target_pairs={{0,8},{8,0},{16,24},{24,16},{1,9},{9,1},{17,25},{25,17},{2,10},{10... | collective-permute-start | bytes 589832 | tf_op jit(solution)/shard_map/ppermute | solution.py:16
  114.1 19.5 %collective-permute-start.26 = (bf16[128,768]{1,0:T(8,128)(2,1)}, bf16[128,768]{1,0:T(8,128)(2,1)}, u32[]{:S(2)}, u32[]{:S(2)}) collective-permute-start(bf16[128,768]{1,0:T(8,128)(2,1)} %fusion.51), channel_id=1, source_target_pairs={{0,16},{8,24},{16,0},{24,8},{1,17},{9,25},{17,1},{25,9},{2,18},{10... | collective-permute-start | bytes 589832 | tf_op jit(solution)/shard_map/ppermute | solution.py:16
  116.6 20.9 %collective-permute-start.71 = (bf16[2,2,96,768]{3,2,1,0:T(8,128)(2,1)}, bf16[2,2,96,768]{3,2,1,0:T(8,128)(2,1)}, u32[]{:S(2)}, u32[]{:S(2)}) collective-permute-start(bf16[2,2,96,768]{3,2,1,0:T(8,128)(2,1)} %dynamic-slice_bitcast_fusion), channel_id=1, source_target_pairs={{0,1},{1,0},{2,3},{3,2},{4,5},{5,4},{6,7},{7,6},{8,9},{9,8},{10,11... | collective-permute-start | bytes 1769480 | tf_op jit(solution)/shard_map/ppermute | solution.py:20
  119.0 24.3 %collective-permute-start.62 = (bf16[2,2,4,24,768]{4,3,2,1,0:T(8,128)(2,1)}, bf16[2,2,4,24,768]{4,3,2,1,0:T(8,128)(2,1)}, u32[]{:S(2)}, u32[]{:S(2)}) collective-permute-start(bf16[2,2,4,24,768]{4,3,2,1,0:T(8,128)(2,1)} %dynamic-slice_bitcast_fusion.1), channel_id=1, source_target_pairs={{0,2},{1,3},{2,0},{3,1},{4,6},{5,7},{6,4},{7,5},{8,10},{9,11},{10,... | collective-permute-start | bytes 1769480 | tf_op jit(solution)/shard_map/ppermute | solution.py:20
  136.9 6.4 %collective-permute-start.28 = (bf16[128,768]{1,0:T(8,128)(2,1)}, bf16[128,768]{1,0:T(8,128)(2,1)}, u32[]{:S(2)}, u32[]{:S(2)}) collective-permute-start(bf16[128,768]{1,0:T(8,128)(2,1)} %get-tuple-element.32), channel_id=1, source_target_pairs={{0,16},{8,24},{16,0},{24,8},{1,17},{9,25},{17,1},{25,9},{2,18},{10... | collective-permute-start | bytes 589832 | tf_op jit(solution)/shard_map/ppermute | solution.py:16
  137.4 10.4 %collective-permute-start.27 = (bf16[128,768]{1,0:T(8,128)(2,1)}, bf16[128,768]{1,0:T(8,128)(2,1)}, u32[]{:S(2)}, u32[]{:S(2)}) collective-permute-start(bf16[128,768]{1,0:T(8,128)(2,1)} %get-tuple-element.32), channel_id=1, source_target_pairs={{0,8},{8,0},{16,24},{24,16},{1,9},{9,1},{17,25},{25,17},{2,10},{10... | collective-permute-start | bytes 589832 | tf_op jit(solution)/shard_map/ppermute | solution.py:16
  139.7 33.2 %collective-permute-start.72 = (bf16[2,96,768]{2,1,0:T(8,128)(2,1)}, bf16[2,96,768]{2,1,0:T(8,128)(2,1)}, u32[]{:S(2)}, u32[]{:S(2)}) collective-permute-start(bf16[2,96,768]{2,1,0:T(8,128)(2,1)} %dynamic-slice_bitcast_fusion.2), channel_id=1, source_target_pairs={{0,2},{1,3},{2,0},{3,1},{4,6},{5,7},{6,4},{7,5},{8,10},{9,11},{10,... | collective-permute-start | bytes 884744 | tf_op jit(solution)/shard_map/ppermute | solution.py:20
  145.3 28.7 %collective-permute-start.63 = (bf16[2,4,24,768]{3,2,1,0:T(8,128)(2,1)}, bf16[2,4,24,768]{3,2,1,0:T(8,128)(2,1)}, u32[]{:S(2)}, u32[]{:S(2)}) collective-permute-start(bf16[2,4,24,768]{3,2,1,0:T(8,128)(2,1)} %dynamic-slice_bitcast_fusion.3), channel_id=1, source_target_pairs={{0,4},{1,5},{2,6},{3,7},{4,0},{5,1},{6,2},{7,3},{8,12},{9,13},{10,... | collective-permute-start | bytes 884744 | tf_op jit(solution)/shard_map/ppermute | solution.py:20
  161.1 17.0 %collective-permute-start.56 = (bf16[2,2,24,768]{3,2,1,0:T(8,128)(2,1)}, bf16[2,2,24,768]{3,2,1,0:T(8,128)(2,1)}, u32[]{:S(2)}, u32[]{:S(2)}) collective-permute-start(bf16[2,2,24,768]{3,2,1,0:T(8,128)(2,1)} %dynamic-slice_bitcast_fusion.6), channel_id=1, source_target_pairs={{0,1},{1,0},{2,3},{3,2},{4,5},{5,4},{6,7},{7,6},{8,9},{9,8},{10,11... | collective-permute-start | bytes 442376 | tf_op jit(solution)/shard_map/ppermute | solution.py:20
  164.4 34.6 %collective-permute-start.33 = (bf16[2,2,4,24,288]{4,3,2,1,0:T(8,128)(2,1)S(1)}, bf16[2,2,4,24,288]{4,3,2,1,0:T(8,128)(2,1)S(1)}, u32[]{:S(2)}, u32[]{:S(2)}) collective-permute-start(bf16[2,2,4,24,288]{4,3,2,1,0:T(8,128)(2,1)S(1)} %bitcast.317), channel_id=1, source_target_pairs={{0,1},{1,0},{2,3},{3,2},{4,5},{5,4},{6,7},{7,6},{8,9},{9,8},{10,11... | collective-permute-start | bytes 663560 | tf_op jit(solution)/shard_map/ppermute | solution.py:20
  172.2 28.5 %collective-permute-start.42 = (bf16[2,2,4,24,288]{4,3,2,1,0:T(8,128)(2,1)}, bf16[2,2,4,24,288]{4,3,2,1,0:T(8,128)(2,1)}, u32[]{:S(2)}, u32[]{:S(2)}) collective-permute-start(bf16[2,2,4,24,288]{4,3,2,1,0:T(8,128)(2,1)} %bitcast.287), channel_id=1, source_target_pairs={{0,2},{1,3},{2,0},{3,1},{4,6},{5,7},{6,4},{7,5},{8,10},{9,11},{10,... | collective-permute-start | bytes 663560 | tf_op jit(solution)/shard_map/ppermute | solution.py:20
  172.8 66.1 %collective-permute-start.30 = (bf16[128,768]{1,0:T(8,128)(2,1)}, bf16[128,768]{1,0:T(8,128)(2,1)}, u32[]{:S(2)}, u32[]{:S(2)}) collective-permute-start(bf16[128,768]{1,0:T(8,128)(2,1)} %get-tuple-element.64), channel_id=1, source_target_pairs={{0,8},{8,0},{16,24},{24,16},{1,9},{9,1},{17,25},{25,17},{2,10},{10... | collective-permute-start | bytes 589832 | tf_op jit(solution)/shard_map/ppermute | solution.py:16
  182.4 21.3 %collective-permute-start.73 = (bf16[96,768]{1,0:T(8,128)(2,1)S(1)}, bf16[96,768]{1,0:T(8,128)(2,1)S(1)}, u32[]{:S(2)}, u32[]{:S(2)}) collective-permute-start(bf16[96,768]{1,0:T(8,128)(2,1)S(1)} %dynamic-slice_bitcast_fusion.4), channel_id=1, source_target_pairs={{0,4},{1,5},{2,6},{3,7},{4,0},{5,1},{6,2},{7,3},{8,12},{9,13},{10,... | collective-permute-start | bytes 442376 | tf_op jit(solution)/shard_map/ppermute | solution.py:20
  182.8 11.3 %collective-permute-start.55 = (f32[13,768]{1,0:T(8,128)S(1)}, f32[13,768]{1,0:T(8,128)S(1)}, u32[]{:S(2)}, u32[]{:S(2)}) collective-permute-start(f32[13,768]{1,0:T(8,128)S(1)} %add.363), channel_id=1, source_target_pairs={{0,4},{1,5},{2,6},{3,7},{4,0},{5,1},{6,2},{7,3},{8,12},{9,13},{10,... | collective-permute-start | bytes 119816 | tf_op jit(solution)/shard_map/ppermute | solution.py:20
  199.0 40.3 %collective-permute-start.32 = (bf16[128,768]{1,0:T(8,128)(2,1)S(1)}, bf16[128,768]{1,0:T(8,128)(2,1)S(1)}, u32[]{:S(2)}, u32[]{:S(2)}) collective-permute-start(bf16[128,768]{1,0:T(8,128)(2,1)S(1)} %fusion.47), channel_id=1, source_target_pairs={{0,16},{8,24},{16,0},{24,8},{1,17},{9,25},{17,1},{25,9},{2,18},{10... | collective-permute-start | bytes 589832 | tf_op jit(solution)/shard_map/ppermute | solution.py:16
  207.0 12.2 %collective-permute-start.34 = (bf16[2,4,24,288]{3,2,1,0:T(8,128)(2,1)S(1)}, bf16[2,4,24,288]{3,2,1,0:T(8,128)(2,1)S(1)}, u32[]{:S(2)}, u32[]{:S(2)}) collective-permute-start(bf16[2,4,24,288]{3,2,1,0:T(8,128)(2,1)S(1)} %dynamic-slice_bitcast_fusion.8), channel_id=1, source_target_pairs={{0,2},{1,3},{2,0},{3,1},{4,6},{5,7},{6,4},{7,5},{8,10},{9,11},{10,... | collective-permute-start | bytes 331784 | tf_op jit(solution)/shard_map/ppermute | solution.py:20
  207.8 13.1 %collective-permute-start.43 = (bf16[2,4,24,288]{3,2,1,0:T(8,128)(2,1)S(1)}, bf16[2,4,24,288]{3,2,1,0:T(8,128)(2,1)S(1)}, u32[]{:S(2)}, u32[]{:S(2)}) collective-permute-start(bf16[2,4,24,288]{3,2,1,0:T(8,128)(2,1)S(1)} %dynamic-slice_bitcast_fusion.7), channel_id=1, source_target_pairs={{0,4},{1,5},{2,6},{3,7},{4,0},{5,1},{6,2},{7,3},{8,12},{9,13},{10,... | collective-permute-start | bytes 331784 | tf_op jit(solution)/shard_map/ppermute | solution.py:20
  209.1 10.1 %collective-permute-start.59 = (bf16[24,768]{1,0:T(8,128)(2,1)S(1)}, bf16[24,768]{1,0:T(8,128)(2,1)S(1)}, u32[]{:S(2)}, u32[]{:S(2)}) collective-permute-start(bf16[24,768]{1,0:T(8,128)(2,1)S(1)} %fusion.89), channel_id=1, source_target_pairs={{0,4},{1,5},{2,6},{3,7},{4,0},{5,1},{6,2},{7,3},{8,12},{9,13},{10,... | collective-permute-start | bytes 110600 | tf_op jit(solution)/shard_map/ppermute | solution.py:20
  219.2 19.6 %collective-permute-start.74 = (bf16[96,768]{1,0:T(8,128)(2,1)S(1)}, bf16[96,768]{1,0:T(8,128)(2,1)S(1)}, u32[]{:S(2)}, u32[]{:S(2)}) collective-permute-start(bf16[96,768]{1,0:T(8,128)(2,1)S(1)} %fusion.63), channel_id=1, source_target_pairs={{0,4},{1,5},{2,6},{3,7},{4,0},{5,1},{6,2},{7,3},{8,12},{9,13},{10,... | collective-permute-start | bytes 442376 | tf_op jit(solution)/shard_map/ppermute | solution.py:20
  219.2 31.1 %collective-permute-start.68 = (bf16[4,24,768]{2,1,0:T(8,128)(2,1)S(1)}, bf16[4,24,768]{2,1,0:T(8,128)(2,1)S(1)}, u32[]{:S(2)}, u32[]{:S(2)}) collective-permute-start(bf16[4,24,768]{2,1,0:T(8,128)(2,1)S(1)} %pad_maximum_fusion.21), channel_id=1, source_target_pairs={{0,1},{1,0},{2,3},{3,2},{4,5},{5,4},{6,7},{7,6},{8,9},{9,8},{10,11... | collective-permute-start | bytes 442376 | tf_op jit(solution)/shard_map/ppermute | solution.py:20
  221.0 8.1 %collective-permute-start.60 = (bf16[2,24,768]{2,1,0:T(8,128)(2,1)S(1)}, bf16[2,24,768]{2,1,0:T(8,128)(2,1)S(1)}, u32[]{:S(2)}, u32[]{:S(2)}) collective-permute-start(bf16[2,24,768]{2,1,0:T(8,128)(2,1)S(1)} %pad_maximum_fusion.34), channel_id=1, source_target_pairs={{0,2},{1,3},{2,0},{3,1},{4,6},{5,7},{6,4},{7,5},{8,10},{9,11},{10,... | collective-permute-start | bytes 221192 | tf_op jit(solution)/shard_map/ppermute | solution.py:20
  238.7 20.3 %collective-permute-start.61 = (bf16[2,2,24,768]{3,2,0,1:T(8,128)(2,1)S(1)}, bf16[2,2,24,768]{3,2,0,1:T(8,128)(2,1)S(1)}, u32[]{:S(2)}, u32[]{:S(2)}) collective-permute-start(bf16[2,2,24,768]{3,2,0,1:T(8,128)(2,1)S(1)} %pad_maximum_fusion.20), channel_id=1, source_target_pairs={{0,1},{1,0},{2,3},{3,2},{4,5},{5,4},{6,7},{7,6},{8,9},{9,8},{10,11... | collective-permute-start | bytes 442376 | tf_op jit(solution)/shard_map/ppermute | solution.py:20
  245.9 28.2 %collective-permute-start.75 = (bf16[2,96,768]{2,1,0:T(8,128)(2,1)S(1)}, bf16[2,96,768]{2,1,0:T(8,128)(2,1)S(1)}, u32[]{:S(2)}, u32[]{:S(2)}) collective-permute-start(bf16[2,96,768]{2,1,0:T(8,128)(2,1)S(1)} %pad_maximum_fusion.14), channel_id=1, source_target_pairs={{0,2},{1,3},{2,0},{3,1},{4,6},{5,7},{6,4},{7,5},{8,10},{9,11},{10,... | collective-permute-start | bytes 884744 | tf_op jit(solution)/shard_map/ppermute | solution.py:20
  246.8 8.5 %collective-permute-start.39 = (bf16[4,24,288]{2,1,0:T(8,128)(2,1)S(1)}, bf16[4,24,288]{2,1,0:T(8,128)(2,1)S(1)}, u32[]{:S(2)}, u32[]{:S(2)}) collective-permute-start(bf16[4,24,288]{2,1,0:T(8,128)(2,1)S(1)} %pad_maximum_fusion.32), channel_id=1, source_target_pairs={{0,4},{1,5},{2,6},{3,7},{4,0},{5,1},{6,2},{7,3},{8,12},{9,13},{10,... | collective-permute-start | bytes 165896 | tf_op jit(solution)/shard_map/ppermute | solution.py:20
  248.2 10.1 %collective-permute-start.48 = (bf16[4,24,288]{2,1,0:T(8,128)(2,1)S(1)}, bf16[4,24,288]{2,1,0:T(8,128)(2,1)S(1)}, u32[]{:S(2)}, u32[]{:S(2)}) collective-permute-start(bf16[4,24,288]{2,1,0:T(8,128)(2,1)S(1)} %pad_maximum_fusion.33), channel_id=1, source_target_pairs={{0,1},{1,0},{2,3},{3,2},{4,5},{5,4},{6,7},{7,6},{8,9},{9,8},{10,11... | collective-permute-start | bytes 165896 | tf_op jit(solution)/shard_map/ppermute | solution.py:20
  250.4 25.4 %collective-permute-start.69 = (bf16[2,4,24,768]{3,2,1,0:T(8,128)(2,1)S(1)}, bf16[2,4,24,768]{3,2,1,0:T(8,128)(2,1)S(1)}, u32[]{:S(2)}, u32[]{:S(2)}) collective-permute-start(bf16[2,4,24,768]{3,2,1,0:T(8,128)(2,1)S(1)} %pad_maximum_fusion.13), channel_id=1, source_target_pairs={{0,4},{1,5},{2,6},{3,7},{4,0},{5,1},{6,2},{7,3},{8,12},{9,13},{10,... | collective-permute-start | bytes 884744 | tf_op jit(solution)/shard_map/ppermute | solution.py:20
  255.3 9.4 %collective-permute-start.40 = (bf16[2,4,24,288]{3,2,1,0:T(8,128)(2,1)S(1)}, bf16[2,4,24,288]{3,2,1,0:T(8,128)(2,1)S(1)}, u32[]{:S(2)}, u32[]{:S(2)}) collective-permute-start(bf16[2,4,24,288]{3,2,1,0:T(8,128)(2,1)S(1)} %pad_maximum_fusion.18), channel_id=1, source_target_pairs={{0,2},{1,3},{2,0},{3,1},{4,6},{5,7},{6,4},{7,5},{8,10},{9,11},{10,... | collective-permute-start | bytes 331784 | tf_op jit(solution)/shard_map/ppermute | solution.py:20
  258.4 15.5 %collective-permute-start.49 = (bf16[2,4,24,288]{3,2,1,0:T(8,128)(2,1)S(1)}, bf16[2,4,24,288]{3,2,1,0:T(8,128)(2,1)S(1)}, u32[]{:S(2)}, u32[]{:S(2)}) collective-permute-start(bf16[2,4,24,288]{3,2,1,0:T(8,128)(2,1)S(1)} %pad_maximum_fusion.19), channel_id=1, source_target_pairs={{0,4},{1,5},{2,6},{3,7},{4,0},{5,1},{6,2},{7,3},{8,12},{9,13},{10,... | collective-permute-start | bytes 331784 | tf_op jit(solution)/shard_map/ppermute | solution.py:20
  264.8 19.6 %collective-permute-start.41 = (bf16[2,2,4,24,288]{4,3,2,0,1:T(8,128)(2,1)S(1)}, bf16[2,2,4,24,288]{4,3,2,0,1:T(8,128)(2,1)S(1)}, u32[]{:S(2)}, u32[]{:S(2)}) collective-permute-start(bf16[2,2,4,24,288]{4,3,2,0,1:T(8,128)(2,1)S(1)} %pad_maximum_fusion.11), channel_id=1, source_target_pairs={{0,1},{1,0},{2,3},{3,2},{4,5},{5,4},{6,7},{7,6},{8,9},{9,8},{10,11... | collective-permute-start | bytes 663560 | tf_op jit(solution)/shard_map/ppermute | solution.py:20
  274.0 10.0 %collective-permute-start.50 = (bf16[2,2,4,24,288]{4,3,2,1,0:T(8,128)(2,1)S(1)}, bf16[2,2,4,24,288]{4,3,2,1,0:T(8,128)(2,1)S(1)}, u32[]{:S(2)}, u32[]{:S(2)}) collective-permute-start(bf16[2,2,4,24,288]{4,3,2,1,0:T(8,128)(2,1)S(1)} %pad_maximum_fusion.12), channel_id=1, source_target_pairs={{0,2},{1,3},{2,0},{3,1},{4,6},{5,7},{6,4},{7,5},{8,10},{9,11},{10,... | collective-permute-start | bytes 663560 | tf_op jit(solution)/shard_map/ppermute | solution.py:20
  275.0 24.6 %collective-permute-start.76 = (bf16[2,2,96,768]{3,2,0,1:T(8,128)(2,1)}, bf16[2,2,96,768]{3,2,0,1:T(8,128)(2,1)}, u32[]{:S(2)}, u32[]{:S(2)}) collective-permute-start(bf16[2,2,96,768]{3,2,0,1:T(8,128)(2,1)} %pad_maximum_fusion.10), channel_id=1, source_target_pairs={{0,1},{1,0},{2,3},{3,2},{4,5},{5,4},{6,7},{7,6},{8,9},{9,8},{10,11... | collective-permute-start | bytes 1769480 | tf_op jit(solution)/shard_map/ppermute | solution.py:20
  276.7 25.8 %collective-permute-start.70 = (bf16[2,2,4,24,768]{4,3,2,1,0:T(8,128)(2,1)}, bf16[2,2,4,24,768]{4,3,2,1,0:T(8,128)(2,1)}, u32[]{:S(2)}, u32[]{:S(2)}) collective-permute-start(bf16[2,2,4,24,768]{4,3,2,1,0:T(8,128)(2,1)} %pad_maximum_fusion.9), channel_id=1, source_target_pairs={{0,2},{1,3},{2,0},{3,1},{4,6},{5,7},{6,4},{7,5},{8,10},{9,11},{10,... | collective-permute-start | bytes 1769480 | tf_op jit(solution)/shard_map/ppermute | solution.py:20
  (101 other events, 518.2 us)

commit v2 on v1

--- a/solution.py
+++ b/solution.py
@@ -3,6 +3,8 @@
 import jax
 import jax.numpy as jnp
 from jax import lax
+from jax.experimental import pallas as pl
+from jax.experimental.pallas import tpu as pltpu
 from jax.sharding import PartitionSpec as P
 
 HD = 64
@@ -55,33 +57,139 @@
     return parts[0] + near.astype(F32) + far.astype(F32)
 
 
-def replica_scatter(value, order, me, count):
-    top = count.bit_length() - 1
-    rest = value.shape[1:]
-    value = value.reshape((2,) * top + rest)
-    left = list(range(top - 1, -1, -1))
-    for bit in order:
-        axis = left.index(bit)
-        mine = (me >> bit) & 1
-        other = lax.dynamic_index_in_dim(value, 1 - mine, axis, keepdims=False)
-        keep = lax.dynamic_index_in_dim(value, mine, axis, keepdims=False)
-        got = rx(other, 1 << bit, count)
-        value = (keep.astype(F32) + got.astype(F32)).astype(BF)
-        left.remove(bit)
-    return value
-
-
-def replica_gather(value, order, me, count):
-    top = count.bit_length() - 1
-    rest = value.shape
-    left = []
-    for bit in reversed(order):
-        got = rx(value, 1 << bit, count)
-        on = ((me >> bit) & 1) != 0
-        left = sorted(left + [bit], reverse=True)
-        axis = left.index(bit)
-        value = jnp.stack([jnp.where(on, got, value), jnp.where(on, value, got)], axis=axis)
-    return value.reshape((count,) + rest)
+def after(value, *others):
+    return lax.optimization_barrier((value, others))[0]
+
+
+class Scatter:
+    def __init__(self, value, order, me, count):
+        self.held, self.rows = [(value, 0)], value.shape[1]
+        self.left, self.me, self.count = list(order), me, count
+
+    def total(self, side):
+        cut = [
+            lax.dynamic_slice_in_dim(array, start + side * self.rows, self.rows, 1).astype(F32)
+            for array, start in self.held
+        ]
+        return sum(cut[1:], cut[0])
+
+    def send(self):
+        self.rows //= 2
+        self.mine = (self.me >> self.left[0]) & 1
+        return self.total(1 - self.mine).astype(BF)
+
+    def swap(self, half):
+        return rx(half, 1 << self.left.pop(0), self.count)
+
+    def take(self, got):
+        moved = [(array, start + self.mine * self.rows) for array, start in self.held]
+        self.held = moved + [(got, 0)]
+
+    def step(self, got):
+        self.take(got)
+        return self.swap(self.send())
+
+    def piece(self, got):
+        self.take(got)
+        return self.total(0).astype(BF)
+
+
+class Gather:
+    def __init__(self, value, order, me, count):
+        self.value, self.left, self.me, self.count = value, list(order), me, count
+
+    def swap(self):
+        return rx(self.value, 1 << self.left[-1], self.count)
+
+    def take(self, got):
+        on = ((self.me >> self.left.pop()) & 1) != 0
+        self.value = jnp.concatenate(
+            [jnp.where(on, got, self.value), jnp.where(on, self.value, got)], axis=1
+        )
+
+    def step(self, got):
+        self.take(got)
+        return self.swap()
+
+
+def whole_spec():
+    return pl.BlockSpec(memory_space=pltpu.VMEM)
+
+
+def index_spec():
+    return pl.BlockSpec(memory_space=pltpu.SMEM)
+
+
+def call(kernel, out_shape, inputs, flops=0):
+    single = not isinstance(out_shape, (list, tuple))
+    outs = [out_shape] if single else list(out_shape)
+    moved = sum(v.size * v.dtype.itemsize for v in list(inputs) + outs)
+    got = pl.pallas_call(
+        kernel,
+        out_shape=outs,
+        in_specs=[index_spec()] + [whole_spec()] * (len(inputs) - 1),
+        out_specs=[whole_spec()] * len(outs),
+        compiler_params=pltpu.CompilerParams(vmem_limit_bytes=48 * 1024 * 1024),
+        cost_estimate=pl.CostEstimate(flops=flops, bytes_accessed=moved, transcendentals=0),
+    )(*inputs)
+    return got[0] if single else got
+
+
+def pack_kernel(index, weight, *sends):
+    part = weight.shape[0]
+    for own in range(G):
+
+        @pl.when(index[0] == own)
+        def _():
+            for k in range(G):
+                dest = own ^ k
+                for j in range(3):
+                    start = (j * G + dest) * part
+                    sends[k][:, j * part : (j + 1) * part] = weight[:, start : start + part]
+
+
+def join_kernel(index, held, got, out):
+    rows = held.shape[0]
+    mine = index[1]
+    out[pl.ds(pl.multiple_of(mine * rows, rows), rows), :] = held[...].astype(F32)
+    out[pl.ds(pl.multiple_of((1 - mine) * rows, rows), rows), :] = got[...].astype(F32)
+
+
+def join_up_kernel(index, held, got, out):
+    rows, columns = held.shape[1], held.shape[2]
+    mine = index[2]
+    for k in range(G):
+        where = pl.ds(pl.multiple_of((index[0] ^ k) * columns, columns), columns)
+        out[pl.ds(pl.multiple_of(mine * rows, rows), rows), where] = held[k].astype(F32)
+        out[pl.ds(pl.multiple_of((1 - mine) * rows, rows), rows), where] = got[k].astype(F32)
+
+
+def join_tail_kernel(index, held_one, got_one, held_two, got_two, out, qkv):
+    rows, part = held_one.shape[1], held_one.shape[2] // 2
+
+    def in_order(pieces):
+        bit = 1
+        while bit < G:
+            on = (index[0] & bit) != 0
+            pieces = [jnp.where(on, pieces[i ^ bit], pieces[i]) for i in range(G)]
+            bit *= 2
+        return pieces
+
+    for side, one, two in ((0, held_one, held_two), (1, got_one, got_two)):
+        mine = index[2] if side == 0 else 1 - index[2]
+        where = pl.ds(pl.multiple_of(mine * rows, rows), rows)
+        ones = [one[k].astype(F32) for k in range(G)]
+        for k in range(G):
+            out[where, k * part : (k + 1) * part] = ones[k][:, :part]
+        for i, piece in enumerate(in_order([p[:, part:] for p in ones])):
+            qkv[where, (2 * G + i) * part : (2 * G + i + 1) * part] = piece
+        mine = index[1] if side == 0 else 1 - index[1]
+        where = pl.ds(pl.multiple_of(mine * rows, rows), rows)
+        for i, piece in enumerate(in_order([two[k].astype(F32) for k in range(G)])):
+            for j in range(2):
+                qkv[where, (j * G + i) * part : (j * G + i + 1) * part] = piece[
+                    :, j * part : (j + 1) * part
+                ]
 
 
 def norm_parts(value):
@@ -123,32 +231,29 @@
     hidden = up_weight.shape[1] // G
     heads = part // HD
     bits = list(range(replicas.bit_length() - 1))
-    order_a = bits
-    order_b = bits[1:] + bits[:1]
+    first_y = bits
+    first_z = [1, 0] + bits[2:]
+    index = jnp.stack([place, me & 1, (me >> 1) & 1]).astype(jnp.int32)
 
     own_x = tokens[0]
     x_blocks = gather_rows(own_x)
-    qkv_by_dest = qkv_weight.reshape(part, 3, G, part)
-    qkv_rows = [
-        lax.dynamic_index_in_dim(qkv_by_dest, place ^ k, 2, keepdims=False).reshape(part, 3 * part)
-        for k in range(G)
-    ]
+    block = jax.ShapeDtypeStruct((part, 3 * part), BF)
+    qkv_rows = call(pack_kernel, [block] * G, [index, qkv_weight])
     qkv_rows = [qkv_rows[0]] + [gx(qkv_rows[k], k) for k in range(1, G)]
-    small = jnp.concatenate(
-        [qv_bias, out_bias, norm1_gain, norm1_shift, down_bias, norm2_gain, norm2_shift]
-    ).reshape(1, -1)
+    smalls = (qv_bias, out_bias, norm1_gain, norm1_shift, down_bias, norm2_gain, norm2_shift)
+    smalls = after(smalls, qkv_rows[1], x_blocks[1])
+    small = jnp.concatenate(smalls).reshape(1, -1)
     small = jnp.concatenate(xor_order(list(gather_rows(small)), place), axis=0).astype(F32)
     qv = small[:, : 2 * part].reshape(2, width)
     vectors = small[:, 2 * part :].reshape(G, 6, part).transpose(1, 0, 2).reshape(6, width)
     out_b, gain1, shift1, down_b, gain2, shift2 = [vectors[i] for i in range(6)]
+    up_bias = up_bias.astype(F32)
+    qkv_local = jnp.concatenate(xor_order(qkv_rows, place), axis=0)
+    qkv_local, up_weight = lax.optimization_barrier((qkv_local, up_weight))
     up_rows = [
         lax.dynamic_slice_in_dim(up_weight, (place ^ k) * hidden, hidden, 1) for k in range(G)
     ]
     up_rows = [up_rows[0]] + [gx(up_rows[k], k) for k in range(1, G)]
-    up_bias = up_bias.astype(F32)
-
-    qkv_local = jnp.concatenate(xor_order(qkv_rows, place), axis=0)
-    up_local = jnp.concatenate(xor_order(up_rows, place), axis=0)
     own_qv = lax.dynamic_slice_in_dim(qv, place * part, part, 1)
     bias = jnp.concatenate([own_qv[0], jnp.zeros((part,), F32), own_qv[1]])
     segs = segment_ids.reshape(G, rows)
@@ -173,7 +278,8 @@
         attended.append(dot(low, v).astype(BF))
         kept.append((q, k, v, probs, low))
     attended = jnp.concatenate(attended, axis=1)
-    branch = dot(attended, out_weight)
+    branch, up_rows = lax.optimization_barrier((dot(attended, out_weight), up_rows))
+    up_local = jnp.concatenate(xor_order(up_rows, place), axis=0)
     branch = scatter_rows([branch[k * rows : (k + 1) * rows] for k in range(G)])
     first = own_x.astype(F32) + branch + out_b
     hat1, scale1 = norm_parts(first)
@@ -195,65 +301,58 @@
     vec_shift2 = jnp.sum(up_stream, axis=0)
     vec_down = jnp.sum(d_second.astype(F32), axis=0)
     d_second_all = jnp.concatenate(gather_rows(d_second), axis=0)
-    grad_down = t_dot(act, d_second_all).astype(BF)
+    down = Scatter(t_dot(act, d_second_all).astype(BF)[None], first_y, me, replicas)
+    down_got = down.swap(down.send())
     d_pre = (dot_t(d_second_all, down_weight) * slope).astype(BF)
     vec_up = jnp.sum(d_pre.astype(F32), axis=0)
-    grad_up = t_dot(normed_low, d_pre).astype(BF)
     d_normed = dot_t(d_pre, up_local)
-    d_normed = d_sum + scatter_rows([d_normed[k * rows : (k + 1) * rows] for k in range(G)])
-
-    down_piece = replica_scatter(grad_down.reshape(replicas, -1, width), order_a, me, replicas)
-    grad_down = replica_gather(down_piece, order_a, me, replicas).reshape(hidden, width)
-    cut = part // replicas
-
-    def column_grad(value, order):
-        columns = value.shape[1]
-        pieces = value.reshape(G, replicas, cut, columns).transpose(1, 0, 2, 3)
-        mine = replica_scatter(pieces, order, me, replicas)
-        mine = [lax.dynamic_index_in_dim(mine, place ^ k, 0, keepdims=False) for k in range(G)]
-        mine = [mine[0]] + [gx(mine[k], k) for k in range(1, G)]
-        whole = replica_gather(jnp.stack(mine), order, me, replicas)
-        whole = xor_order([whole[:, k].reshape(part, columns).astype(F32) for k in range(G)], place)
-        return jnp.stack(whole, axis=1)
-
-    grad_up = column_grad(grad_up, order_b).reshape(part, G * hidden)
+    far = d_normed[2 * rows : 3 * rows] + gx(d_normed[3 * rows :].astype(BF), 1).astype(F32)
+    far = far.astype(BF)
+    near = gx(d_normed[rows : 2 * rows].astype(BF), 1)
+    grad_up = t_dot(normed_low, after(d_pre, far)).astype(BF).reshape(G, part, hidden)
+    up = Scatter(grad_up, first_z, me, replicas)
+    up_got = up.swap(up.send())
+    d_normed = d_sum + d_normed[:rows] + near.astype(F32) + gx(far, 2).astype(F32)
 
     d_first = norm_back(d_normed, hat1, scale1, gain1)
     vec_gain1 = jnp.sum(d_normed * hat1, axis=0)
     vec_shift1 = jnp.sum(d_normed, axis=0)
     d_branch = d_first.astype(BF)
     vec_out = jnp.sum(d_branch.astype(F32), axis=0)
-    d_branch_all = jnp.concatenate(gather_rows(d_branch), axis=0)
+    d_branch_blocks = gather_rows(d_branch)
+    d_branch_all = jnp.concatenate(d_branch_blocks, axis=0)
+    down_got = down.step(after(down_got, d_branch_blocks[2]))
+    up_got = up.step(after(up_got, d_branch_blocks[2]))
     grad_out = t_dot(attended, d_branch_all).astype(BF)
-    out_piece = replica_scatter(grad_out.reshape(replicas, -1, width), order_a, me, replicas)
-    grad_out = replica_gather(out_piece, order_a, me, replicas).reshape(part, width)
+    grad_out = grad_out.reshape(part, G, part).transpose(1, 0, 2)
     d_att = dot_t(d_branch_all, out_weight).astype(BF)
     d_q, d_k, d_v = [], [], []
     for h in range(heads):
         q, k, v, probs, low = kept[h]
         d_o = d_att[:, h * HD : (h + 1) * HD]
+        d_v.append(t_dot(low, d_o).astype(BF))
         d_probs = dot_t(d_o, v)
         inner = jnp.sum(probs * d_probs, axis=-1, keepdims=True)
         d_scores = (probs * (d_probs - inner)).astype(BF)
         d_q.append((dot(d_scores, k) * scale).astype(BF))
         d_k.append((t_dot(d_scores, q) * scale).astype(BF))
-        d_v.append(t_dot(low, d_o).astype(BF))
-    d_proj = jnp.concatenate(d_q + d_k + d_v, axis=1)
+    d_v = jnp.concatenate(d_v, axis=1)
+    d_qk = jnp.concatenate(d_q + d_k, axis=1)
+    grad_v = t_dot(x_all, d_v).astype(BF).reshape(G, part, part)
+    one = Scatter(jnp.concatenate([grad_out, grad_v], axis=2), first_z, me, replicas)
+    one_send = one.send()
+    grad_qk = t_dot(x_all, d_qk).astype(BF).reshape(G, part, 2 * part)
+    two = Scatter(grad_qk, first_y, me, replicas)
+    two_send = two.send()
+
+    one_got, two_got = one.swap(one_send), two.swap(two_send)
+    down_got = down.step(after(down_got, two_send))
+    up_got = up.step(after(up_got, two_send))
+    d_proj = jnp.concatenate([after(d_qk, two_send), d_v], axis=1)
     sums = jnp.sum(d_proj.astype(F32), axis=0)
-    grad_qkv = t_dot(x_all, d_proj).astype(BF)
-    half = 3 * part // 2
-    grad_qkv = jnp.concatenate(
-        [
-            column_grad(grad_qkv[:, :half], order_a),
-            column_grad(grad_qkv[:, half:], order_b),
-        ],
-        axis=2,
-    )
-    grad_qkv = grad_qkv.reshape(part, G, 3, part).transpose(0, 2, 1, 3).reshape(part, 3 * width)
     d_in = dot_t(d_proj, qkv_local)
-    d_in = d_first + scatter_rows([d_in[k * rows : (k + 1) * rows] for k in range(G)])
-    grad_tokens = d_in.astype(BF)
-
+    far = d_in[2 * rows : 3 * rows] + gx(d_in[3 * rows :].astype(BF), 1).astype(F32)
+    near = gx(d_in[rows : 2 * rows].astype(BF), 1)
     vecs = jnp.concatenate(
         [
             jnp.stack([vec_out, vec_gain1, vec_shift1, vec_down, vec_gain2, vec_shift2]).reshape(-1),
@@ -263,10 +362,78 @@
             ).reshape(-1),
         ]
     ).reshape(-1, width)
-    for bit in range(2):
-        vecs = vecs + gx(vecs, 1 << bit)
-    for bit in bits:
-        vecs = vecs + rx(vecs, 1 << bit, replicas)
+    vecs = vecs + gx(vecs, 1)
+
+    one_got, two_got = one.step(one_got), two.step(two_got)
+    far = gx(after(far.astype(BF), two_got), 2)
+    d_in = d_first + d_in[:rows] + near.astype(F32) + far.astype(F32)
+    grad_tokens = d_in.astype(BF)
+    vecs = vecs + gx(after(vecs, two_got), 2)
+    down_piece = down.piece(after(down_got, one_got, two_got))
+    up_piece = up.piece(after(up_got, one_got, two_got))
+
+    one_got, two_got = one.step(one_got), two.step(two_got)
+
+    def outgoing(pieces):
+        return [lax.dynamic_index_in_dim(pieces, place ^ k, 0, keepdims=False) for k in range(G)]
+
+    def exchange(pieces):
+        return jnp.stack([pieces[0]] + [gx(pieces[k], k) for k in range(1, G)])
+
+    down = Gather(after(down_piece, two_send), first_y, me, replicas)
+    down_got = down.swap()
+    up_piece = exchange(outgoing(up_piece))
+    vecs = vecs + rx(vecs, 1, replicas)
+
+    one_piece, two_piece = one.piece(one_got), two.piece(two_got)
+    mine = jnp.concatenate([one_piece[:, :, part:], two_piece], axis=2)
+    mine = outgoing(mine)
+    qkv_piece = exchange(mine)
+    up = Gather(after(up_piece, mine), first_z, me, replicas)
+    up_got = up.swap()
+    down_got = down.step(after(down_got, mine))
+    vecs = vecs + rx(after(vecs, mine), 2, replicas)
+
+    one = Gather(
+        jnp.concatenate([one_piece[:, :, :part], qkv_piece[:, :, :part]], axis=2),
+        first_z,
+        me,
+        replicas,
+    )
+    two = Gather(qkv_piece[:, :, part:], first_y, me, replicas)
+    one_got, two_got = one.swap(), two.swap()
+    up_got = up.step(after(up_got, one.value))
+    down_got = down.step(after(down_got, one.value))
+    for bit in bits[2:]:
+        vecs = vecs + rx(after(vecs, one.value), 1 << bit, replicas)
+
+    while len(one.left) > 1:
+        one_got, two_got = one.step(one_got), two.step(two_got)
+        if len(up.left) > 1:
+            up_got = up.step(after(up_got, one.value))
+        while len(down.left) > 1:
+            down_got = down.step(after(down_got, one.value))
+    while len(up.left) > 1:
+        up_got = up.step(up_got)
+    grad_down = call(
+        join_kernel,
+        jax.ShapeDtypeStruct((hidden, width), F32),
+        [index, down.value[0], after(down_got, one.value)[0]],
+    )
+    grad_up = call(
+        join_up_kernel,
+        jax.ShapeDtypeStruct((part, G * hidden), F32),
+        [index, up.value, after(up_got, one.value)],
+    )
+    grad_out, grad_qkv = call(
+        join_tail_kernel,
+        [
+            jax.ShapeDtypeStruct((part, width), F32),
+            jax.ShapeDtypeStruct((part, 3 * width), F32),
+        ],
+        [index, one.value, one_got, two.value, two_got],
+    )
+
     six = lax.dynamic_slice_in_dim(vecs[:6], place * part, part, 1)
     vec_up = lax.dynamic_slice_in_dim(vecs[6 : 6 + G].reshape(-1), place * hidden, hidden, 0)
     qvs = jnp.concatenate([vecs[6 + G], vecs[8 + G]])
@@ -276,13 +443,13 @@
         grad_tokens[None],
         grad_qkv,
         vec_qv,
-        grad_out.astype(F32),
+        grad_out,
         six[0],
         six[1],
         six[2],
         grad_up,
         vec_up,
-        grad_down.astype(F32),
+        grad_down,
         six[3],
         six[4],
         six[5],

time: 309 us -> 231 us (0.75)
  local copies, waits for them, and re-layouts: 66.6 us -> 25 us
  waiting for transfers between devices: 111 us -> 80.8 us
  Pallas kernels: 0 us -> 7.3 us
  matrix products: 30.8 us -> 24.4 us
  other arithmetic: 35.3 us -> 30 us
    ppermute x33 -> x27, waiting for transfers between devices: 61.1 us -> 44.8 us  [rx(): return lax.ppermute(value, 'replica', [(i, i ^ bits) for i in range(count)])]
    ppermute x44 -> x41, waiting for transfers between devices: 49.6 us -> 35.9 us  [gx(): return lax.ppermute(value, 'group', [(i, i ^ bits) for i in range(G)])]
    dynamic_update_slice x1, local copies, waits for them, and re-layouts: 13.1 us -> 0.3 us  [on_device(): lax.dynamic_update_slice_in_dim(jnp.zeros((G * hidden,), F32), vec_up, pl...]
    reshape x5 -> x3, local copies, waits for them, and re-layouts: 8.91 us -> 0.41 us  [the longest x2 0.4 us: on_device(): grad_out = grad_out.reshape(part, G, part).transpose(1, 0, 2)]
    pallas_call x0 -> x4, Pallas kernels: none -> 7.3 us  [call(): pl.pallas_call(kernel, out_shape=outs, in_specs=[index_spec()] + [whole_s...]
    select_n x8 -> x0, local copies, waits for them, and re-layouts: 6.83 us -> none  [xor_order(): items = [jnp.where(on, items[i ^ bit], items[i]) for i in range(count)]]
    another operation x31 -> x4, other arithmetic: 5.29 us -> 0.28 us  [the longest x2 0.12 us: exchange(): return jnp.stack([pieces[0]] + [gx(pieces[k], k) for k in range(1, G)])]
    convert_element_type x17 -> x14, other arithmetic: 8.13 us -> 12.8 us  [the longest x8 7.85 us: send(): return self.total(1 - self.mine).astype(BF)]
  transfers between devices with their start and end apart: 77 -> 68, of which waited for: 28 -> 24; matrix products, arithmetic and copies ran while one was open for 31% -> 25% of each run, Pallas kernels for 0% -> 2%
where the time goes in v2:
time: 231 us; the launch traced here: 230 us
  waiting for transfers between devices  80.8 us (35%)
  starting transfers between devices  60.7 us (26%)
  other arithmetic  30 us (13%)
  local copies, waits for them, and re-layouts  25 us (11%)
  matrix products  24.4 us (11%)
  Pallas kernels  7.3 us (3%)
    ppermute x27, waiting for transfers between devices, rx(): return lax.ppermute(value, 'replica', [(i, i ^ bits) for i in range(count)])  44.8 us
    ppermute x41, waiting for transfers between devices, gx(): return lax.ppermute(value, 'group', [(i, i ^ bits) for i in range(G)])  35.9 us
    ppermute x27, starting transfers between devices, rx(): return lax.ppermute(value, 'replica', [(i, i ^ bits) for i in range(count)])  32.7 us
    ppermute x41, starting transfers between devices, gx(): return lax.ppermute(value, 'group', [(i, i ^ bits) for i in range(G)])  28 us
    dot_general x10, matrix products, dot_t(): lax.dot_general(a, b, (((1,), (1,)), ((), ())), preferred_element_type=F32)  9.76 us
    unnamed x156, local copies, waits for them, and re-layouts  9.09 us
    dot_general x11, matrix products, t_dot(): lax.dot_general(a, b, (((0,), (0,)), ((), ())), preferred_element_type=F32)  8.06 us
    convert_element_type x8, other arithmetic, send(): return self.total(1 - self.mine).astype(BF)  7.85 us
  transfers between devices with their start and end apart: 68, of which 24 were waited for; matrix products, arithmetic and copies ran while one was open for 25% of the time, Pallas kernels for 2%

profile of v2, /device:TPU:0, one launch (start us, length us, event | category | flops | bytes accessed | tf_op | source)
XLA Modules:
  0.0 230.3 jit_solution(2519829292761736922)
XLA Ops:
  1.2 2.6 %collective-permute-start.1 = (bf16[128,768]{1,0:T(8,128)(2,1)}, bf16[128,768]{1,0:T(8,128)(2,1)}, u32[]{:S(2)}, u32[]{:S(2)}) collective-permute-start(bf16[128,768]{1,0:T(8,128)(2,1)} %bitcast.128), channel_id=1, source_target_pairs={{0,16},{8,24},{16,0},{24,8},{1,17},{9,25},{17,1},{25,9},{2,18},{10... | collective-permute-start | bytes 589832 | tf_op jit(solution)/shard_map/ppermute | solution.py:18
  6.1 1.9 collective-permute-start.4
  9.8 4.8 %concatenate.85 = bf16[1536]{0:T(1024)(128)(2,1)S(1)} concatenate(bf16[384]{0:T(512)(128)(2,1)} %param.19, bf16[192]{0:T(256)(128)(2,1)} %param.21, bf16[192]{0:T(256)(128)(2,1)} %param.22, bf16[192]{0:T(256)(128)(2,1)} %param.23, bf16[192]{0:T(256)(128)(2,1)} %param.27, bf16[192]{0:T(256)(128)(2,1)} %param.28, bf16[192]{0:T(256)(128)(2,1)} %param.29), dimensions={0} | concatenate | bytes 6144 | tf_op jit(solution)/shard_map/concatenate | solution.py:245
  15.2 1.9 collective-permute-start.6
  17.2 2.9 %collective-permute-done.4 = bf16[192,576]{1,0:T(8,128)(2,1)S(1)} collective-permute-done((bf16[192,576]{1,0:T(8,128)(2,1)S(1)}, bf16[192,576]{1,0:T(8,128)(2,1)S(1)}, u32[]{:S(2)}, u32[]{:S(2)}) %collective-permute-start.4) | collective-permute-done | bytes 221216 | tf_op jit(solution)/shard_map/ppermute | solution.py:18
  22.5 1.8 collective-permute-start.10
  24.6 1.8 fusion.6
  32.6 5.6 %collective-permute-done.11 = bf16[192,768]{1,0:T(8,128)(2,1)} collective-permute-done((bf16[192,768]{1,0:T(8,128)(2,1)}, bf16[192,768]{1,0:T(8,128)(2,1)}, u32[]{:S(2)}, u32[]{:S(2)}) %collective-permute-start.11) | collective-permute-done | bytes 294944 | tf_op jit(solution)/shard_map/ppermute | solution.py:18
  40.5 1.7 collective-permute-start.14
  43.9 3.9 %collective-permute-done.14 = bf16[128,768]{1,0:T(8,128)(2,1)} collective-permute-done((bf16[128,768]{1,0:T(8,128)(2,1)}, bf16[128,768]{1,0:T(8,128)(2,1)}, u32[]{:S(2)}, u32[]{:S(2)}) %collective-permute-start.14) | collective-permute-done | bytes 196640 | tf_op jit(solution)/shard_map/ppermute | solution.py:18
  49.6 1.8 collective-permute-start.16
  51.4 4.4 %collective-permute-done.16 = bf16[128,768]{1,0:T(8,128)(2,1)S(1)} collective-permute-done((bf16[128,768]{1,0:T(8,128)(2,1)S(1)}, bf16[128,768]{1,0:T(8,128)(2,1)S(1)}, u32[]{:S(2)}, u32[]{:S(2)}) %collective-permute-start.16) | collective-permute-done | bytes 196640 | tf_op jit(solution)/shard_map/ppermute | solution.py:18
  57.3 2.0 multiply_convert_fusion
  62.6 1.8 collective-permute-start.20
  66.4 3.6 %collective-permute-done.20 = bf16[128,768]{1,0:T(8,128)(2,1)} collective-permute-done((bf16[128,768]{1,0:T(8,128)(2,1)}, bf16[128,768]{1,0:T(8,128)(2,1)}, u32[]{:S(2)}, u32[]{:S(2)}) %collective-permute-start.20) | collective-permute-done | bytes 196640 | tf_op jit(solution)/shard_map/ppermute | solution.py:18
  73.9 1.8 collective-permute-start.22
  75.7 4.6 %collective-permute-done.22 = bf16[128,768]{1,0:T(8,128)(2,1)S(1)} collective-permute-done((bf16[128,768]{1,0:T(8,128)(2,1)S(1)}, bf16[128,768]{1,0:T(8,128)(2,1)S(1)}, u32[]{:S(2)}, u32[]{:S(2)}) %collective-permute-start.22) | collective-permute-done | bytes 196640 | tf_op jit(solution)/shard_map/ppermute | solution.py:18
  81.8 3.3 %convert_reduce_fusion = (f32[768]{0:T(1024)S(1)}, bf16[512,768]{1,0:T(8,128)(2,1)S(1)}) fusion(f32[512,768]{1,0:T(8,128)} %get-tuple-element.193, bf16[768,768]{1,0:T(8,128)(2,1)S(1)} %copy-done, bf16[128,768]{1,0:T(8,128)(2,1)S(1)} %collective-permute-done.23, bf16[128,768]{1,0:T(8,128)(2,1)S(1)} %collective-permute-done.22, ...), kind=kOutput, calls=%fused_computation.10 | convolution fusion | flops 611843328 | bytes 4328448 | tf_op jit(solution)/shard_map/dot_general | solution.py:30
  87.6 1.8 collective-permute-start.62
  89.5 1.6 collective-permute-start.26
  92.8 1.6 collective-permute-start.53
  94.4 1.8 collective-permute-done.26
  100.4 2.8 %collective-permute-done.62 = bf16[1,384,768]{2,1,0:T(8,128)(2,1)} collective-permute-done((bf16[1,384,768]{2,1,0:T(8,128)(2,1)S(1)}, bf16[1,384,768]{2,1,0:T(8,128)(2,1)}, u32[]{:S(2)}, u32[]{:S(2)}) %collective-permute-start.62) | collective-permute-done | bytes 589856 | tf_op jit(solution)/shard_map/ppermute | solution.py:22
  104.5 1.8 fusion.25
  106.3 1.6 collective-permute-start.63
  108.0 1.8 add_convert_fusion
  118.9 1.7 convolution_convert_fusion.2
  122.9 2.0 fusion.147
  131.3 1.6 collective-permute-start.35
  133.9 2.7 %collective-permute-start.64 = (bf16[1,96,768]{2,1,0:T(8,128)(2,1)S(1)}, bf16[1,96,768]{2,1,0:T(8,128)(2,1)S(1)}, u32[]{:S(2)}, u32[]{:S(2)}) collective-permute-start(bf16[1,96,768]{2,1,0:T(8,128)(2,1)S(1)} %fusion.49), channel_id=1, source_target_pairs={{0,4},{1,5},{2,6},{3,7},{4,0},{5,1},{6,2},{7,3},{8,12},{9,13},{10,... | collective-permute-start | bytes 442376 | tf_op jit(solution)/shard_map/ppermute | solution.py:22
  136.6 1.8 fusion.35
  139.8 4.5 %collective-permute-done.35 = bf16[4,96,384]{2,1,0:T(8,128)(2,1)S(1)} collective-permute-done((bf16[4,96,384]{2,1,0:T(8,128)(2,1)S(1)}, bf16[4,96,384]{2,1,0:T(8,128)(2,1)S(1)}, u32[]{:S(2)}, u32[]{:S(2)}) %collective-permute-start.35) | collective-permute-done | bytes 294944 | tf_op jit(solution)/shard_map/ppermute | solution.py:22
  146.1 1.8 collective-permute-start.55
  148.8 1.7 collective-permute-start.38
  152.9 6.2 %collective-permute-done.55 = bf16[4,24,768]{2,1,0:T(8,128)(2,1)S(1)} collective-permute-done((bf16[4,24,768]{2,1,0:T(8,128)(2,1)S(1)}, bf16[4,24,768]{2,1,0:T(8,128)(2,1)S(1)}, u32[]{:S(2)}, u32[]{:S(2)}) %collective-permute-start.55) | collective-permute-done | bytes 147488 | tf_op jit(solution)/shard_map/ppermute | solution.py:22
  170.6 2.8 %collective-permute-start.59 = (bf16[4,24,768]{2,1,0:T(8,128)(2,1)S(1)}, bf16[4,24,768]{2,1,0:T(8,128)(2,1)S(1)}, u32[]{:S(2)}, u32[]{:S(2)}) collective-permute-start(bf16[4,24,768]{2,1,0:T(8,128)(2,1)S(1)} %pad_maximum_fusion.18), channel_id=1, source_target_pairs={{0,4},{1,5},{2,6},{3,7},{4,0},{5,1},{6,2},{7,3},{8,12},{9,13},{10,... | collective-permute-start | bytes 442376 | tf_op jit(solution)/shard_map/ppermute | solution.py:22
  173.5 4.2 %collective-permute-done.51 = f32[13,768]{1,0:T(8,128)S(1)} collective-permute-done((f32[13,768]{1,0:T(8,128)S(1)}, f32[13,768]{1,0:T(8,128)S(1)}, u32[]{:S(2)}, u32[]{:S(2)}) %collective-permute-start.51) | collective-permute-done | bytes 39968 | tf_op jit(solution)/shard_map/ppermute | solution.py:22
  177.6 3.1 %collective-permute-start.42 = (bf16[4,24,384]{2,1,0:T(8,128)(2,1)S(1)}, bf16[4,24,384]{2,1,0:T(8,128)(2,1)S(1)}, u32[]{:S(2)}, u32[]{:S(2)}) collective-permute-start(bf16[4,24,384]{2,1,0:T(8,128)(2,1)S(1)} %get-tuple-element.163), channel_id=1, source_target_pairs={{0,4},{1,5},{2,6},{3,7},{4,0},{5,1},{6,2},{7,3},{8,12},{9,13},{10,... | collective-permute-start | bytes 221192 | tf_op jit(solution)/shard_map/ppermute | solution.py:22
  180.9 5.8 %collective-permute-done.52 = f32[13,768]{1,0:T(8,128)S(1)} collective-permute-done((f32[13,768]{1,0:T(8,128)S(1)}, f32[13,768]{1,0:T(8,128)S(1)}, u32[]{:S(2)}, u32[]{:S(2)}) %collective-permute-start.52) | collective-permute-done | bytes 39968 | tf_op jit(solution)/shard_map/ppermute | solution.py:22
  187.4 2.5 %collective-permute-start.66 = (bf16[1,192,768]{2,1,0:T(8,128)(2,1)S(1)}, bf16[1,192,768]{2,1,0:T(8,128)(2,1)S(1)}, u32[]{:S(2)}, u32[]{:S(2)}) collective-permute-start(bf16[1,192,768]{2,1,0:T(8,128)(2,1)S(1)} %pad_maximum_fusion.12), channel_id=1, source_target_pairs={{0,2},{1,3},{2,0},{3,1},{4,6},{5,7},{6,4},{7,5},{8,10},{9,11},{10,... | collective-permute-start | bytes 884744 | tf_op jit(solution)/shard_map/ppermute | solution.py:22
  190.0 2.1 collective-permute-done.45
  193.4 3.8 %collective-permute-done.43 = bf16[4,48,384]{2,1,0:T(8,128)(2,1)S(1)} collective-permute-done((bf16[4,48,384]{2,1,0:T(8,128)(2,1)S(1)}, bf16[4,48,384]{2,1,0:T(8,128)(2,1)S(1)}, u32[]{:S(2)}, u32[]{:S(2)}) %collective-permute-start.43) | collective-permute-done | bytes 147488 | tf_op jit(solution)/shard_map/ppermute | solution.py:22
  200.5 4.0 %collective-permute-done.60 = bf16[4,48,768]{2,1,0:T(8,128)(2,1)S(1)} collective-permute-done((bf16[4,48,768]{2,1,0:T(8,128)(2,1)S(1)}, bf16[4,48,768]{2,1,0:T(8,128)(2,1)S(1)}, u32[]{:S(2)}, u32[]{:S(2)}) %collective-permute-start.60) | collective-permute-done | bytes 294944 | tf_op jit(solution)/shard_map/ppermute | solution.py:22
  210.2 2.1 fusion.61
  212.3 11.5 %collective-permute-done.47.got_two = bf16[4,96,384]{2,1,0:T(8,128)(2,1)S(1)} collective-permute-done((bf16[4,96,384]{2,1,0:T(8,128)(2,1)S(1)}, bf16[4,96,384]{2,1,0:T(8,128)(2,1)S(1)}, u32[]{:S(2)}, u32[]{:S(2)}) %collective-permute-start.47) | collective-permute-done | bytes 294944 | tf_op jit(solution)/shard_map/ppermute | solution.py:22
  223.8 2.3 %shard_map.255 = (f32[192,768]{1,0:T(8,128)}, f32[192,2304]{1,0:T(8,128)}) custom-call(s32[3]{0:T(128)S(1)} %pad_add_fusion.1.index, bf16[4,96,384]{2,1,0:T(8,128)(2,1)S(1)} %pad_maximum_fusion.9.held_one, bf16[4,96,384]{2,1,0:T(8,128)(2,1)S(1)} %collective-permute-done.44.got_one, bf16[4,96,384]{2,1,0:T(8,128)(2,1)S(1)} %pad_maximum_fusion.10.held_two, ...), custom_call_target="tpu_custom_call" | custom-call | bytes 3538956 | tf_op jit(solution)/shard_map/pallas_call | solution.py:127
  226.1 2.1 shard_map.257
  228.2 2.1 shard_map.256
  (406 shorter events, 89.0 us)
Async XLA Ops:
  0.7 9.2 %collective-permute-start = (bf16[128,768]{1,0:T(8,128)(2,1)}, bf16[128,768]{1,0:T(8,128)(2,1)S(1)}, u32[]{:S(2)}, u32[]{:S(2)}) collective-permute-start(bf16[128,768]{1,0:T(8,128)(2,1)} %bitcast.127), channel_id=1, source_target_pairs={{0,8},{8,0},{16,24},{24,16},{1,9},{9,1},{17,25},{25,17},{2,10},{10... | collective-permute-start | bytes 589832 | tf_op jit(solution)/shard_map/ppermute | solution.py:18
  1.2 8.6 %collective-permute-start.1 = (bf16[128,768]{1,0:T(8,128)(2,1)}, bf16[128,768]{1,0:T(8,128)(2,1)}, u32[]{:S(2)}, u32[]{:S(2)}) collective-permute-start(bf16[128,768]{1,0:T(8,128)(2,1)} %bitcast.128), channel_id=1, source_target_pairs={{0,16},{8,24},{16,0},{24,8},{1,17},{9,25},{17,1},{25,9},{2,18},{10... | collective-permute-start | bytes 589832 | tf_op jit(solution)/shard_map/ppermute | solution.py:18
  6.0 11.2 %collective-permute-start.3 = (bf16[192,576]{1,0:T(8,128)(2,1)S(1)}, bf16[192,576]{1,0:T(8,128)(2,1)S(1)}, u32[]{:S(2)}, u32[]{:S(2)}) collective-permute-start(bf16[192,576]{1,0:T(8,128)(2,1)S(1)} %get-tuple-element.54), channel_id=1, source_target_pairs={{0,24},{8,16},{16,8},{24,0},{1,25},{9,17},{17,9},{25,1},{2,26},{10... | collective-permute-start | bytes 663560 | tf_op jit(solution)/shard_map/ppermute | solution.py:18
  6.1 14.0 %collective-permute-start.4 = (bf16[192,576]{1,0:T(8,128)(2,1)S(1)}, bf16[192,576]{1,0:T(8,128)(2,1)S(1)}, u32[]{:S(2)}, u32[]{:S(2)}) collective-permute-start(bf16[192,576]{1,0:T(8,128)(2,1)S(1)} %get-tuple-element.55), channel_id=1, source_target_pairs={{0,16},{8,24},{16,0},{24,8},{1,17},{9,25},{17,1},{25,9},{2,18},{10... | collective-permute-start | bytes 663560 | tf_op jit(solution)/shard_map/ppermute | solution.py:18
  9.8 14.8 %collective-permute-start.2 = (bf16[128,768]{1,0:T(8,128)(2,1)}, bf16[128,768]{1,0:T(8,128)(2,1)}, u32[]{:S(2)}, u32[]{:S(2)}) collective-permute-start(bf16[128,768]{1,0:T(8,128)(2,1)} %collective-permute-done.1), channel_id=1, source_target_pairs={{0,8},{8,0},{16,24},{24,16},{1,9},{9,1},{17,25},{25,17},{2,10},{10... | collective-permute-start | bytes 589832 | tf_op jit(solution)/shard_map/ppermute | solution.py:18
  14.7 9.6 %collective-permute-start.8 = (bf16[1,1536]{1,0:T(2,128)(2,1)S(1)}, bf16[1,1536]{1,0:T(2,128)(2,1)S(1)}, u32[]{:S(2)}, u32[]{:S(2)}) collective-permute-start(bf16[1,1536]{1,0:T(2,128)(2,1)S(1)} %reshape.145), channel_id=1, source_target_pairs={{0,8},{8,0},{16,24},{24,16},{1,9},{9,1},{17,25},{25,17},{2,10},{10... | collective-permute-start | bytes 9224 | tf_op jit(solution)/shard_map/ppermute | solution.py:18
  22.5 9.0 %collective-permute-start.9 = (bf16[192,768]{1,0:T(8,128)(2,1)}, bf16[192,768]{1,0:T(8,128)(2,1)}, u32[]{:S(2)}, u32[]{:S(2)}) collective-permute-start(bf16[192,768]{1,0:T(8,128)(2,1)} %get-tuple-element.125), channel_id=1, source_target_pairs={{0,8},{8,0},{16,24},{24,16},{1,9},{9,1},{17,25},{25,17},{2,10},{10... | collective-permute-start | bytes 884744 | tf_op jit(solution)/shard_map/ppermute | solution.py:18
  22.5 10.1 %collective-permute-start.10 = (bf16[192,768]{1,0:T(8,128)(2,1)}, bf16[192,768]{1,0:T(8,128)(2,1)}, u32[]{:S(2)}, u32[]{:S(2)}) collective-permute-start(bf16[192,768]{1,0:T(8,128)(2,1)} %get-tuple-element.124), channel_id=1, source_target_pairs={{0,16},{8,24},{16,0},{24,8},{1,17},{9,25},{17,1},{25,9},{2,18},{10... | collective-permute-start | bytes 884744 | tf_op jit(solution)/shard_map/ppermute | solution.py:18
  24.3 13.9 %collective-permute-start.11 = (bf16[192,768]{1,0:T(8,128)(2,1)}, bf16[192,768]{1,0:T(8,128)(2,1)}, u32[]{:S(2)}, u32[]{:S(2)}) collective-permute-start(bf16[192,768]{1,0:T(8,128)(2,1)} %get-tuple-element.123), channel_id=1, source_target_pairs={{0,24},{8,16},{16,8},{24,0},{1,25},{9,17},{17,9},{25,1},{2,26},{10... | collective-permute-start | bytes 884744 | tf_op jit(solution)/shard_map/ppermute | solution.py:18
  40.5 7.3 %collective-permute-start.14 = (bf16[128,768]{1,0:T(8,128)(2,1)}, bf16[128,768]{1,0:T(8,128)(2,1)}, u32[]{:S(2)}, u32[]{:S(2)}) collective-permute-start(bf16[128,768]{1,0:T(8,128)(2,1)} %add_convert_fusion.2), channel_id=1, source_target_pairs={{0,16},{8,24},{16,0},{24,8},{1,17},{9,25},{17,1},{25,9},{2,18},{10... | collective-permute-start | bytes 589832 | tf_op jit(solution)/shard_map/ppermute | solution.py:18
  49.6 6.3 %collective-permute-start.16 = (bf16[128,768]{1,0:T(8,128)(2,1)S(1)}, bf16[128,768]{1,0:T(8,128)(2,1)S(1)}, u32[]{:S(2)}, u32[]{:S(2)}) collective-permute-start(bf16[128,768]{1,0:T(8,128)(2,1)S(1)} %fusion.46), channel_id=1, source_target_pairs={{0,16},{8,24},{16,0},{24,8},{1,17},{9,25},{17,1},{25,9},{2,18},{10... | collective-permute-start | bytes 589832 | tf_op jit(solution)/shard_map/ppermute | solution.py:18
  51.4 5.9 %collective-permute-start.15 = (bf16[128,768]{1,0:T(8,128)(2,1)S(1)}, bf16[128,768]{1,0:T(8,128)(2,1)S(1)}, u32[]{:S(2)}, u32[]{:S(2)}) collective-permute-start(bf16[128,768]{1,0:T(8,128)(2,1)S(1)} %fusion.46), channel_id=1, source_target_pairs={{0,8},{8,0},{16,24},{24,16},{1,9},{9,1},{17,25},{25,17},{2,10},{10... | collective-permute-start | bytes 589832 | tf_op jit(solution)/shard_map/ppermute | solution.py:18
  62.6 7.5 %collective-permute-start.20 = (bf16[128,768]{1,0:T(8,128)(2,1)}, bf16[128,768]{1,0:T(8,128)(2,1)}, u32[]{:S(2)}, u32[]{:S(2)}) collective-permute-start(bf16[128,768]{1,0:T(8,128)(2,1)} %fusion.42), channel_id=1, source_target_pairs={{0,16},{8,24},{16,0},{24,8},{1,17},{9,25},{17,1},{25,9},{2,18},{10... | collective-permute-start | bytes 589832 | tf_op jit(solution)/shard_map/ppermute | solution.py:18
  73.9 6.4 %collective-permute-start.22 = (bf16[128,768]{1,0:T(8,128)(2,1)S(1)}, bf16[128,768]{1,0:T(8,128)(2,1)S(1)}, u32[]{:S(2)}, u32[]{:S(2)}) collective-permute-start(bf16[128,768]{1,0:T(8,128)(2,1)S(1)} %get-tuple-element.110), channel_id=1, source_target_pairs={{0,16},{8,24},{16,0},{24,8},{1,17},{9,25},{17,1},{25,9},{2,18},{10... | collective-permute-start | bytes 589832 | tf_op jit(solution)/shard_map/ppermute | solution.py:18
  86.3 8.1 %collective-permute-start.24 = (bf16[128,768]{1,0:T(8,128)(2,1)S(1)}, bf16[128,768]{1,0:T(8,128)(2,1)S(1)}, u32[]{:S(2)}, u32[]{:S(2)}) collective-permute-start(bf16[128,768]{1,0:T(8,128)(2,1)S(1)} %get-tuple-element.133), channel_id=1, source_target_pairs={{0,8},{8,0},{16,24},{24,16},{1,9},{9,1},{17,25},{25,17},{2,10},{10... | collective-permute-start | bytes 589832 | tf_op jit(solution)/shard_map/ppermute | solution.py:18
  87.6 15.6 %collective-permute-start.62 = (bf16[1,384,768]{2,1,0:T(8,128)(2,1)S(1)}, bf16[1,384,768]{2,1,0:T(8,128)(2,1)}, u32[]{:S(2)}, u32[]{:S(2)}) collective-permute-start(bf16[1,384,768]{2,1,0:T(8,128)(2,1)S(1)} %dynamic-slice_bitcast_fusion), channel_id=1, source_target_pairs={{0,1},{1,0},{2,3},{3,2},{4,5},{5,4},{6,7},{7,6},{8,9},{9,8},{10,11... | collective-permute-start | bytes 1769480 | tf_op jit(solution)/shard_map/ppermute | solution.py:22
  89.5 6.7 %collective-permute-start.26 = (bf16[128,768]{1,0:T(8,128)(2,1)S(1)}, bf16[128,768]{1,0:T(8,128)(2,1)S(1)}, u32[]{:S(2)}, u32[]{:S(2)}) collective-permute-start(bf16[128,768]{1,0:T(8,128)(2,1)S(1)} %fusion.39), channel_id=1, source_target_pairs={{0,16},{8,24},{16,0},{24,8},{1,17},{9,25},{17,1},{25,9},{2,18},{10... | collective-permute-start | bytes 589832 | tf_op jit(solution)/shard_map/ppermute | solution.py:18
  92.8 15.1 %collective-permute-start.53 = (bf16[4,96,768]{2,1,0:T(8,128)(2,1)}, bf16[4,96,768]{2,1,0:T(8,128)(2,1)}, u32[]{:S(2)}, u32[]{:S(2)}) collective-permute-start(bf16[4,96,768]{2,1,0:T(8,128)(2,1)} %constant_dynamic-slice_fusion.1), channel_id=1, source_target_pairs={{0,2},{1,3},{2,0},{3,1},{4,6},{5,7},{6,4},{7,5},{8,10},{9,11},{10,... | collective-permute-start | bytes 1769480 | tf_op jit(solution)/shard_map/ppermute | solution.py:22
  98.4 6.1 %collective-permute-start.28 = (bf16[128,768]{1,0:T(8,128)(2,1)}, bf16[128,768]{1,0:T(8,128)(2,1)S(1)}, u32[]{:S(2)}, u32[]{:S(2)}) collective-permute-start(bf16[128,768]{1,0:T(8,128)(2,1)} %get-tuple-element.112), channel_id=1, source_target_pairs={{0,16},{8,24},{16,0},{24,8},{1,17},{9,25},{17,1},{25,9},{2,18},{10... | collective-permute-start | bytes 589832 | tf_op jit(solution)/shard_map/ppermute | solution.py:18
  100.3 10.0 %collective-permute-start.27 = (bf16[128,768]{1,0:T(8,128)(2,1)}, bf16[128,768]{1,0:T(8,128)(2,1)S(1)}, u32[]{:S(2)}, u32[]{:S(2)}) collective-permute-start(bf16[128,768]{1,0:T(8,128)(2,1)} %get-tuple-element.112), channel_id=1, source_target_pairs={{0,8},{8,0},{16,24},{24,16},{1,9},{9,1},{17,25},{25,17},{2,10},{10... | collective-permute-start | bytes 589832 | tf_op jit(solution)/shard_map/ppermute | solution.py:18
  104.5 5.8 %collective-permute-start.29 = (bf16[128,768]{1,0:T(8,128)(2,1)S(1)}, bf16[128,768]{1,0:T(8,128)(2,1)S(1)}, u32[]{:S(2)}, u32[]{:S(2)}) collective-permute-start(bf16[128,768]{1,0:T(8,128)(2,1)S(1)} %collective-permute-done.28), channel_id=1, source_target_pairs={{0,8},{8,0},{16,24},{24,16},{1,9},{9,1},{17,25},{25,17},{2,10},{10... | collective-permute-start | bytes 589832 | tf_op jit(solution)/shard_map/ppermute | solution.py:18
  106.3 26.6 %collective-permute-start.63 = (bf16[1,192,768]{2,1,0:T(8,128)(2,1)}, bf16[1,192,768]{2,1,0:T(8,128)(2,1)S(1)}, u32[]{:S(2)}, u32[]{:S(2)}) collective-permute-start(bf16[1,192,768]{2,1,0:T(8,128)(2,1)} %fusion.25), channel_id=1, source_target_pairs={{0,2},{1,3},{2,0},{3,1},{4,6},{5,7},{6,4},{7,5},{8,10},{9,11},{10,... | collective-permute-start | bytes 884744 | tf_op jit(solution)/shard_map/ppermute | solution.py:22
  109.8 28.5 %collective-permute-start.54 = (bf16[4,48,768]{2,1,0:T(8,128)(2,1)}, bf16[4,48,768]{2,1,0:T(8,128)(2,1)}, u32[]{:S(2)}, u32[]{:S(2)}) collective-permute-start(bf16[4,48,768]{2,1,0:T(8,128)(2,1)} %add_convert_fusion), channel_id=1, source_target_pairs={{0,1},{1,0},{2,3},{3,2},{4,5},{5,4},{6,7},{7,6},{8,9},{9,8},{10,11... | collective-permute-start | bytes 884744 | tf_op jit(solution)/shard_map/ppermute | solution.py:22
  121.3 17.0 %collective-permute-start.32 = (bf16[4,96,384]{2,1,0:T(8,128)(2,1)}, bf16[4,96,384]{2,1,0:T(8,128)(2,1)}, u32[]{:S(2)}, u32[]{:S(2)}) collective-permute-start(bf16[4,96,384]{2,1,0:T(8,128)(2,1)} %constant_dynamic-slice_fusion.4), channel_id=1, source_target_pairs={{0,1},{1,0},{2,3},{3,2},{4,5},{5,4},{6,7},{7,6},{8,9},{9,8},{10,11... | collective-permute-start | bytes 884744 | tf_op jit(solution)/shard_map/ppermute | solution.py:22
  125.7 10.9 %collective-permute-start.31 = (bf16[128,768]{1,0:T(8,128)(2,1)S(1)}, bf16[128,768]{1,0:T(8,128)(2,1)}, u32[]{:S(2)}, u32[]{:S(2)}) collective-permute-start(bf16[128,768]{1,0:T(8,128)(2,1)S(1)} %get-tuple-element.132), channel_id=1, source_target_pairs={{0,8},{8,0},{16,24},{24,16},{1,9},{9,1},{17,25},{25,17},{2,10},{10... | collective-permute-start | bytes 589832 | tf_op jit(solution)/shard_map/ppermute | solution.py:18
  131.3 13.0 %collective-permute-start.35 = (bf16[4,96,384]{2,1,0:T(8,128)(2,1)S(1)}, bf16[4,96,384]{2,1,0:T(8,128)(2,1)S(1)}, u32[]{:S(2)}, u32[]{:S(2)}) collective-permute-start(bf16[4,96,384]{2,1,0:T(8,128)(2,1)S(1)} %fusion.47), channel_id=1, source_target_pairs={{0,2},{1,3},{2,0},{3,1},{4,6},{5,7},{6,4},{7,5},{8,10},{9,11},{10,... | collective-permute-start | bytes 884744 | tf_op jit(solution)/shard_map/ppermute | solution.py:22
  133.9 26.4 %collective-permute-start.64 = (bf16[1,96,768]{2,1,0:T(8,128)(2,1)S(1)}, bf16[1,96,768]{2,1,0:T(8,128)(2,1)S(1)}, u32[]{:S(2)}, u32[]{:S(2)}) collective-permute-start(bf16[1,96,768]{2,1,0:T(8,128)(2,1)S(1)} %fusion.49), channel_id=1, source_target_pairs={{0,4},{1,5},{2,6},{3,7},{4,0},{5,1},{6,2},{7,3},{8,12},{9,13},{10,... | collective-permute-start | bytes 442376 | tf_op jit(solution)/shard_map/ppermute | solution.py:22
  139.3 8.6 %collective-permute-start.33 = (bf16[4,48,384]{2,1,0:T(8,128)(2,1)S(1)}, bf16[4,48,384]{2,1,0:T(8,128)(2,1)S(1)}, u32[]{:S(2)}, u32[]{:S(2)}) collective-permute-start(bf16[4,48,384]{2,1,0:T(8,128)(2,1)S(1)} %add_convert_fusion.6), channel_id=1, source_target_pairs={{0,2},{1,3},{2,0},{3,1},{4,6},{5,7},{6,4},{7,5},{8,10},{9,11},{10,... | collective-permute-start | bytes 442376 | tf_op jit(solution)/shard_map/ppermute | solution.py:22
  144.4 6.1 %collective-permute-start.36 = (bf16[4,48,384]{2,1,0:T(8,128)(2,1)S(1)}, bf16[4,48,384]{2,1,0:T(8,128)(2,1)S(1)}, u32[]{:S(2)}, u32[]{:S(2)}) collective-permute-start(bf16[4,48,384]{2,1,0:T(8,128)(2,1)S(1)} %add_convert_fusion.5), channel_id=1, source_target_pairs={{0,1},{1,0},{2,3},{3,2},{4,5},{5,4},{6,7},{7,6},{8,9},{9,8},{10,11... | collective-permute-start | bytes 442376 | tf_op jit(solution)/shard_map/ppermute | solution.py:22
  146.1 12.9 %collective-permute-start.55 = (bf16[4,24,768]{2,1,0:T(8,128)(2,1)S(1)}, bf16[4,24,768]{2,1,0:T(8,128)(2,1)S(1)}, u32[]{:S(2)}, u32[]{:S(2)}) collective-permute-start(bf16[4,24,768]{2,1,0:T(8,128)(2,1)S(1)} %add_convert_fusion.4), channel_id=1, source_target_pairs={{0,4},{1,5},{2,6},{3,7},{4,0},{5,1},{6,2},{7,3},{8,12},{9,13},{10,... | collective-permute-start | bytes 442376 | tf_op jit(solution)/shard_map/ppermute | solution.py:22
  148.8 14.7 %collective-permute-start.38 = (bf16[4,24,384]{2,1,0:T(8,128)(2,1)S(1)}, bf16[4,24,384]{2,1,0:T(8,128)(2,1)S(1)}, u32[]{:S(2)}, u32[]{:S(2)}) collective-permute-start(bf16[4,24,384]{2,1,0:T(8,128)(2,1)S(1)} %add_convert_fusion.8), channel_id=1, source_target_pairs={{0,4},{1,5},{2,6},{3,7},{4,0},{5,1},{6,2},{7,3},{8,12},{9,13},{10,... | collective-permute-start | bytes 221192 | tf_op jit(solution)/shard_map/ppermute | solution.py:22
  150.6 12.6 %collective-permute-start.37 = (bf16[4,24,384]{2,1,0:T(8,128)(2,1)S(1)}, bf16[4,24,384]{2,1,0:T(8,128)(2,1)S(1)}, u32[]{:S(2)}, u32[]{:S(2)}) collective-permute-start(bf16[4,24,384]{2,1,0:T(8,128)(2,1)S(1)} %add_convert_fusion.10), channel_id=1, source_target_pairs={{0,4},{1,5},{2,6},{3,7},{4,0},{5,1},{6,2},{7,3},{8,12},{9,13},{10,... | collective-permute-start | bytes 221192 | tf_op jit(solution)/shard_map/ppermute | solution.py:22
  152.0 10.4 %collective-permute-start.49 = (f32[13,768]{1,0:T(8,128)S(1)}, f32[13,768]{1,0:T(8,128)S(1)}, u32[]{:S(2)}, u32[]{:S(2)}) collective-permute-start(f32[13,768]{1,0:T(8,128)S(1)} %add.493), channel_id=1, source_target_pairs={{0,16},{8,24},{16,0},{24,8},{1,17},{9,25},{17,1},{25,9},{2,18},{10... | collective-permute-start | bytes 119816 | tf_op jit(solution)/shard_map/ppermute | solution.py:18
  160.2 5.9 %collective-permute-start.58 = (bf16[24,768]{1,0:T(8,128)(2,1)S(1)}, bf16[24,768]{1,0:T(8,128)(2,1)S(1)}, u32[]{:S(2)}, u32[]{:S(2)}) collective-permute-start(bf16[24,768]{1,0:T(8,128)(2,1)S(1)} %get-tuple-element.155), channel_id=1, source_target_pairs={{0,24},{8,16},{16,8},{24,0},{1,25},{9,17},{17,9},{25,1},{2,26},{10... | collective-permute-start | bytes 110600 | tf_op jit(solution)/shard_map/ppermute | solution.py:18
  160.3 6.1 %collective-permute-start.57 = (bf16[24,768]{1,0:T(8,128)(2,1)S(1)}, bf16[24,768]{1,0:T(8,128)(2,1)S(1)}, u32[]{:S(2)}, u32[]{:S(2)}) collective-permute-start(bf16[24,768]{1,0:T(8,128)(2,1)S(1)} %get-tuple-element.156), channel_id=1, source_target_pairs={{0,16},{8,24},{16,0},{24,8},{1,17},{9,25},{17,1},{25,9},{2,18},{10... | collective-permute-start | bytes 110600 | tf_op jit(solution)/shard_map/ppermute | solution.py:18
  163.2 17.5 %collective-permute-start.65 = (bf16[1,96,768]{2,1,0:T(8,128)(2,1)S(1)}, bf16[1,96,768]{2,1,0:T(8,128)(2,1)S(1)}, u32[]{:S(2)}, u32[]{:S(2)}) collective-permute-start(bf16[1,96,768]{2,1,0:T(8,128)(2,1)S(1)} %fusion.52), channel_id=1, source_target_pairs={{0,4},{1,5},{2,6},{3,7},{4,0},{5,1},{6,2},{7,3},{8,12},{9,13},{10,... | collective-permute-start | bytes 442376 | tf_op jit(solution)/shard_map/ppermute | solution.py:22
  168.1 38.3 %collective-permute-start.30 = (bf16[128,768]{1,0:T(8,128)(2,1)S(1)}, bf16[128,768]{1,0:T(8,128)(2,1)S(1)}, u32[]{:S(2)}, u32[]{:S(2)}) collective-permute-start(bf16[128,768]{1,0:T(8,128)(2,1)S(1)} %copy-done.32), channel_id=1, source_target_pairs={{0,8},{8,0},{16,24},{24,16},{1,9},{9,1},{17,25},{25,17},{2,10},{10... | collective-permute-start | bytes 589832 | tf_op jit(solution)/shard_map/ppermute | solution.py:18
  169.8 40.5 %collective-permute-start.34 = (bf16[128,768]{1,0:T(8,128)(2,1)}, bf16[128,768]{1,0:T(8,128)(2,1)}, u32[]{:S(2)}, u32[]{:S(2)}) collective-permute-start(bf16[128,768]{1,0:T(8,128)(2,1)} %fusion.35), channel_id=1, source_target_pairs={{0,16},{8,24},{16,0},{24,8},{1,17},{9,25},{17,1},{25,9},{2,18},{10... | collective-permute-start | bytes 589832 | tf_op jit(solution)/shard_map/ppermute | solution.py:18
  170.6 22.7 %collective-permute-start.59 = (bf16[4,24,768]{2,1,0:T(8,128)(2,1)S(1)}, bf16[4,24,768]{2,1,0:T(8,128)(2,1)S(1)}, u32[]{:S(2)}, u32[]{:S(2)}) collective-permute-start(bf16[4,24,768]{2,1,0:T(8,128)(2,1)S(1)} %pad_maximum_fusion.18), channel_id=1, source_target_pairs={{0,4},{1,5},{2,6},{3,7},{4,0},{5,1},{6,2},{7,3},{8,12},{9,13},{10,... | collective-permute-start | bytes 442376 | tf_op jit(solution)/shard_map/ppermute | solution.py:22
  177.6 9.7 %collective-permute-start.42 = (bf16[4,24,384]{2,1,0:T(8,128)(2,1)S(1)}, bf16[4,24,384]{2,1,0:T(8,128)(2,1)S(1)}, u32[]{:S(2)}, u32[]{:S(2)}) collective-permute-start(bf16[4,24,384]{2,1,0:T(8,128)(2,1)S(1)} %get-tuple-element.163), channel_id=1, source_target_pairs={{0,4},{1,5},{2,6},{3,7},{4,0},{5,1},{6,2},{7,3},{8,12},{9,13},{10,... | collective-permute-start | bytes 221192 | tf_op jit(solution)/shard_map/ppermute | solution.py:22
  180.7 5.9 %collective-permute-start.52 = (f32[13,768]{1,0:T(8,128)S(1)}, f32[13,768]{1,0:T(8,128)S(1)}, u32[]{:S(2)}, u32[]{:S(2)}) collective-permute-start(f32[13,768]{1,0:T(8,128)S(1)} %add.496), channel_id=1, source_target_pairs={{0,4},{1,5},{2,6},{3,7},{4,0},{5,1},{6,2},{7,3},{8,12},{9,13},{10,... | collective-permute-start | bytes 119816 | tf_op jit(solution)/shard_map/ppermute | solution.py:22
  187.4 11.2 %collective-permute-start.66 = (bf16[1,192,768]{2,1,0:T(8,128)(2,1)S(1)}, bf16[1,192,768]{2,1,0:T(8,128)(2,1)S(1)}, u32[]{:S(2)}, u32[]{:S(2)}) collective-permute-start(bf16[1,192,768]{2,1,0:T(8,128)(2,1)S(1)} %pad_maximum_fusion.12), channel_id=1, source_target_pairs={{0,2},{1,3},{2,0},{3,1},{4,6},{5,7},{6,4},{7,5},{8,10},{9,11},{10,... | collective-permute-start | bytes 884744 | tf_op jit(solution)/shard_map/ppermute | solution.py:22
  193.3 12.9 %collective-permute-start.46 = (bf16[4,48,384]{2,1,0:T(8,128)(2,1)S(1)}, bf16[4,48,384]{2,1,0:T(8,128)(2,1)S(1)}, u32[]{:S(2)}, u32[]{:S(2)}) collective-permute-start(bf16[4,48,384]{2,1,0:T(8,128)(2,1)S(1)} %pad_maximum_fusion.17), channel_id=1, source_target_pairs={{0,2},{1,3},{2,0},{3,1},{4,6},{5,7},{6,4},{7,5},{8,10},{9,11},{10,... | collective-permute-start | bytes 442376 | tf_op jit(solution)/shard_map/ppermute | solution.py:22
  197.2 7.3 %collective-permute-start.60 = (bf16[4,48,768]{2,1,0:T(8,128)(2,1)S(1)}, bf16[4,48,768]{2,1,0:T(8,128)(2,1)S(1)}, u32[]{:S(2)}, u32[]{:S(2)}) collective-permute-start(bf16[4,48,768]{2,1,0:T(8,128)(2,1)S(1)} %pad_maximum_fusion.11), channel_id=1, source_target_pairs={{0,1},{1,0},{2,3},{3,2},{4,5},{5,4},{6,7},{7,6},{8,9},{9,8},{10,11... | collective-permute-start | bytes 884744 | tf_op jit(solution)/shard_map/ppermute | solution.py:22
  198.6 13.7 %collective-permute-start.44 = (bf16[4,96,384]{2,1,0:T(8,128)(2,1)S(1)}, bf16[4,96,384]{2,1,0:T(8,128)(2,1)S(1)}, u32[]{:S(2)}, u32[]{:S(2)}) collective-permute-start(bf16[4,96,384]{2,1,0:T(8,128)(2,1)S(1)} %pad_maximum_fusion.9.held_one), channel_id=1, source_target_pairs={{0,2},{1,3},{2,0},{3,1},{4,6},{5,7},{6,4},{7,5},{8,10},{9,11},{10,... | collective-permute-start | bytes 884744 | tf_op jit(solution)/shard_map/ppermute | solution.py:22
  204.5 21.6 %collective-permute-start.67 = (bf16[1,384,768]{2,1,0:T(8,128)(2,1)}, bf16[1,384,768]{2,1,0:T(8,128)(2,1)S(1)}, u32[]{:S(2)}, u32[]{:S(2)}) collective-permute-start(bf16[1,384,768]{2,1,0:T(8,128)(2,1)} %get-tuple-element.139), channel_id=1, source_target_pairs={{0,1},{1,0},{2,3},{3,2},{4,5},{5,4},{6,7},{7,6},{8,9},{9,8},{10,11... | collective-permute-start | bytes 1769480 | tf_op jit(solution)/shard_map/ppermute | solution.py:22
  206.2 22.0 %collective-permute-start.61 = (bf16[4,96,768]{2,1,0:T(8,128)(2,1)S(1)}, bf16[4,96,768]{2,1,0:T(8,128)(2,1)S(1)}, u32[]{:S(2)}, u32[]{:S(2)}) collective-permute-start(bf16[4,96,768]{2,1,0:T(8,128)(2,1)S(1)} %pad_maximum_fusion.7.held), channel_id=1, source_target_pairs={{0,2},{1,3},{2,0},{3,1},{4,6},{5,7},{6,4},{7,5},{8,10},{9,11},{10,... | collective-permute-start | bytes 1769480 | tf_op jit(solution)/shard_map/ppermute | solution.py:22
  207.1 16.7 %collective-permute-start.47 = (bf16[4,96,384]{2,1,0:T(8,128)(2,1)S(1)}, bf16[4,96,384]{2,1,0:T(8,128)(2,1)S(1)}, u32[]{:S(2)}, u32[]{:S(2)}) collective-permute-start(bf16[4,96,384]{2,1,0:T(8,128)(2,1)S(1)} %pad_maximum_fusion.10.held_two), channel_id=1, source_target_pairs={{0,1},{1,0},{2,3},{3,2},{4,5},{5,4},{6,7},{7,6},{8,9},{9,8},{10,11... | collective-permute-start | bytes 884744 | tf_op jit(solution)/shard_map/ppermute | solution.py:22
  (98 other events, 390.8 us)

commit v3 on v2

--- a/solution.py
+++ b/solution.py
@@ -10,6 +10,7 @@
 HD = 64
 G = 4
 EPS = 1e-05
+VECS = 16
 BF = jnp.bfloat16
 F32 = jnp.float32
 
@@ -73,10 +74,14 @@
         ]
         return sum(cut[1:], cut[0])
 
-    def send(self):
+    def begin(self):
         self.rows //= 2
         self.mine = (self.me >> self.left[0]) & 1
-        return self.total(1 - self.mine).astype(BF)
+
+    def send(self):
+        self.begin()
+        self.sent = self.total(1 - self.mine).astype(BF)
+        return self.sent
 
     def swap(self, half):
         return rx(half, 1 << self.left.pop(0), self.count)
@@ -95,13 +100,22 @@
 
 
 class Gather:
-    def __init__(self, value, order, me, count):
+    def __init__(self, value, order, me, count, vecs=None):
         self.value, self.left, self.me, self.count = value, list(order), me, count
+        self.vecs = vecs
 
     def swap(self):
-        return rx(self.value, 1 << self.left[-1], self.count)
+        sent = self.value
+        if self.vecs is not None:
+            sent = sent.reshape(-1, sent.shape[2])
+            sent = jnp.concatenate([sent, self.vecs.astype(BF)], axis=0)
+        return rx(sent, 1 << self.left[-1], self.count)
 
     def take(self, got):
+        if self.vecs is not None:
+            blocks, rows, columns = self.value.shape
+            self.vecs = self.vecs + got[blocks * rows :].astype(F32)
+            got = got[: blocks * rows].reshape(blocks, rows, columns)
         on = ((self.me >> self.left.pop()) & 1) != 0
         self.value = jnp.concatenate(
             [jnp.where(on, got, self.value), jnp.where(on, self.value, got)], axis=1
@@ -120,17 +134,16 @@
     return pl.BlockSpec(memory_space=pltpu.SMEM)
 
 
-def call(kernel, out_shape, inputs, flops=0):
+def call(kernel, out_shape, inputs):
     single = not isinstance(out_shape, (list, tuple))
     outs = [out_shape] if single else list(out_shape)
-    moved = sum(v.size * v.dtype.itemsize for v in list(inputs) + outs)
     got = pl.pallas_call(
         kernel,
         out_shape=outs,
         in_specs=[index_spec()] + [whole_spec()] * (len(inputs) - 1),
         out_specs=[whole_spec()] * len(outs),
         compiler_params=pltpu.CompilerParams(vmem_limit_bytes=48 * 1024 * 1024),
-        cost_estimate=pl.CostEstimate(flops=flops, bytes_accessed=moved, transcendentals=0),
+        cost_estimate=pl.CostEstimate(flops=0, bytes_accessed=0, transcendentals=0),
     )(*inputs)
     return got[0] if single else got
 
@@ -164,7 +177,7 @@
         out[pl.ds(pl.multiple_of((1 - mine) * rows, rows), rows), where] = got[k].astype(F32)
 
 
-def join_tail_kernel(index, held_one, got_one, held_two, got_two, out, qkv):
+def join_tail_kernel(index, held_one, got_one, held_two, got_two, vecs, out, qkv, sums):
     rows, part = held_one.shape[1], held_one.shape[2] // 2
 
     def in_order(pieces):
@@ -185,11 +198,96 @@
             qkv[where, (2 * G + i) * part : (2 * G + i + 1) * part] = piece
         mine = index[1] if side == 0 else 1 - index[1]
         where = pl.ds(pl.multiple_of(mine * rows, rows), rows)
-        for i, piece in enumerate(in_order([two[k].astype(F32) for k in range(G)])):
+        if side == 0:
+            twos = [two[k].astype(F32) for k in range(G)]
+        else:
+            twos = [two[k * rows : (k + 1) * rows, :].astype(F32) for k in range(G)]
+        for i, piece in enumerate(in_order(twos)):
             for j in range(2):
                 qkv[where, (j * G + i) * part : (j * G + i + 1) * part] = piece[
                     :, j * part : (j + 1) * part
                 ]
+    sums[...] = vecs[...] + got_two[G * held_two.shape[1] :, :].astype(F32)
+
+
+def attention_back_kernel(index, d_branch, out_weight, proj, lse, seg_key, seg_query, attended, x, *outs):
+    d_qk, d_v, one, two, one_send, two_send = outs
+    part = out_weight.shape[0]
+    scale = HD**-0.5
+    d_att = dot_t(out_weight[...], d_branch[...]).astype(BF)
+    same = seg_key[...] == seg_query[...]
+    for h in range(part // HD):
+        at = h * HD
+        q = proj[at : at + HD, :]
+        k = proj[part + at : part + at + HD, :]
+        v = proj[2 * part + at : 2 * part + at + HD, :]
+        d_o = d_att[at : at + HD, :]
+        scores = jnp.where(same, t_dot(k, q) * scale, jnp.float32(-1e30))
+        probs = jnp.exp(scores - lse[h : h + 1, :])
+        d_probs = t_dot(v, d_o)
+        inner = jnp.sum(probs * d_probs, axis=0, keepdims=True)
+        d_scores = (probs * (d_probs - inner)).astype(BF)
+        d_v[at : at + HD, :] = dot_t(d_o, probs.astype(BF)).astype(BF)
+        d_qk[at : at + HD, :] = (dot(k, d_scores) * scale).astype(BF)
+        d_qk[part + at : part + at + HD, :] = (dot_t(q, d_scores) * scale).astype(BF)
+    grad_out = dot(attended[...], d_branch[...])
+    grad_v = dot_t(x[...], d_v[...])
+    grad_qk = dot_t(x[...], d_qk[...])
+    for i in range(G):
+        where = slice(i * part, (i + 1) * part)
+        one[i] = jnp.concatenate([grad_out[:, where], grad_v[where, :]], axis=1).astype(BF)
+        two[i] = grad_qk[where, :].astype(BF)
+    keep = part // 2
+    one_side = pl.ds(pl.multiple_of((1 - index[2]) * keep, keep), keep)
+    two_side = pl.ds(pl.multiple_of((1 - index[1]) * keep, keep), keep)
+    for i in range(G):
+        one_send[i] = one[i, one_side, :]
+        two_send[i] = two[i, two_side, :]
+
+
+def input_grad_kernel(index, d_qk, d_v, weight, *refs):
+    vectors, (near, far_send, own, far, vecs) = refs[:7], refs[7:]
+    rows, width = own.shape
+    part, total = d_v.shape
+    for block, out in enumerate((own, near, far, far_send)):
+        where = pl.ds(block * rows, rows)
+        value = lax.dot_general(
+            d_qk[:, where],
+            weight[:, : 2 * part],
+            (((0,), (1,)), ((), ())),
+            preferred_element_type=F32,
+        )
+        value += lax.dot_general(
+            d_v[:, where],
+            weight[:, 2 * part :],
+            (((0,), (1,)), ((), ())),
+            preferred_element_type=F32,
+        )
+        if block == 3:
+            out[:rows, :] = value.astype(BF)
+        else:
+            out[...] = value.astype(out.dtype)
+    ones = jnp.ones((8, total), BF)
+    sums = dot_t(ones, d_qk[...])[:1]
+    sums = [sums[:, :part], sums[:, part:], dot_t(ones, d_v[...])[:1]]
+    lines = [vector[...] for vector in vectors[:6]]
+    lines += [jnp.where(index[0] == i, vectors[6][...], 0.0) for i in range(G)]
+    for j in range(3):
+        lines.append(
+            jnp.concatenate([jnp.where(index[0] == i, sums[j], 0.0) for i in range(G)], axis=1)
+        )
+    lines.append(jnp.zeros((VECS - len(lines), width), F32))
+    value = jnp.concatenate(lines, axis=0)
+    vecs[...] = value
+    far_send[rows:, :] = value.astype(BF)
+
+
+def add_two_kernel(index, far, vecs, got, far_out, vecs_out):
+    rows = far.shape[0]
+    far_out[:rows, :] = (far[...] + got[:rows, :].astype(F32)).astype(BF)
+    value = vecs[...] + got[rows:, :].astype(F32)
+    vecs_out[...] = value
+    far_out[rows:, :] = value.astype(BF)
 
 
 def norm_parts(value):
@@ -243,16 +341,17 @@
     smalls = (qv_bias, out_bias, norm1_gain, norm1_shift, down_bias, norm2_gain, norm2_shift)
     smalls = after(smalls, qkv_rows[1], x_blocks[1])
     small = jnp.concatenate(smalls).reshape(1, -1)
-    small = jnp.concatenate(xor_order(list(gather_rows(small)), place), axis=0).astype(F32)
-    qv = small[:, : 2 * part].reshape(2, width)
-    vectors = small[:, 2 * part :].reshape(G, 6, part).transpose(1, 0, 2).reshape(6, width)
+    small_all = jnp.concatenate(xor_order(list(gather_rows(small)), place), axis=0).astype(F32)
+    qv = small_all[:, : 2 * part].reshape(2, width)
+    vectors = small_all[:, 2 * part :].reshape(G, 6, part).transpose(1, 0, 2).reshape(6, width)
     out_b, gain1, shift1, down_b, gain2, shift2 = [vectors[i] for i in range(6)]
     up_bias = up_bias.astype(F32)
     qkv_local = jnp.concatenate(xor_order(qkv_rows, place), axis=0)
-    qkv_local, up_weight = lax.optimization_barrier((qkv_local, up_weight))
+    up_weight = after(up_weight, small)
     up_rows = [
         lax.dynamic_slice_in_dim(up_weight, (place ^ k) * hidden, hidden, 1) for k in range(G)
     ]
+    qkv_local = after(qkv_local, up_rows)
     up_rows = [up_rows[0]] + [gx(up_rows[k], k) for k in range(1, G)]
     own_qv = lax.dynamic_slice_in_dim(qv, place * part, part, 1)
     bias = jnp.concatenate([own_qv[0], jnp.zeros((part,), F32), own_qv[1]])
@@ -265,7 +364,7 @@
     x_all = jnp.concatenate(x_blocks, axis=0)
     proj = (dot(x_all, qkv_local) + bias).astype(BF)
     scale = HD**-0.5
-    attended, kept = [], []
+    attended, lse = [], []
     for h in range(heads):
         q = proj[:, h * HD : (h + 1) * HD]
         k = proj[:, part + h * HD : part + (h + 1) * HD]
@@ -273,10 +372,9 @@
         scores = jnp.where(same, dot_t(q, k) * scale, jnp.float32(-1e30))
         peak = jnp.max(scores, axis=-1, keepdims=True)
         expo = jnp.exp(scores - peak)
-        probs = expo / jnp.sum(expo, axis=-1, keepdims=True)
-        low = probs.astype(BF)
-        attended.append(dot(low, v).astype(BF))
-        kept.append((q, k, v, probs, low))
+        total = jnp.sum(expo, axis=-1, keepdims=True)
+        attended.append(dot((expo / total).astype(BF), v).astype(BF))
+        lse.append((peak + jnp.log(total)).reshape(1, -1))
     attended = jnp.concatenate(attended, axis=1)
     branch, up_rows = lax.optimization_barrier((dot(attended, out_weight), up_rows))
     up_local = jnp.concatenate(xor_order(up_rows, place), axis=0)
@@ -284,7 +382,7 @@
     first = own_x.astype(F32) + branch + out_b
     hat1, scale1 = norm_parts(first)
     normed = hat1 * gain1 + shift1
-    normed_low = jnp.concatenate(gather_rows(normed.astype(BF)), axis=0)
+    normed_low = jnp.concatenate(gather_rows(after(normed.astype(BF), up_local)), axis=0)
     pre = dot(normed_low, up_local) + up_bias
     cdf = 0.5 * (1.0 + lax.erf(pre * (0.5**0.5)))
     act = (pre * cdf).astype(BF)
@@ -297,14 +395,14 @@
     up_stream = cotangent[0].astype(F32)
     d_sum = norm_back(up_stream, hat2, scale2, gain2)
     d_second = d_sum.astype(BF)
-    vec_gain2 = jnp.sum(up_stream * hat2, axis=0)
-    vec_shift2 = jnp.sum(up_stream, axis=0)
-    vec_down = jnp.sum(d_second.astype(F32), axis=0)
+    vec_gain2 = jnp.sum(up_stream * hat2, axis=0, keepdims=True)
+    vec_shift2 = jnp.sum(up_stream, axis=0, keepdims=True)
+    vec_down = jnp.sum(d_second.astype(F32), axis=0, keepdims=True)
     d_second_all = jnp.concatenate(gather_rows(d_second), axis=0)
     down = Scatter(t_dot(act, d_second_all).astype(BF)[None], first_y, me, replicas)
     down_got = down.swap(down.send())
     d_pre = (dot_t(d_second_all, down_weight) * slope).astype(BF)
-    vec_up = jnp.sum(d_pre.astype(F32), axis=0)
+    vec_up = jnp.sum(d_pre.astype(F32), axis=0, keepdims=True)
     d_normed = dot_t(d_pre, up_local)
     far = d_normed[2 * rows : 3 * rows] + gx(d_normed[3 * rows :].astype(BF), 1).astype(F32)
     far = far.astype(BF)
@@ -315,60 +413,71 @@
     d_normed = d_sum + d_normed[:rows] + near.astype(F32) + gx(far, 2).astype(F32)
 
     d_first = norm_back(d_normed, hat1, scale1, gain1)
-    vec_gain1 = jnp.sum(d_normed * hat1, axis=0)
-    vec_shift1 = jnp.sum(d_normed, axis=0)
+    vec_gain1 = jnp.sum(d_normed * hat1, axis=0, keepdims=True)
+    vec_shift1 = jnp.sum(d_normed, axis=0, keepdims=True)
     d_branch = d_first.astype(BF)
-    vec_out = jnp.sum(d_branch.astype(F32), axis=0)
+    vec_out = jnp.sum(d_branch.astype(F32), axis=0, keepdims=True)
     d_branch_blocks = gather_rows(d_branch)
     d_branch_all = jnp.concatenate(d_branch_blocks, axis=0)
     down_got = down.step(after(down_got, d_branch_blocks[2]))
     up_got = up.step(after(up_got, d_branch_blocks[2]))
-    grad_out = t_dot(attended, d_branch_all).astype(BF)
-    grad_out = grad_out.reshape(part, G, part).transpose(1, 0, 2)
-    d_att = dot_t(d_branch_all, out_weight).astype(BF)
-    d_q, d_k, d_v = [], [], []
-    for h in range(heads):
-        q, k, v, probs, low = kept[h]
-        d_o = d_att[:, h * HD : (h + 1) * HD]
-        d_v.append(t_dot(low, d_o).astype(BF))
-        d_probs = dot_t(d_o, v)
-        inner = jnp.sum(probs * d_probs, axis=-1, keepdims=True)
-        d_scores = (probs * (d_probs - inner)).astype(BF)
-        d_q.append((dot(d_scores, k) * scale).astype(BF))
-        d_k.append((t_dot(d_scores, q) * scale).astype(BF))
-    d_v = jnp.concatenate(d_v, axis=1)
-    d_qk = jnp.concatenate(d_q + d_k, axis=1)
-    grad_v = t_dot(x_all, d_v).astype(BF).reshape(G, part, part)
-    one = Scatter(jnp.concatenate([grad_out, grad_v], axis=2), first_z, me, replicas)
-    one_send = one.send()
-    grad_qk = t_dot(x_all, d_qk).astype(BF).reshape(G, part, 2 * part)
-    two = Scatter(grad_qk, first_y, me, replicas)
-    two_send = two.send()
+    half = jax.ShapeDtypeStruct((G, part // 2, 2 * part), BF)
+    d_qk, d_v, grad_one, grad_two, one_send, two_send = call(
+        attention_back_kernel,
+        [
+            jax.ShapeDtypeStruct((2 * part, G * rows), BF),
+            jax.ShapeDtypeStruct((part, G * rows), BF),
+            jax.ShapeDtypeStruct((G, part, 2 * part), BF),
+            jax.ShapeDtypeStruct((G, part, 2 * part), BF),
+            half,
+            half,
+        ],
+        [
+            index,
+            after(d_branch_all, down.sent, up.sent),
+            out_weight,
+            proj.T,
+            jnp.concatenate(lse),
+            segs.reshape(-1, 1),
+            segs.reshape(1, -1),
+            attended.T,
+            x_all.T,
+        ],
+    )
+    one = Scatter(grad_one, first_z, me, replicas)
+    two = Scatter(grad_two, first_y, me, replicas)
+    one.begin()
+    two.begin()
 
     one_got, two_got = one.swap(one_send), two.swap(two_send)
     down_got = down.step(after(down_got, two_send))
     up_got = up.step(after(up_got, two_send))
-    d_proj = jnp.concatenate([after(d_qk, two_send), d_v], axis=1)
-    sums = jnp.sum(d_proj.astype(F32), axis=0)
-    d_in = dot_t(d_proj, qkv_local)
-    far = d_in[2 * rows : 3 * rows] + gx(d_in[3 * rows :].astype(BF), 1).astype(F32)
-    near = gx(d_in[rows : 2 * rows].astype(BF), 1)
-    vecs = jnp.concatenate(
+    vectors = [vec_out, vec_gain1, vec_shift1, vec_down, vec_gain2, vec_shift2, vec_up]
+    near, far_send, own, far, vecs = call(
+        input_grad_kernel,
         [
-            jnp.stack([vec_out, vec_gain1, vec_shift1, vec_down, vec_gain2, vec_shift2]).reshape(-1),
-            lax.dynamic_update_slice_in_dim(jnp.zeros((G * hidden,), F32), vec_up, place * hidden, 0),
-            lax.dynamic_update_slice_in_dim(
-                jnp.zeros((3, width), F32), sums.reshape(3, part), place * part, 1
-            ).reshape(-1),
-        ]
-    ).reshape(-1, width)
-    vecs = vecs + gx(vecs, 1)
+            jax.ShapeDtypeStruct((rows, width), BF),
+            jax.ShapeDtypeStruct((rows + VECS, width), BF),
+            jax.ShapeDtypeStruct((rows, width), F32),
+            jax.ShapeDtypeStruct((rows, width), F32),
+            jax.ShapeDtypeStruct((VECS, width), F32),
+        ],
+        [index, d_qk, d_v, qkv_local]
+        + vectors,
+    )
+    near, far_got = gx(near, 1), gx(far_send, 1)
+    one_got, two_got = after((one_got, two_got), down.sent, up.sent)
 
     one_got, two_got = one.step(one_got), two.step(two_got)
-    far = gx(after(far.astype(BF), two_got), 2)
-    d_in = d_first + d_in[:rows] + near.astype(F32) + far.astype(F32)
-    grad_tokens = d_in.astype(BF)
-    vecs = vecs + gx(after(vecs, two_got), 2)
+    far, vecs = call(
+        add_two_kernel,
+        [
+            jax.ShapeDtypeStruct((rows + VECS, width), BF),
+            jax.ShapeDtypeStruct((VECS, width), F32),
+        ],
+        [index, far, vecs, after(far_got, two_got)],
+    )
+    far = gx(far, 2)
     down_piece = down.piece(after(down_got, one_got, two_got))
     up_piece = up.piece(after(up_got, one_got, two_got))
 
@@ -383,7 +492,7 @@
     down = Gather(after(down_piece, two_send), first_y, me, replicas)
     down_got = down.swap()
     up_piece = exchange(outgoing(up_piece))
-    vecs = vecs + rx(vecs, 1, replicas)
+    one_got, two_got = after((one_got, two_got), far)
 
     one_piece, two_piece = one.piece(one_got), two.piece(two_got)
     mine = jnp.concatenate([one_piece[:, :, part:], two_piece], axis=2)
@@ -392,7 +501,10 @@
     up = Gather(after(up_piece, mine), first_z, me, replicas)
     up_got = up.swap()
     down_got = down.step(after(down_got, mine))
-    vecs = vecs + rx(after(vecs, mine), 2, replicas)
+    vecs = vecs + far[rows:].astype(F32)
+    vecs = vecs.reshape(-1, 2 * part)
+    far = after(far, qkv_piece)
+    grad_tokens = (d_first + own + near.astype(F32) + far[:rows].astype(F32)).astype(BF)
 
     one = Gather(
         jnp.concatenate([one_piece[:, :, :part], qkv_piece[:, :, :part]], axis=2),
@@ -400,12 +512,10 @@
         me,
         replicas,
     )
-    two = Gather(qkv_piece[:, :, part:], first_y, me, replicas)
+    two = Gather(qkv_piece[:, :, part:], first_y, me, replicas, vecs)
     one_got, two_got = one.swap(), two.swap()
     up_got = up.step(after(up_got, one.value))
     down_got = down.step(after(down_got, one.value))
-    for bit in bits[2:]:
-        vecs = vecs + rx(after(vecs, one.value), 1 << bit, replicas)
 
     while len(one.left) > 1:
         one_got, two_got = one.step(one_got), two.step(two_got)
@@ -425,14 +535,17 @@
         jax.ShapeDtypeStruct((part, G * hidden), F32),
         [index, up.value, after(up_got, one.value)],
     )
-    grad_out, grad_qkv = call(
+    one_got, two_got = after((one_got, two_got), grad_down, grad_up, grad_tokens)
+    grad_out, grad_qkv, vecs = call(
         join_tail_kernel,
         [
             jax.ShapeDtypeStruct((part, width), F32),
             jax.ShapeDtypeStruct((part, 3 * width), F32),
+            jax.ShapeDtypeStruct((2 * VECS, 2 * part), F32),
         ],
-        [index, one.value, one_got, two.value, two_got],
-    )
+        [index, one.value, one_got, two.value, two_got, two.vecs],
+    )
+    vecs = vecs.reshape(VECS, width)
 
     six = lax.dynamic_slice_in_dim(vecs[:6], place * part, part, 1)
     vec_up = lax.dynamic_slice_in_dim(vecs[6 : 6 + G].reshape(-1), place * hidden, hidden, 0)

time: 231 us -> 213 us (0.922)
  starting transfers between devices: 60.7 us -> 47.2 us
  matrix products: 24.4 us -> 12.8 us
  Pallas kernels: 7.3 us -> 15.8 us
  local copies, waits for them, and re-layouts: 25 us -> 17.6 us
  waiting for transfers between devices: 80.8 us -> 84.9 us
    ppermute x41 -> x39, starting transfers between devices: 28 us -> 19.4 us  [gx(): return lax.ppermute(value, 'group', [(i, i ^ bits) for i in range(G)])]
    pallas_call x4 -> x7, Pallas kernels: 7.3 us -> 15.8 us  [call(): pl.pallas_call(kernel, out_shape=outs, in_specs=[index_spec()] + [whole_s...]
    dot_general x11 -> x2, matrix products: 8.06 us -> 1.62 us  [t_dot(): lax.dot_general(a, b, (((0,), (0,)), ((), ())), preferred_element_type=F32)]
    dot_general x10 -> x5, matrix products: 9.76 us -> 3.92 us  [dot_t(): lax.dot_general(a, b, (((1,), (1,)), ((), ())), preferred_element_type=F32)]
    unnamed x156 -> x115, local copies, waits for them, and re-layouts: 9.09 us -> 4.12 us
    ppermute x27 -> x24, starting transfers between devices: 32.7 us -> 27.8 us  [rx(): return lax.ppermute(value, 'replica', [(i, i ^ bits) for i in range(count)])]
    ppermute x41 -> x39, waiting for transfers between devices: 35.9 us -> 39.5 us  [gx(): return lax.ppermute(value, 'group', [(i, i ^ bits) for i in range(G)])]
    reduce_sum x9 -> x8, other arithmetic: 5.23 us -> 3.13 us  [the longest x1 1.12 us: on_device(): vec_gain1 = jnp.sum(d_normed * hat1, axis=0, keepdims=True)]
  transfers between devices with their start and end apart: 68 -> 63, of which waited for: 24 -> 28; matrix products, arithmetic and copies ran while one was open for 25% -> 21% of each run, Pallas kernels for 2% -> 6%
where the time goes in v3:
time: 213 us; the launch traced here: 212 us
  waiting for transfers between devices  84.9 us (40%)
  starting transfers between devices  47.2 us (22%)
  other arithmetic  31.9 us (15%)
  local copies, waits for them, and re-layouts  17.6 us (8%)
  Pallas kernels  15.8 us (7%)
  matrix products  12.8 us (6%)
    ppermute x24, waiting for transfers between devices, rx(): return lax.ppermute(value, 'replica', [(i, i ^ bits) for i in range(count)])  45.4 us
    ppermute x39, waiting for transfers between devices, gx(): return lax.ppermute(value, 'group', [(i, i ^ bits) for i in range(G)])  39.5 us
    ppermute x24, starting transfers between devices, rx(): return lax.ppermute(value, 'replica', [(i, i ^ bits) for i in range(count)])  27.8 us
    ppermute x39, starting transfers between devices, gx(): return lax.ppermute(value, 'group', [(i, i ^ bits) for i in range(G)])  19.4 us
    pallas_call x7, Pallas kernels, call(): pl.pallas_call(kernel, out_shape=outs, in_specs=[index_spec()] + [whole_s...  15.8 us
    convert_element_type x8, other arithmetic, send(): self.sent = self.total(1 - self.mine).astype(BF)  9.43 us
    dot_general x7, matrix products, dot(): return jnp.dot(a, b, preferred_element_type=F32)  7.22 us
    concatenate x1, local copies, waits for them, and re-layouts, on_device(): small = jnp.concatenate(smalls).reshape(1, -1)  4.82 us
  transfers between devices with their start and end apart: 63, of which 28 were waited for; matrix products, arithmetic and copies ran while one was open for 21% of the time, Pallas kernels for 6%

profile of v3, /device:TPU:0, one launch (start us, length us, event | category | flops | bytes accessed | tf_op | source)
XLA Modules:
  0.0 211.9 jit_solution(9620149461805389990)
XLA Ops:
  1.2 2.6 %collective-permute-start.1 = (bf16[128,768]{1,0:T(8,128)(2,1)}, bf16[128,768]{1,0:T(8,128)(2,1)}, u32[]{:S(2)}, u32[]{:S(2)}) collective-permute-start(bf16[128,768]{1,0:T(8,128)(2,1)} %bitcast.122), channel_id=1, source_target_pairs={{0,16},{8,24},{16,0},{24,8},{1,17},{9,25},{17,1},{25,9},{2,18},{10... | collective-permute-start | bytes 589832 | tf_op jit(solution)/shard_map/ppermute | solution.py:19
  6.1 1.9 collective-permute-start.4
  9.8 4.8 %concatenate.81 = bf16[1536]{0:T(1024)(128)(2,1)S(1)} concatenate(bf16[384]{0:T(512)(128)(2,1)} %param.19, bf16[192]{0:T(256)(128)(2,1)} %param.21, bf16[192]{0:T(256)(128)(2,1)} %param.22, bf16[192]{0:T(256)(128)(2,1)} %param.23, bf16[192]{0:T(256)(128)(2,1)} %param.27, bf16[192]{0:T(256)(128)(2,1)} %param.28, bf16[192]{0:T(256)(128)(2,1)} %param.29), dimensions={0} | concatenate | bytes 6144 | tf_op jit(solution)/shard_map/concatenate | solution.py:343
  14.7 2.0 collective-permute-start.6
  16.9 2.3 %constant_dynamic-slice_fusion.4 = (bf16[192,768]{1,0:T(8,128)(2,1)}, bf16[192,768]{1,0:T(8,128)(2,1)}, bf16[192,768]{1,0:T(8,128)(2,1)}, bf16[192,768]{1,0:T(8,128)(2,1)}) fusion(bf16[192,3072]{1,0:T(8,128)(2,1)} %param.24, s32[]{:T(128)S(6)} %select_n.356, s32[]{:T(128)S(6)} %select_n.355, s32[]{:T(128)S(6)} %select_n.354, s32[]{:T(128)S(6)} %select_n.353), kind=kLoop, calls=%fused_computation.181 | loop fusion | bytes 2359312 | tf_op jit(solution)/shard_map/dynamic_slice | solution.py:352
  24.5 1.8 fusion.6
  30.6 3.8 %collective-permute-done.11 = bf16[192,768]{1,0:T(8,128)(2,1)} collective-permute-done((bf16[192,768]{1,0:T(8,128)(2,1)}, bf16[192,768]{1,0:T(8,128)(2,1)}, u32[]{:S(2)}, u32[]{:S(2)}) %collective-permute-start.11) | collective-permute-done | bytes 294944 | tf_op jit(solution)/shard_map/ppermute | solution.py:19
  38.3 5.9 %collective-permute-done.14 = bf16[128,768]{1,0:T(8,128)(2,1)} collective-permute-done((bf16[128,768]{1,0:T(8,128)(2,1)S(1)}, bf16[128,768]{1,0:T(8,128)(2,1)}, u32[]{:S(2)}, u32[]{:S(2)}) %collective-permute-start.14) | collective-permute-done | bytes 196640 | tf_op jit(solution)/shard_map/ppermute | solution.py:19
  47.7 5.7 %collective-permute-done.16 = bf16[128,768]{1,0:T(8,128)(2,1)S(1)} collective-permute-done((bf16[128,768]{1,0:T(8,128)(2,1)S(1)}, bf16[128,768]{1,0:T(8,128)(2,1)S(1)}, u32[]{:S(2)}, u32[]{:S(2)}) %collective-permute-start.16) | collective-permute-done | bytes 196640 | tf_op jit(solution)/shard_map/ppermute | solution.py:19
  54.8 2.2 %multiply_convert_fusion = (bf16[512,768]{1,0:T(8,128)(2,1)S(1)}, f32[512,768]{1,0:T(8,128)}) fusion(f32[768]{0:T(1024)S(1)} %convert_element_type.313, bf16[512,768]{1,0:T(8,128)(2,1)S(1)} %constant_dynamic-update-slice_fusion, bf16[192,768]{1,0:T(8,128)(2,1)S(1)} %get-tuple-element.160, bf16[192,768]{1,0:T(8,128)(2,1)S(1)} %get-tuple-element.159, ...), kind=kOutput, calls=%fused_computation.11 | convolution fusion | flops 611057664 | bytes 4328448 | tf_op jit(solution)/shard_map/dot_general | solution.py:27
  57.0 1.9 fusion.82
  60.3 2.2 %fusion.34 = bf16[768,512]{0,1:T(8,128)(2,1)} fusion(bf16[128,768]{1,0:T(8,128)(2,1)} %collective-permute-done.2, bf16[128,768]{1,0:T(8,128)(2,1)} %collective-permute-done.1, bf16[128,768]{1,0:T(8,128)(2,1)} %copy-done.38, bf16[128,768]{1,0:T(8,128)(2,1)} %bitcast.123), kind=kLoop, calls=%fused_computation.144 | loop fusion | flops 3145728 | bytes 1572864 | tf_op jit(solution)/shard_map/transpose | solution.py:444
  62.4 1.4 copy.31.x
  65.8 6.6 %collective-permute-done.20 = bf16[128,768]{1,0:T(8,128)(2,1)S(1)} collective-permute-done((bf16[128,768]{1,0:T(8,128)(2,1)S(1)}, bf16[128,768]{1,0:T(8,128)(2,1)S(1)}, u32[]{:S(2)}, u32[]{:S(2)}) %collective-permute-start.20) | collective-permute-done | bytes 196640 | tf_op jit(solution)/shard_map/ppermute | solution.py:19
  74.9 5.7 %collective-permute-done.22 = bf16[128,768]{1,0:T(8,128)(2,1)S(1)} collective-permute-done((bf16[128,768]{1,0:T(8,128)(2,1)S(1)}, bf16[128,768]{1,0:T(8,128)(2,1)S(1)}, u32[]{:S(2)}, u32[]{:S(2)}) %collective-permute-start.22) | collective-permute-done | bytes 196640 | tf_op jit(solution)/shard_map/ppermute | solution.py:19
  80.7 1.4 collective-permute-done.23
  82.1 2.0 convert_reduce_fusion
  86.5 1.6 collective-permute-start.30
  89.6 1.6 collective-permute-start.31
  91.3 3.6 %collective-permute-done.26 = bf16[128,768]{1,0:T(8,128)(2,1)S(1)} collective-permute-done((bf16[128,768]{1,0:T(8,128)(2,1)S(1)}, bf16[128,768]{1,0:T(8,128)(2,1)S(1)}, u32[]{:S(2)}, u32[]{:S(2)}) %collective-permute-start.26) | collective-permute-done | bytes 196640 | tf_op jit(solution)/shard_map/ppermute | solution.py:19
  97.6 4.3 %collective-permute-done.30 = bf16[1,384,768]{2,1,0:T(8,128)(2,1)S(1)} collective-permute-done((bf16[1,384,768]{2,1,0:T(8,128)(2,1)S(1)}, bf16[1,384,768]{2,1,0:T(8,128)(2,1)S(1)}, u32[]{:S(2)}, u32[]{:S(2)}) %collective-permute-start.30) | collective-permute-done | bytes 589856 | tf_op jit(solution)/shard_map/ppermute | solution.py:23
  103.5 1.6 collective-permute-start.36
  107.0 5.0 %shard_map.255 = (bf16[384,512]{1,0:T(8,128)(2,1)S(1)}, bf16[192,512]{1,0:T(8,128)(2,1)S(1)}, bf16[4,192,384]{2,1,0:T(8,128)(2,1)S(1)}, bf16[4,192,384]{2,1,0:T(...) custom-call(s32[3]{0:T(128)S(1)} %pad_add_fusion.1.index, ...), custom_call_target="tpu_custom_call" | custom-call | tf_op jit(solution)/shard_map/pallas_call | solution.py:140
  112.7 1.4 collective-permute-start.34
  114.9 1.8 fusion.32
  116.7 1.8 add_convert_fusion.7
  118.4 2.6 %collective-permute-start.56 = (bf16[4,24,768]{2,1,0:T(8,128)(2,1)}, bf16[4,24,768]{2,1,0:T(8,128)(2,1)S(1)}, u32[]{:S(2)}, u32[]{:S(2)}) collective-permute-start(bf16[4,24,768]{2,1,0:T(8,128)(2,1)} %add_convert_fusion.7), channel_id=1, source_target_pairs={{0,4},{1,5},{2,6},{3,7},{4,0},{5,1},{6,2},{7,3},{8,12},{9,13},{10,... | collective-permute-start | bytes 442376 | tf_op jit(solution)/shard_map/ppermute | solution.py:23
  121.0 2.4 %collective-permute-done.34 = bf16[4,96,384]{2,1,0:T(8,128)(2,1)S(1)} collective-permute-done((bf16[4,96,384]{2,1,0:T(8,128)(2,1)}, bf16[4,96,384]{2,1,0:T(8,128)(2,1)S(1)}, u32[]{:S(2)}, u32[]{:S(2)}) %collective-permute-start.34) | collective-permute-done | bytes 294944 | tf_op jit(solution)/shard_map/ppermute | solution.py:23
  123.4 1.6 add_convert_fusion.5
  127.2 2.4 %shard_map.256 = (bf16[128,768]{1,0:T(8,128)(2,1)}, bf16[144,768]{1,0:T(8,128)(2,1)S(1)}, f32[128,768]{1,0:T(8,128)S(1)}, f32[128,768]{1,0:T(8,128)S(1)}, f32[16,768]{1,0:T(8,128)S(1)}) custom-call(s32[3]{0:T(128)S(1)} %pad_add_fusion.1.index, bf16[384,512]{1,0:T(8,128)(2,1)S(1)} %get-tuple-element.96.d_qk, bf16[192,512]{1,0:T(8,128)(2,1)S(1)} %get-tuple-element.97.d_v, ...), custom_call_target="tpu_custom_call" | custom-call | tf_op jit(solution)/shard_map/pallas_call | solution.py:140
  130.1 2.6 %collective-permute-start.52 = (bf16[1,96,768]{2,1,0:T(8,128)(2,1)S(1)}, bf16[1,96,768]{2,1,0:T(8,128)(2,1)S(1)}, u32[]{:S(2)}, u32[]{:S(2)}) collective-permute-start(bf16[1,96,768]{2,1,0:T(8,128)(2,1)S(1)} %copy-done.41), channel_id=1, source_target_pairs={{0,4},{1,5},{2,6},{3,7},{4,0},{5,1},{6,2},{7,3},{8,12},{9,13},{10,... | collective-permute-start | bytes 442376 | tf_op jit(solution)/shard_map/ppermute | solution.py:23
  136.5 3.5 %collective-permute-done.52 = bf16[1,96,768]{2,1,0:T(8,128)(2,1)S(1)} collective-permute-done((bf16[1,96,768]{2,1,0:T(8,128)(2,1)S(1)}, bf16[1,96,768]{2,1,0:T(8,128)(2,1)S(1)}, u32[]{:S(2)}, u32[]{:S(2)}) %collective-permute-start.52) | collective-permute-done | bytes 147488 | tf_op jit(solution)/shard_map/ppermute | solution.py:23
  143.7 2.9 %collective-permute-start.41 = (bf16[4,24,384]{2,1,0:T(8,128)(2,1)S(1)}, bf16[4,24,384]{2,1,0:T(8,128)(2,1)S(1)}, u32[]{:S(2)}, u32[]{:S(2)}) collective-permute-start(bf16[4,24,384]{2,1,0:T(8,128)(2,1)S(1)} %add_convert_fusion.11), channel_id=1, source_target_pairs={{0,4},{1,5},{2,6},{3,7},{4,0},{5,1},{6,2},{7,3},{8,12},{9,13},{10,... | collective-permute-start | bytes 221192 | tf_op jit(solution)/shard_map/ppermute | solution.py:23
  146.7 8.9 %collective-permute-done.42 = bf16[4,24,384]{2,1,0:T(8,128)(2,1)S(1)} collective-permute-done((bf16[4,24,384]{2,1,0:T(8,128)(2,1)S(1)}, bf16[4,24,384]{2,1,0:T(8,128)(2,1)S(1)}, u32[]{:S(2)}, u32[]{:S(2)}) %collective-permute-start.42) | collective-permute-done | bytes 73760 | tf_op jit(solution)/shard_map/ppermute | solution.py:23
  155.6 1.6 collective-permute-done.41
  159.5 1.4 collective-permute-start.44
  164.8 2.7 %collective-permute-start.49 = (bf16[128,384]{1,0:T(8,128)(2,1)S(1)}, bf16[128,384]{1,0:T(8,128)(2,1)S(1)}, u32[]{:S(2)}, u32[]{:S(2)}) collective-permute-start(bf16[128,384]{1,0:T(8,128)(2,1)S(1)} %pad_maximum_fusion.21), channel_id=1, source_target_pairs={{0,4},{1,5},{2,6},{3,7},{4,0},{5,1},{6,2},{7,3},{8,12},{9,13},{10,... | collective-permute-start | bytes 294920 | tf_op jit(solution)/shard_map/ppermute | solution.py:23
  167.5 6.0 %collective-permute-done.46 = bf16[4,24,384]{2,1,0:T(8,128)(2,1)S(1)} collective-permute-done((bf16[4,24,384]{2,1,0:T(8,128)(2,1)S(1)}, bf16[4,24,384]{2,1,0:T(8,128)(2,1)S(1)}, u32[]{:S(2)}, u32[]{:S(2)}) %collective-permute-start.46) | collective-permute-done | bytes 73760 | tf_op jit(solution)/shard_map/ppermute | solution.py:23
  174.5 2.5 %collective-permute-done.49 = bf16[128,384]{1,0:T(8,128)(2,1)S(1)} collective-permute-done((bf16[128,384]{1,0:T(8,128)(2,1)S(1)}, bf16[128,384]{1,0:T(8,128)(2,1)S(1)}, u32[]{:S(2)}, u32[]{:S(2)}) %collective-permute-start.49) | collective-permute-done | bytes 98336 | tf_op jit(solution)/shard_map/ppermute | solution.py:23
  180.7 2.7 %collective-permute-done.50 = bf16[224,384]{1,0:T(8,128)(2,1)S(1)} collective-permute-done((bf16[224,384]{1,0:T(8,128)(2,1)S(1)}, bf16[224,384]{1,0:T(8,128)(2,1)S(1)}, u32[]{:S(2)}, u32[]{:S(2)}) %collective-permute-start.50) | collective-permute-done | bytes 172064 | tf_op jit(solution)/shard_map/ppermute | solution.py:23
  183.6 3.9 %collective-permute-done.61 = bf16[4,48,768]{2,1,0:T(8,128)(2,1)S(1)} collective-permute-done((bf16[4,48,768]{2,1,0:T(8,128)(2,1)S(1)}, bf16[4,48,768]{2,1,0:T(8,128)(2,1)S(1)}, u32[]{:S(2)}, u32[]{:S(2)}) %collective-permute-start.61) | collective-permute-done | bytes 294944 | tf_op jit(solution)/shard_map/ppermute | solution.py:23
  187.6 1.9 collective-permute-start.62
  191.7 1.9 add_convert_fusion.1
  193.6 6.6 %collective-permute-done.55 = bf16[1,384,768]{2,1,0:T(8,128)(2,1)S(1)} collective-permute-done((bf16[1,384,768]{2,1,0:T(8,128)(2,1)}, bf16[1,384,768]{2,1,0:T(8,128)(2,1)S(1)}, u32[]{:S(2)}, u32[]{:S(2)}) %collective-permute-start.55) | collective-permute-done | bytes 589856 | tf_op jit(solution)/shard_map/ppermute | solution.py:23
  200.1 2.1 shard_map.258
  202.2 1.5 collective-permute-done.62.got
  203.7 2.1 shard_map.259
  207.0 2.8 %shard_map.260 = (f32[192,768]{1,0:T(8,128)}, f32[192,2304]{1,0:T(8,128)}, f32[32,384]{1,0:T(8,128)S(1)}) custom-call(s32[3]{0:T(128)S(1)} %pad_add_fusion.1.index, bf16[4,96,384]{2,1,0:T(8,128)(2,1)S(1)} %pad_maximum_fusion.8.held_one, bf16[4,96,384]{2,1,0:T(8,128)(2,1)} %collective-permute-done.48.got_one, ...), custom_call_target="tpu_custom_call" | custom-call | tf_op jit(solution)/shard_map/pallas_call | solution.py:140
  (342 shorter events, 66.6 us)
Async XLA Ops:
  0.7 9.2 %collective-permute-start = (bf16[128,768]{1,0:T(8,128)(2,1)}, bf16[128,768]{1,0:T(8,128)(2,1)S(1)}, u32[]{:S(2)}, u32[]{:S(2)}) collective-permute-start(bf16[128,768]{1,0:T(8,128)(2,1)} %bitcast.121), channel_id=1, source_target_pairs={{0,8},{8,0},{16,24},{24,16},{1,9},{9,1},{17,25},{25,17},{2,10},{10... | collective-permute-start | bytes 589832 | tf_op jit(solution)/shard_map/ppermute | solution.py:19
  1.2 8.6 %collective-permute-start.1 = (bf16[128,768]{1,0:T(8,128)(2,1)}, bf16[128,768]{1,0:T(8,128)(2,1)}, u32[]{:S(2)}, u32[]{:S(2)}) collective-permute-start(bf16[128,768]{1,0:T(8,128)(2,1)} %bitcast.122), channel_id=1, source_target_pairs={{0,16},{8,24},{16,0},{24,8},{1,17},{9,25},{17,1},{25,9},{2,18},{10... | collective-permute-start | bytes 589832 | tf_op jit(solution)/shard_map/ppermute | solution.py:19
  6.0 13.2 %collective-permute-start.3 = (bf16[192,576]{1,0:T(8,128)(2,1)S(1)}, bf16[192,576]{1,0:T(8,128)(2,1)S(1)}, u32[]{:S(2)}, u32[]{:S(2)}) collective-permute-start(bf16[192,576]{1,0:T(8,128)(2,1)S(1)} %get-tuple-element.73), channel_id=1, source_target_pairs={{0,24},{8,16},{16,8},{24,0},{1,25},{9,17},{17,9},{25,1},{2,26},{10... | collective-permute-start | bytes 663560 | tf_op jit(solution)/shard_map/ppermute | solution.py:19
  6.1 14.0 %collective-permute-start.4 = (bf16[192,576]{1,0:T(8,128)(2,1)S(1)}, bf16[192,576]{1,0:T(8,128)(2,1)S(1)}, u32[]{:S(2)}, u32[]{:S(2)}) collective-permute-start(bf16[192,576]{1,0:T(8,128)(2,1)S(1)} %get-tuple-element.74), channel_id=1, source_target_pairs={{0,16},{8,24},{16,0},{24,8},{1,17},{9,25},{17,1},{25,9},{2,18},{10... | collective-permute-start | bytes 663560 | tf_op jit(solution)/shard_map/ppermute | solution.py:19
  9.8 14.6 %collective-permute-start.2 = (bf16[128,768]{1,0:T(8,128)(2,1)}, bf16[128,768]{1,0:T(8,128)(2,1)}, u32[]{:S(2)}, u32[]{:S(2)}) collective-permute-start(bf16[128,768]{1,0:T(8,128)(2,1)} %collective-permute-done.1), channel_id=1, source_target_pairs={{0,8},{8,0},{16,24},{24,16},{1,9},{9,1},{17,25},{25,17},{2,10},{10... | collective-permute-start | bytes 589832 | tf_op jit(solution)/shard_map/ppermute | solution.py:19
  14.7 7.7 %collective-permute-start.6 = (bf16[1,1536]{1,0:T(2,128)(2,1)S(1)}, bf16[1,1536]{1,0:T(2,128)(2,1)S(1)}, u32[]{:S(2)}, u32[]{:S(2)}) collective-permute-start(bf16[1,1536]{1,0:T(2,128)(2,1)S(1)} %reshape.212), channel_id=1, source_target_pairs={{0,16},{8,24},{16,0},{24,8},{1,17},{9,25},{17,1},{25,9},{2,18},{10... | collective-permute-start | bytes 9224 | tf_op jit(solution)/shard_map/ppermute | solution.py:19
  16.7 6.8 %collective-permute-start.8 = (bf16[1,1536]{1,0:T(2,128)(2,1)S(1)}, bf16[1,1536]{1,0:T(2,128)(2,1)S(1)}, u32[]{:S(2)}, u32[]{:S(2)}) collective-permute-start(bf16[1,1536]{1,0:T(2,128)(2,1)S(1)} %reshape.212), channel_id=1, source_target_pairs={{0,8},{8,0},{16,24},{24,16},{1,9},{9,1},{17,25},{25,17},{2,10},{10... | collective-permute-start | bytes 9224 | tf_op jit(solution)/shard_map/ppermute | solution.py:19
  19.2 11.4 %collective-permute-start.10 = (bf16[192,768]{1,0:T(8,128)(2,1)}, bf16[192,768]{1,0:T(8,128)(2,1)}, u32[]{:S(2)}, u32[]{:S(2)}) collective-permute-start(bf16[192,768]{1,0:T(8,128)(2,1)} %get-tuple-element.162), channel_id=1, source_target_pairs={{0,16},{8,24},{16,0},{24,8},{1,17},{9,25},{17,1},{25,9},{2,18},{10... | collective-permute-start | bytes 884744 | tf_op jit(solution)/shard_map/ppermute | solution.py:19
  20.1 14.4 %collective-permute-start.11 = (bf16[192,768]{1,0:T(8,128)(2,1)}, bf16[192,768]{1,0:T(8,128)(2,1)}, u32[]{:S(2)}, u32[]{:S(2)}) collective-permute-start(bf16[192,768]{1,0:T(8,128)(2,1)} %get-tuple-element.161), channel_id=1, source_target_pairs={{0,24},{8,16},{16,8},{24,0},{1,25},{9,17},{17,9},{25,1},{2,26},{10... | collective-permute-start | bytes 884744 | tf_op jit(solution)/shard_map/ppermute | solution.py:19
  23.5 11.0 %collective-permute-start.9 = (bf16[192,768]{1,0:T(8,128)(2,1)}, bf16[192,768]{1,0:T(8,128)(2,1)}, u32[]{:S(2)}, u32[]{:S(2)}) collective-permute-start(bf16[192,768]{1,0:T(8,128)(2,1)} %get-tuple-element.163), channel_id=1, source_target_pairs={{0,8},{8,0},{16,24},{24,16},{1,9},{9,1},{17,25},{25,17},{2,10},{10... | collective-permute-start | bytes 884744 | tf_op jit(solution)/shard_map/ppermute | solution.py:19
  36.8 7.3 %collective-permute-start.14 = (bf16[128,768]{1,0:T(8,128)(2,1)S(1)}, bf16[128,768]{1,0:T(8,128)(2,1)}, u32[]{:S(2)}, u32[]{:S(2)}) collective-permute-start(bf16[128,768]{1,0:T(8,128)(2,1)S(1)} %add_convert_fusion.3), channel_id=1, source_target_pairs={{0,16},{8,24},{16,0},{24,8},{1,17},{9,25},{17,1},{25,9},{2,18},{10... | collective-permute-start | bytes 589832 | tf_op jit(solution)/shard_map/ppermute | solution.py:19
  45.9 7.4 %collective-permute-start.15 = (bf16[128,768]{1,0:T(8,128)(2,1)S(1)}, bf16[128,768]{1,0:T(8,128)(2,1)S(1)}, u32[]{:S(2)}, u32[]{:S(2)}) collective-permute-start(bf16[128,768]{1,0:T(8,128)(2,1)S(1)} %fusion.27), channel_id=1, source_target_pairs={{0,8},{8,0},{16,24},{24,16},{1,9},{9,1},{17,25},{25,17},{2,10},{10... | collective-permute-start | bytes 589832 | tf_op jit(solution)/shard_map/ppermute | solution.py:19
  46.0 7.3 %collective-permute-start.16 = (bf16[128,768]{1,0:T(8,128)(2,1)S(1)}, bf16[128,768]{1,0:T(8,128)(2,1)S(1)}, u32[]{:S(2)}, u32[]{:S(2)}) collective-permute-start(bf16[128,768]{1,0:T(8,128)(2,1)S(1)} %fusion.27), channel_id=1, source_target_pairs={{0,16},{8,24},{16,0},{24,8},{1,17},{9,25},{17,1},{25,9},{2,18},{10... | collective-permute-start | bytes 589832 | tf_op jit(solution)/shard_map/ppermute | solution.py:19
  65.4 7.0 %collective-permute-start.20 = (bf16[128,768]{1,0:T(8,128)(2,1)S(1)}, bf16[128,768]{1,0:T(8,128)(2,1)S(1)}, u32[]{:S(2)}, u32[]{:S(2)}) collective-permute-start(bf16[128,768]{1,0:T(8,128)(2,1)S(1)} %fusion.23), channel_id=1, source_target_pairs={{0,16},{8,24},{16,0},{24,8},{1,17},{9,25},{17,1},{25,9},{2,18},{10... | collective-permute-start | bytes 589832 | tf_op jit(solution)/shard_map/ppermute | solution.py:19
  74.4 6.2 %collective-permute-start.22 = (bf16[128,768]{1,0:T(8,128)(2,1)S(1)}, bf16[128,768]{1,0:T(8,128)(2,1)S(1)}, u32[]{:S(2)}, u32[]{:S(2)}) collective-permute-start(bf16[128,768]{1,0:T(8,128)(2,1)S(1)} %get-tuple-element.148), channel_id=1, source_target_pairs={{0,16},{8,24},{16,0},{24,8},{1,17},{9,25},{17,1},{25,9},{2,18},{10... | collective-permute-start | bytes 589832 | tf_op jit(solution)/shard_map/ppermute | solution.py:19
  74.8 5.8 %collective-permute-start.21 = (bf16[128,768]{1,0:T(8,128)(2,1)S(1)}, bf16[128,768]{1,0:T(8,128)(2,1)S(1)}, u32[]{:S(2)}, u32[]{:S(2)}) collective-permute-start(bf16[128,768]{1,0:T(8,128)(2,1)S(1)} %get-tuple-element.148), channel_id=1, source_target_pairs={{0,8},{8,0},{16,24},{24,16},{1,9},{9,1},{17,25},{25,17},{2,10},{10... | collective-permute-start | bytes 589832 | tf_op jit(solution)/shard_map/ppermute | solution.py:19
  85.2 6.1 %collective-permute-start.24 = (bf16[128,768]{1,0:T(8,128)(2,1)S(1)}, bf16[128,768]{1,0:T(8,128)(2,1)S(1)}, u32[]{:S(2)}, u32[]{:S(2)}) collective-permute-start(bf16[128,768]{1,0:T(8,128)(2,1)S(1)} %get-tuple-element.169), channel_id=1, source_target_pairs={{0,8},{8,0},{16,24},{24,16},{1,9},{9,1},{17,25},{25,17},{2,10},{10... | collective-permute-start | bytes 589832 | tf_op jit(solution)/shard_map/ppermute | solution.py:19
  86.5 15.4 %collective-permute-start.30 = (bf16[1,384,768]{2,1,0:T(8,128)(2,1)S(1)}, bf16[1,384,768]{2,1,0:T(8,128)(2,1)S(1)}, u32[]{:S(2)}, u32[]{:S(2)}) collective-permute-start(bf16[1,384,768]{2,1,0:T(8,128)(2,1)S(1)} %dynamic-slice_bitcast_fusion), channel_id=1, source_target_pairs={{0,1},{1,0},{2,3},{3,2},{4,5},{5,4},{6,7},{7,6},{8,9},{9,8},{10,11... | collective-permute-start | bytes 1769480 | tf_op jit(solution)/shard_map/ppermute | solution.py:23
  88.1 6.7 %collective-permute-start.26 = (bf16[128,768]{1,0:T(8,128)(2,1)S(1)}, bf16[128,768]{1,0:T(8,128)(2,1)S(1)}, u32[]{:S(2)}, u32[]{:S(2)}) collective-permute-start(bf16[128,768]{1,0:T(8,128)(2,1)S(1)} %fusion.20), channel_id=1, source_target_pairs={{0,16},{8,24},{16,0},{24,8},{1,17},{9,25},{17,1},{25,9},{2,18},{10... | collective-permute-start | bytes 589832 | tf_op jit(solution)/shard_map/ppermute | solution.py:19
  89.6 15.5 %collective-permute-start.31 = (bf16[4,96,768]{2,1,0:T(8,128)(2,1)S(1)}, bf16[4,96,768]{2,1,0:T(8,128)(2,1)S(1)}, u32[]{:S(2)}, u32[]{:S(2)}) collective-permute-start(bf16[4,96,768]{2,1,0:T(8,128)(2,1)S(1)} %constant_dynamic-slice_fusion.3), channel_id=1, source_target_pairs={{0,2},{1,3},{2,0},{3,1},{4,6},{5,7},{6,4},{7,5},{8,10},{9,11},{10,... | collective-permute-start | bytes 1769480 | tf_op jit(solution)/shard_map/ppermute | solution.py:23
  96.9 5.8 %collective-permute-start.28 = (bf16[128,768]{1,0:T(8,128)(2,1)S(1)}, bf16[128,768]{1,0:T(8,128)(2,1)S(1)}, u32[]{:S(2)}, u32[]{:S(2)}) collective-permute-start(bf16[128,768]{1,0:T(8,128)(2,1)S(1)} %get-tuple-element.150), channel_id=1, source_target_pairs={{0,16},{8,24},{16,0},{24,8},{1,17},{9,25},{17,1},{25,9},{2,18},{10... | collective-permute-start | bytes 589832 | tf_op jit(solution)/shard_map/ppermute | solution.py:19
  97.5 9.3 %collective-permute-start.27 = (bf16[128,768]{1,0:T(8,128)(2,1)S(1)}, bf16[128,768]{1,0:T(8,128)(2,1)S(1)}, u32[]{:S(2)}, u32[]{:S(2)}) collective-permute-start(bf16[128,768]{1,0:T(8,128)(2,1)S(1)} %get-tuple-element.150), channel_id=1, source_target_pairs={{0,8},{8,0},{16,24},{24,16},{1,9},{9,1},{17,25},{25,17},{2,10},{10... | collective-permute-start | bytes 589832 | tf_op jit(solution)/shard_map/ppermute | solution.py:19
  103.5 11.3 %collective-permute-start.36 = (bf16[1,192,768]{2,1,0:T(8,128)(2,1)}, bf16[1,192,768]{2,1,0:T(8,128)(2,1)}, u32[]{:S(2)}, u32[]{:S(2)}) collective-permute-start(bf16[1,192,768]{2,1,0:T(8,128)(2,1)} %fusion.10), channel_id=1, source_target_pairs={{0,2},{1,3},{2,0},{3,1},{4,6},{5,7},{6,4},{7,5},{8,10},{9,11},{10,... | collective-permute-start | bytes 884744 | tf_op jit(solution)/shard_map/ppermute | solution.py:23
  106.0 10.6 %collective-permute-start.37 = (bf16[4,48,768]{2,1,0:T(8,128)(2,1)}, bf16[4,48,768]{2,1,0:T(8,128)(2,1)}, u32[]{:S(2)}, u32[]{:S(2)}) collective-permute-start(bf16[4,48,768]{2,1,0:T(8,128)(2,1)} %add_convert_fusion), channel_id=1, source_target_pairs={{0,1},{1,0},{2,3},{3,2},{4,5},{5,4},{6,7},{7,6},{8,9},{9,8},{10,11... | collective-permute-start | bytes 884744 | tf_op jit(solution)/shard_map/ppermute | solution.py:23
  112.7 10.7 %collective-permute-start.34 = (bf16[4,96,384]{2,1,0:T(8,128)(2,1)}, bf16[4,96,384]{2,1,0:T(8,128)(2,1)S(1)}, u32[]{:S(2)}, u32[]{:S(2)}) collective-permute-start(bf16[4,96,384]{2,1,0:T(8,128)(2,1)} %get-tuple-element.104), channel_id=1, source_target_pairs={{0,2},{1,3},{2,0},{3,1},{4,6},{5,7},{6,4},{7,5},{8,10},{9,11},{10,... | collective-permute-start | bytes 884744 | tf_op jit(solution)/shard_map/ppermute | solution.py:23
  114.2 9.2 %collective-permute-start.35 = (bf16[4,96,384]{2,1,0:T(8,128)(2,1)}, bf16[4,96,384]{2,1,0:T(8,128)(2,1)S(1)}, u32[]{:S(2)}, u32[]{:S(2)}) collective-permute-start(bf16[4,96,384]{2,1,0:T(8,128)(2,1)} %get-tuple-element.105), channel_id=1, source_target_pairs={{0,1},{1,0},{2,3},{3,2},{4,5},{5,4},{6,7},{7,6},{8,9},{9,8},{10,11... | collective-permute-start | bytes 884744 | tf_op jit(solution)/shard_map/ppermute | solution.py:23
  118.4 11.7 %collective-permute-start.56 = (bf16[4,24,768]{2,1,0:T(8,128)(2,1)}, bf16[4,24,768]{2,1,0:T(8,128)(2,1)S(1)}, u32[]{:S(2)}, u32[]{:S(2)}) collective-permute-start(bf16[4,24,768]{2,1,0:T(8,128)(2,1)} %add_convert_fusion.7), channel_id=1, source_target_pairs={{0,4},{1,5},{2,6},{3,7},{4,0},{5,1},{6,2},{7,3},{8,12},{9,13},{10,... | collective-permute-start | bytes 442376 | tf_op jit(solution)/shard_map/ppermute | solution.py:23
  125.0 7.7 %collective-permute-start.40 = (bf16[4,48,384]{2,1,0:T(8,128)(2,1)}, bf16[4,48,384]{2,1,0:T(8,128)(2,1)}, u32[]{:S(2)}, u32[]{:S(2)}) collective-permute-start(bf16[4,48,384]{2,1,0:T(8,128)(2,1)} %add_convert_fusion.5), channel_id=1, source_target_pairs={{0,1},{1,0},{2,3},{3,2},{4,5},{5,4},{6,7},{7,6},{8,9},{9,8},{10,11... | collective-permute-start | bytes 442376 | tf_op jit(solution)/shard_map/ppermute | solution.py:23
  127.0 5.7 %collective-permute-start.38 = (bf16[4,48,384]{2,1,0:T(8,128)(2,1)}, bf16[4,48,384]{2,1,0:T(8,128)(2,1)}, u32[]{:S(2)}, u32[]{:S(2)}) collective-permute-start(bf16[4,48,384]{2,1,0:T(8,128)(2,1)} %add_convert_fusion.6), channel_id=1, source_target_pairs={{0,2},{1,3},{2,0},{3,1},{4,6},{5,7},{6,4},{7,5},{8,10},{9,11},{10,... | collective-permute-start | bytes 442376 | tf_op jit(solution)/shard_map/ppermute | solution.py:23
  129.6 62.1 %collective-permute-start.32 = (bf16[128,768]{1,0:T(8,128)(2,1)}, bf16[128,768]{1,0:T(8,128)(2,1)}, u32[]{:S(2)}, u32[]{:S(2)}) collective-permute-start(bf16[128,768]{1,0:T(8,128)(2,1)} %get-tuple-element.99), channel_id=1, source_target_pairs={{0,8},{8,0},{16,24},{24,16},{1,9},{9,1},{17,25},{25,17},{2,10},{10... | collective-permute-start | bytes 589832 | tf_op jit(solution)/shard_map/ppermute | solution.py:19
  130.1 9.9 %collective-permute-start.52 = (bf16[1,96,768]{2,1,0:T(8,128)(2,1)S(1)}, bf16[1,96,768]{2,1,0:T(8,128)(2,1)S(1)}, u32[]{:S(2)}, u32[]{:S(2)}) collective-permute-start(bf16[1,96,768]{2,1,0:T(8,128)(2,1)S(1)} %copy-done.41), channel_id=1, source_target_pairs={{0,4},{1,5},{2,6},{3,7},{4,0},{5,1},{6,2},{7,3},{8,12},{9,13},{10,... | collective-permute-start | bytes 442376 | tf_op jit(solution)/shard_map/ppermute | solution.py:23
  134.0 9.6 %collective-permute-start.57 = (bf16[24,768]{1,0:T(8,128)(2,1)S(1)}, bf16[24,768]{1,0:T(8,128)(2,1)S(1)}, u32[]{:S(2)}, u32[]{:S(2)}) collective-permute-start(bf16[24,768]{1,0:T(8,128)(2,1)S(1)} %get-tuple-element.195), channel_id=1, source_target_pairs={{0,8},{8,0},{16,24},{24,16},{1,9},{9,1},{17,25},{25,17},{2,10},{10... | collective-permute-start | bytes 110600 | tf_op jit(solution)/shard_map/ppermute | solution.py:19
  134.1 9.6 %collective-permute-start.58 = (bf16[24,768]{1,0:T(8,128)(2,1)S(1)}, bf16[24,768]{1,0:T(8,128)(2,1)S(1)}, u32[]{:S(2)}, u32[]{:S(2)}) collective-permute-start(bf16[24,768]{1,0:T(8,128)(2,1)S(1)} %get-tuple-element.194), channel_id=1, source_target_pairs={{0,16},{8,24},{16,0},{24,8},{1,17},{9,25},{17,1},{25,9},{2,18},{10... | collective-permute-start | bytes 110600 | tf_op jit(solution)/shard_map/ppermute | solution.py:19
  134.7 11.9 %collective-permute-start.59 = (bf16[24,768]{1,0:T(8,128)(2,1)S(1)}, bf16[24,768]{1,0:T(8,128)(2,1)S(1)}, u32[]{:S(2)}, u32[]{:S(2)}) collective-permute-start(bf16[24,768]{1,0:T(8,128)(2,1)S(1)} %get-tuple-element.193), channel_id=1, source_target_pairs={{0,24},{8,16},{16,8},{24,0},{1,25},{9,17},{17,9},{25,1},{2,26},{10... | collective-permute-start | bytes 110600 | tf_op jit(solution)/shard_map/ppermute | solution.py:19
  140.0 17.2 %collective-permute-start.39 = (bf16[144,768]{1,0:T(8,128)(2,1)S(1)}, bf16[144,768]{1,0:T(8,128)(2,1)S(1)}, u32[]{:S(2)}, u32[]{:S(2)}) collective-permute-start(bf16[144,768]{1,0:T(8,128)(2,1)S(1)} %get-tuple-element.110), channel_id=1, source_target_pairs={{0,16},{8,24},{16,0},{24,8},{1,17},{9,25},{17,1},{25,9},{2,18},{10... | collective-permute-start | bytes 663560 | tf_op jit(solution)/shard_map/ppermute | solution.py:19
  143.6 12.0 %collective-permute-start.42 = (bf16[4,24,384]{2,1,0:T(8,128)(2,1)S(1)}, bf16[4,24,384]{2,1,0:T(8,128)(2,1)S(1)}, u32[]{:S(2)}, u32[]{:S(2)}) collective-permute-start(bf16[4,24,384]{2,1,0:T(8,128)(2,1)S(1)} %add_convert_fusion.10), channel_id=1, source_target_pairs={{0,4},{1,5},{2,6},{3,7},{4,0},{5,1},{6,2},{7,3},{8,12},{9,13},{10,... | collective-permute-start | bytes 221192 | tf_op jit(solution)/shard_map/ppermute | solution.py:23
  143.7 13.5 %collective-permute-start.41 = (bf16[4,24,384]{2,1,0:T(8,128)(2,1)S(1)}, bf16[4,24,384]{2,1,0:T(8,128)(2,1)S(1)}, u32[]{:S(2)}, u32[]{:S(2)}) collective-permute-start(bf16[4,24,384]{2,1,0:T(8,128)(2,1)S(1)} %add_convert_fusion.11), channel_id=1, source_target_pairs={{0,4},{1,5},{2,6},{3,7},{4,0},{5,1},{6,2},{7,3},{8,12},{9,13},{10,... | collective-permute-start | bytes 221192 | tf_op jit(solution)/shard_map/ppermute | solution.py:23
  146.6 14.8 %collective-permute-start.53 = (bf16[1,96,768]{2,1,0:T(8,128)(2,1)S(1)}, bf16[1,96,768]{2,1,0:T(8,128)(2,1)S(1)}, u32[]{:S(2)}, u32[]{:S(2)}) collective-permute-start(bf16[1,96,768]{2,1,0:T(8,128)(2,1)S(1)} %fusion.30), channel_id=1, source_target_pairs={{0,4},{1,5},{2,6},{3,7},{4,0},{5,1},{6,2},{7,3},{8,12},{9,13},{10,... | collective-permute-start | bytes 442376 | tf_op jit(solution)/shard_map/ppermute | solution.py:23
  161.3 16.1 %collective-permute-start.60 = (bf16[4,24,768]{2,1,0:T(8,128)(2,1)S(1)}, bf16[4,24,768]{2,1,0:T(8,128)(2,1)S(1)}, u32[]{:S(2)}, u32[]{:S(2)}) collective-permute-start(bf16[4,24,768]{2,1,0:T(8,128)(2,1)S(1)} %pad_maximum_fusion.16), channel_id=1, source_target_pairs={{0,4},{1,5},{2,6},{3,7},{4,0},{5,1},{6,2},{7,3},{8,12},{9,13},{10,... | collective-permute-start | bytes 442376 | tf_op jit(solution)/shard_map/ppermute | solution.py:23
  161.5 17.5 %collective-permute-start.54 = (bf16[1,192,768]{2,1,0:T(8,128)(2,1)S(1)}, bf16[1,192,768]{2,1,0:T(8,128)(2,1)S(1)}, u32[]{:S(2)}, u32[]{:S(2)}) collective-permute-start(bf16[1,192,768]{2,1,0:T(8,128)(2,1)S(1)} %pad_maximum_fusion.10), channel_id=1, source_target_pairs={{0,2},{1,3},{2,0},{3,1},{4,6},{5,7},{6,4},{7,5},{8,10},{9,11},{10,... | collective-permute-start | bytes 884744 | tf_op jit(solution)/shard_map/ppermute | solution.py:23
  164.4 9.1 %collective-permute-start.46 = (bf16[4,24,384]{2,1,0:T(8,128)(2,1)S(1)}, bf16[4,24,384]{2,1,0:T(8,128)(2,1)S(1)}, u32[]{:S(2)}, u32[]{:S(2)}) collective-permute-start(bf16[4,24,384]{2,1,0:T(8,128)(2,1)S(1)} %pad_maximum_fusion.23), channel_id=1, source_target_pairs={{0,4},{1,5},{2,6},{3,7},{4,0},{5,1},{6,2},{7,3},{8,12},{9,13},{10,... | collective-permute-start | bytes 221192 | tf_op jit(solution)/shard_map/ppermute | solution.py:23
  164.8 12.2 %collective-permute-start.49 = (bf16[128,384]{1,0:T(8,128)(2,1)S(1)}, bf16[128,384]{1,0:T(8,128)(2,1)S(1)}, u32[]{:S(2)}, u32[]{:S(2)}) collective-permute-start(bf16[128,384]{1,0:T(8,128)(2,1)S(1)} %pad_maximum_fusion.21), channel_id=1, source_target_pairs={{0,4},{1,5},{2,6},{3,7},{4,0},{5,1},{6,2},{7,3},{8,12},{9,13},{10,... | collective-permute-start | bytes 294920 | tf_op jit(solution)/shard_map/ppermute | solution.py:23
  177.2 6.3 %collective-permute-start.50 = (bf16[224,384]{1,0:T(8,128)(2,1)S(1)}, bf16[224,384]{1,0:T(8,128)(2,1)S(1)}, u32[]{:S(2)}, u32[]{:S(2)}) collective-permute-start(bf16[224,384]{1,0:T(8,128)(2,1)S(1)} %pad_maximum_fusion.13), channel_id=1, source_target_pairs={{0,2},{1,3},{2,0},{3,1},{4,6},{5,7},{6,4},{7,5},{8,10},{9,11},{10,... | collective-permute-start | bytes 516104 | tf_op jit(solution)/shard_map/ppermute | solution.py:23
  177.5 10.0 %collective-permute-start.61 = (bf16[4,48,768]{2,1,0:T(8,128)(2,1)S(1)}, bf16[4,48,768]{2,1,0:T(8,128)(2,1)S(1)}, u32[]{:S(2)}, u32[]{:S(2)}) collective-permute-start(bf16[4,48,768]{2,1,0:T(8,128)(2,1)S(1)} %pad_maximum_fusion.11), channel_id=1, source_target_pairs={{0,1},{1,0},{2,3},{3,2},{4,5},{5,4},{6,7},{7,6},{8,9},{9,8},{10,11... | collective-permute-start | bytes 884744 | tf_op jit(solution)/shard_map/ppermute | solution.py:23
  180.0 20.2 %collective-permute-start.55 = (bf16[1,384,768]{2,1,0:T(8,128)(2,1)}, bf16[1,384,768]{2,1,0:T(8,128)(2,1)S(1)}, u32[]{:S(2)}, u32[]{:S(2)}) collective-permute-start(bf16[1,384,768]{2,1,0:T(8,128)(2,1)} %get-tuple-element.177), channel_id=1, source_target_pairs={{0,1},{1,0},{2,3},{3,2},{4,5},{5,4},{6,7},{7,6},{8,9},{9,8},{10,11... | collective-permute-start | bytes 1769480 | tf_op jit(solution)/shard_map/ppermute | solution.py:23
  187.6 16.1 %collective-permute-start.62 = (bf16[4,96,768]{2,1,0:T(8,128)(2,1)S(1)}, bf16[4,96,768]{2,1,0:T(8,128)(2,1)S(1)}, u32[]{:S(2)}, u32[]{:S(2)}) collective-permute-start(bf16[4,96,768]{2,1,0:T(8,128)(2,1)S(1)} %pad_maximum_fusion.6.held), channel_id=1, source_target_pairs={{0,2},{1,3},{2,0},{3,1},{4,6},{5,7},{6,4},{7,5},{8,10},{9,11},{10,... | collective-permute-start | bytes 1769480 | tf_op jit(solution)/shard_map/ppermute | solution.py:23
  190.3 16.7 %collective-permute-start.51 = (bf16[416,384]{1,0:T(8,128)(2,1)}, bf16[416,384]{1,0:T(8,128)(2,1)}, u32[]{:S(2)}, u32[]{:S(2)}) collective-permute-start(bf16[416,384]{1,0:T(8,128)(2,1)} %pad_maximum_fusion.7), channel_id=1, source_target_pairs={{0,1},{1,0},{2,3},{3,2},{4,5},{5,4},{6,7},{7,6},{8,9},{9,8},{10,11... | collective-permute-start | bytes 958472 | tf_op jit(solution)/shard_map/ppermute | solution.py:23
  191.1 15.9 %collective-permute-start.48 = (bf16[4,96,384]{2,1,0:T(8,128)(2,1)S(1)}, bf16[4,96,384]{2,1,0:T(8,128)(2,1)}, u32[]{:S(2)}, u32[]{:S(2)}) collective-permute-start(bf16[4,96,384]{2,1,0:T(8,128)(2,1)S(1)} %pad_maximum_fusion.8.held_one), channel_id=1, source_target_pairs={{0,2},{1,3},{2,0},{3,1},{4,6},{5,7},{6,4},{7,5},{8,10},{9,11},{10,... | collective-permute-start | bytes 884744 | tf_op jit(solution)/shard_map/ppermute | solution.py:23
  (71 other events, 414.2 us)

commit v4 on v3

--- a/solution.py
+++ b/solution.py
@@ -210,6 +210,19 @@
     sums[...] = vecs[...] + got_two[G * held_two.shape[1] :, :].astype(F32)
 
 
+def hidden_kernel(index, own, near, far, last, up, bias, down, act, slope, *outs):
+    rows = own.shape[0]
+    for block, ref in enumerate((own, near, far, last)):
+        where = pl.ds(block * rows, rows)
+        pre = dot(ref[...], up[...]) + bias[...]
+        cdf = 0.5 * (1.0 + lax.erf(pre * (0.5**0.5)))
+        act[where, :] = (pre * cdf).astype(BF)
+        slope[where, :] = cdf + pre * jnp.exp(-0.5 * pre * pre) * ((2 * jnp.pi) ** -0.5)
+    for block, out in enumerate(outs):
+        where = pl.ds(block * rows, rows)
+        out[...] = dot(act[where, :], down[...]).astype(out.dtype)
+
+
 def attention_back_kernel(index, d_branch, out_weight, proj, lse, seg_key, seg_query, attended, x, *outs):
     d_qk, d_v, one, two, one_send, two_send = outs
     part = out_weight.shape[0]
@@ -230,9 +243,10 @@
         d_v[at : at + HD, :] = dot_t(d_o, probs.astype(BF)).astype(BF)
         d_qk[at : at + HD, :] = (dot(k, d_scores) * scale).astype(BF)
         d_qk[part + at : part + at + HD, :] = (dot_t(q, d_scores) * scale).astype(BF)
-    grad_out = dot(attended[...], d_branch[...])
-    grad_v = dot_t(x[...], d_v[...])
-    grad_qk = dot_t(x[...], d_qk[...])
+    grad_out = dot(attended[...].T, d_branch[...])
+    x_turned = x[...].T
+    grad_v = dot_t(x_turned, d_v[...])
+    grad_qk = dot_t(x_turned, d_qk[...])
     for i in range(G):
         where = slice(i * part, (i + 1) * part)
         one[i] = jnp.concatenate([grad_out[:, where], grad_v[where, :]], axis=1).astype(BF)
@@ -382,13 +396,25 @@
     first = own_x.astype(F32) + branch + out_b
     hat1, scale1 = norm_parts(first)
     normed = hat1 * gain1 + shift1
-    normed_low = jnp.concatenate(gather_rows(after(normed.astype(BF), up_local)), axis=0)
-    pre = dot(normed_low, up_local) + up_bias
-    cdf = 0.5 * (1.0 + lax.erf(pre * (0.5**0.5)))
-    act = (pre * cdf).astype(BF)
-    slope = cdf + pre * jnp.exp(-0.5 * pre * pre) * ((2 * jnp.pi) ** -0.5)
-    second = dot(act, down_weight)
-    second = scatter_rows([second[k * rows : (k + 1) * rows] for k in range(G)])
+    normed_blocks = gather_rows(after(normed.astype(BF), up_local))
+    normed_low = jnp.concatenate(normed_blocks, axis=0)
+    block = jax.ShapeDtypeStruct((rows, width), F32)
+    block_low = jax.ShapeDtypeStruct((rows, width), BF)
+    act, slope, second, near, far, far_send = call(
+        hidden_kernel,
+        [
+            jax.ShapeDtypeStruct((G * rows, hidden), BF),
+            jax.ShapeDtypeStruct((G * rows, hidden), F32),
+            block,
+            block_low,
+            block,
+            block_low,
+        ],
+        [index, *normed_blocks, up_local, up_bias.reshape(1, hidden), down_weight],
+    )
+    far = far + gx(far_send, 1).astype(F32)
+    near = gx(near, 1)
+    second = second + near.astype(F32) + gx(far.astype(BF), 2).astype(F32)
     hat2, scale2 = norm_parts(normed + second + down_b)
     output = (hat2 * gain2 + shift2).astype(BF)
 
@@ -440,8 +466,8 @@
             jnp.concatenate(lse),
             segs.reshape(-1, 1),
             segs.reshape(1, -1),
-            attended.T,
-            x_all.T,
+            attended,
+            x_all,
         ],
     )
     one = Scatter(grad_one, first_z, me, replicas)
@@ -478,10 +504,10 @@
         [index, far, vecs, after(far_got, two_got)],
     )
     far = gx(far, 2)
-    down_piece = down.piece(after(down_got, one_got, two_got))
     up_piece = up.piece(after(up_got, one_got, two_got))
 
     one_got, two_got = one.step(one_got), two.step(two_got)
+    down_piece = down.piece(after(down_got, one.sent, two.sent))
 
     def outgoing(pieces):
         return [lax.dynamic_index_in_dim(pieces, place ^ k, 0, keepdims=False) for k in range(G)]
@@ -489,7 +515,7 @@
     def exchange(pieces):
         return jnp.stack([pieces[0]] + [gx(pieces[k], k) for k in range(1, G)])
 
-    down = Gather(after(down_piece, two_send), first_y, me, replicas)
+    down = Gather(down_piece, first_y, me, replicas)
     down_got = down.swap()
     up_piece = exchange(outgoing(up_piece))
     one_got, two_got = after((one_got, two_got), far)
@@ -516,6 +542,7 @@
     one_got, two_got = one.swap(), two.swap()
     up_got = up.step(after(up_got, one.value))
     down_got = down.step(after(down_got, one.value))
+    one_got, two_got = after((one_got, two_got), down.value)
 
     while len(one.left) > 1:
         one_got, two_got = one.step(one_got), two.step(two_got)

time: 213 us -> 207 us (0.972)
  waiting for transfers between devices: 84.9 us -> 77.4 us
  matrix products: 12.8 us -> 9.41 us
  Pallas kernels: 15.8 us -> 18.7 us
    ppermute x24, waiting for transfers between devices: 45.4 us -> 40.7 us  [rx(): return lax.ppermute(value, 'replica', [(i, i ^ bits) for i in range(count)])]
    dot_general x7 -> x5, matrix products: 7.22 us -> 4.1 us  [dot(): return jnp.dot(a, b, preferred_element_type=F32)]
    pallas_call x7 -> x8, Pallas kernels: 15.8 us -> 18.7 us  [call(): pl.pallas_call(kernel, out_shape=outs, in_specs=[index_spec()] + [whole_s...]
    ppermute x39, waiting for transfers between devices: 39.5 us -> 36.7 us  [gx(): return lax.ppermute(value, 'group', [(i, i ^ bits) for i in range(G)])]
    unnamed x115 -> x96, local copies, waits for them, and re-layouts: 4.12 us -> 6.81 us
    transpose x2 -> x0, other arithmetic: 2.17 us -> none  [on_device(): d_qk, d_v, grad_one, grad_two, one_send, two_send = call(attention_back_k...]
  transfers between devices with their start and end apart: 63 -> 63, of which waited for: 28 -> 25; matrix products, arithmetic and copies ran while one was open for 21% -> 22% of each run, Pallas kernels for 6% -> 6%
where the time goes in v4:
time: 207 us; the launch traced here: 206 us
  waiting for transfers between devices  77.4 us (37%)
  starting transfers between devices  48 us (23%)
  other arithmetic  32 us (15%)
  Pallas kernels  18.7 us (9%)
  local copies, waits for them, and re-layouts  18.5 us (9%)
  matrix products  9.41 us (5%)
    ppermute x24, waiting for transfers between devices, rx(): return lax.ppermute(value, 'replica', [(i, i ^ bits) for i in range(count)])  40.7 us
    ppermute x39, waiting for transfers between devices, gx(): return lax.ppermute(value, 'group', [(i, i ^ bits) for i in range(G)])  36.7 us
    ppermute x24, starting transfers between devices, rx(): return lax.ppermute(value, 'replica', [(i, i ^ bits) for i in range(count)])  28.9 us
    ppermute x39, starting transfers between devices, gx(): return lax.ppermute(value, 'group', [(i, i ^ bits) for i in range(G)])  19.1 us
    pallas_call x8, Pallas kernels, call(): pl.pallas_call(kernel, out_shape=outs, in_specs=[index_spec()] + [whole_s...  18.7 us
    convert_element_type x8, other arithmetic, send(): self.sent = self.total(1 - self.mine).astype(BF)  9.65 us
    unnamed x96, local copies, waits for them, and re-layouts  6.81 us
    concatenate x1, local copies, waits for them, and re-layouts, on_device(): small = jnp.concatenate(smalls).reshape(1, -1)  4.81 us
  transfers between devices with their start and end apart: 63, of which 25 were waited for; matrix products, arithmetic and copies ran while one was open for 22% of the time, Pallas kernels for 6%

profile of v4, /device:TPU:0, one launch (start us, length us, event | category | flops | bytes accessed | tf_op | source)
XLA Modules:
  0.0 206.0 jit_solution(11889881018244062078)
XLA Ops:
  1.2 2.6 %collective-permute-start.1 = (bf16[128,768]{1,0:T(8,128)(2,1)}, bf16[128,768]{1,0:T(8,128)(2,1)S(1)}, u32[]{:S(2)}, u32[]{:S(2)}) collective-permute-start(bf16[128,768]{1,0:T(8,128)(2,1)} %bitcast.115), channel_id=1, source_target_pairs={{0,16},{8,24},{16,0},{24,8},{1,17},{9,25},{17,1},{25,9},{2,18},{10... | collective-permute-start | bytes 589832 | tf_op jit(solution)/shard_map/ppermute | solution.py:19
  6.0 2.0 collective-permute-start.4
  9.7 4.8 %concatenate.81 = bf16[1536]{0:T(1024)(128)(2,1)S(1)} concatenate(bf16[384]{0:T(512)(128)(2,1)} %param.19, bf16[192]{0:T(256)(128)(2,1)} %param.21, bf16[192]{0:T(256)(128)(2,1)} %param.22, bf16[192]{0:T(256)(128)(2,1)} %param.23, bf16[192]{0:T(256)(128)(2,1)} %param.27, bf16[192]{0:T(256)(128)(2,1)} %param.28, bf16[192]{0:T(256)(128)(2,1)} %param.29), dimensions={0} | concatenate | bytes 6144 | tf_op jit(solution)/shard_map/concatenate | solution.py:357
  14.6 2.0 collective-permute-start.6
  16.8 2.3 %constant_dynamic-slice_fusion.4 = (bf16[192,768]{1,0:T(8,128)(2,1)}, bf16[192,768]{1,0:T(8,128)(2,1)}, bf16[192,768]{1,0:T(8,128)(2,1)}, bf16[192,768]{1,0:T(8,128)(2,1)}) fusion(bf16[192,3072]{1,0:T(8,128)(2,1)} %param.24, s32[]{:T(128)S(6)} %select_n.356, s32[]{:T(128)S(6)} %select_n.355, s32[]{:T(128)S(6)} %select_n.354, s32[]{:T(128)S(6)} %select_n.353), kind=kLoop, calls=%fused_computation.172 | loop fusion | bytes 2359312 | tf_op jit(solution)/shard_map/dynamic_slice | solution.py:366
  23.2 1.6 fusion
  25.2 1.3 fusion.71
  27.5 1.4 fusion.2
  28.9 1.5 convolution_convert_fusion.3
  32.1 2.1 %collective-permute-done.11 = bf16[192,768]{1,0:T(8,128)(2,1)} collective-permute-done((bf16[192,768]{1,0:T(8,128)(2,1)}, bf16[192,768]{1,0:T(8,128)(2,1)}, u32[]{:S(2)}, u32[]{:S(2)}) %collective-permute-start.11) | collective-permute-done | bytes 294944 | tf_op jit(solution)/shard_map/ppermute | solution.py:19
  40.4 4.5 %collective-permute-done.14 = bf16[128,768]{1,0:T(8,128)(2,1)S(1)} collective-permute-done((bf16[128,768]{1,0:T(8,128)(2,1)S(1)}, bf16[128,768]{1,0:T(8,128)(2,1)S(1)}, u32[]{:S(2)}, u32[]{:S(2)}) %collective-permute-start.14) | collective-permute-done | bytes 196640 | tf_op jit(solution)/shard_map/ppermute | solution.py:19
  46.8 6.1 %collective-permute-done.16.far = bf16[128,768]{1,0:T(8,128)(2,1)S(1)} collective-permute-done((bf16[128,768]{1,0:T(8,128)(2,1)S(1)}, bf16[128,768]{1,0:T(8,128)(2,1)S(1)}, u32[]{:S(2)}, u32[]{:S(2)}) %collective-permute-start.16) | collective-permute-done | bytes 196640 | tf_op jit(solution)/shard_map/ppermute | solution.py:19
  52.9 1.4 collective-permute-done.17.last
  54.3 3.2 %shard_map.255 = (bf16[512,768]{1,0:T(8,128)(2,1)S(1)}, f32[512,768]{1,0:T(8,128)}, f32[128,768]{1,0:T(8,128)S(1)}, bf16[128,768]{1,0:T(8,128)(2,1)S(1)}, f32[12...) custom-call(s32[3]{0:T(128)S(1)} %pad_add_fusion.1.index, bf16[128,768]{1,0:T(8,128)(2,1)S(1)} %fusion.24.own, ...), custom_call_target="tpu_custom_call" | custom-call | tf_op jit(solution)/shard_map/pallas_call | solution.py:140
  63.8 6.7 %collective-permute-done.20 = bf16[128,768]{1,0:T(8,128)(2,1)S(1)} collective-permute-done((bf16[128,768]{1,0:T(8,128)(2,1)S(1)}, bf16[128,768]{1,0:T(8,128)(2,1)S(1)}, u32[]{:S(2)}, u32[]{:S(2)}) %collective-permute-start.20) | collective-permute-done | bytes 196640 | tf_op jit(solution)/shard_map/ppermute | solution.py:19
  70.5 1.5 fusion.63
  73.0 5.8 %collective-permute-done.22 = bf16[128,768]{1,0:T(8,128)(2,1)S(1)} collective-permute-done((bf16[128,768]{1,0:T(8,128)(2,1)S(1)}, bf16[128,768]{1,0:T(8,128)(2,1)S(1)}, u32[]{:S(2)}, u32[]{:S(2)}) %collective-permute-start.22) | collective-permute-done | bytes 196640 | tf_op jit(solution)/shard_map/ppermute | solution.py:19
  78.9 1.4 collective-permute-done.23
  83.9 1.6 collective-permute-start.30
  87.2 1.6 collective-permute-start.31
  88.9 3.4 %collective-permute-done.26 = bf16[128,768]{1,0:T(8,128)(2,1)S(1)} collective-permute-done((bf16[128,768]{1,0:T(8,128)(2,1)S(1)}, bf16[128,768]{1,0:T(8,128)(2,1)S(1)}, u32[]{:S(2)}, u32[]{:S(2)}) %collective-permute-start.26) | collective-permute-done | bytes 196640 | tf_op jit(solution)/shard_map/ppermute | solution.py:19
  96.0 3.3 %collective-permute-done.30 = bf16[1,384,768]{2,1,0:T(8,128)(2,1)S(1)} collective-permute-done((bf16[1,384,768]{2,1,0:T(8,128)(2,1)S(1)}, bf16[1,384,768]{2,1,0:T(8,128)(2,1)S(1)}, u32[]{:S(2)}, u32[]{:S(2)}) %collective-permute-start.30) | collective-permute-done | bytes 589856 | tf_op jit(solution)/shard_map/ppermute | solution.py:23
  100.9 1.6 collective-permute-start.36
  104.4 4.7 %shard_map.256 = (bf16[384,512]{1,0:T(8,128)(2,1)S(1)}, bf16[192,512]{1,0:T(8,128)(2,1)S(1)}, bf16[4,192,384]{2,1,0:T(8,128)(2,1)S(1)}, bf16[4,192,384]{2,1,0:T(...) custom-call(s32[3]{0:T(128)S(1)} %pad_add_fusion.1.index, ...), custom_call_target="tpu_custom_call" | custom-call | tf_op jit(solution)/shard_map/pallas_call | solution.py:140
  109.9 1.6 collective-permute-start.34
  112.2 1.8 fusion.29
  114.0 1.8 add_convert_fusion.8
  115.8 2.6 %collective-permute-start.56 = (bf16[4,24,768]{2,1,0:T(8,128)(2,1)}, bf16[4,24,768]{2,1,0:T(8,128)(2,1)}, u32[]{:S(2)}, u32[]{:S(2)}) collective-permute-start(bf16[4,24,768]{2,1,0:T(8,128)(2,1)} %add_convert_fusion.8), channel_id=1, source_target_pairs={{0,4},{1,5},{2,6},{3,7},{4,0},{5,1},{6,2},{7,3},{8,12},{9,13},{10,... | collective-permute-start | bytes 442376 | tf_op jit(solution)/shard_map/ppermute | solution.py:23
  118.4 2.1 %collective-permute-done.34 = bf16[4,96,384]{2,1,0:T(8,128)(2,1)} collective-permute-done((bf16[4,96,384]{2,1,0:T(8,128)(2,1)}, bf16[4,96,384]{2,1,0:T(8,128)(2,1)}, u32[]{:S(2)}, u32[]{:S(2)}) %collective-permute-start.34) | collective-permute-done | bytes 294944 | tf_op jit(solution)/shard_map/ppermute | solution.py:23
  120.5 1.8 add_convert_fusion.6
  124.4 2.4 %shard_map.257 = (bf16[128,768]{1,0:T(8,128)(2,1)}, bf16[144,768]{1,0:T(8,128)(2,1)S(1)}, f32[128,768]{1,0:T(8,128)S(1)}, f32[128,768]{1,0:T(8,128)S(1)}, f32[16,768]{1,0:T(8,128)S(1)}) custom-call(s32[3]{0:T(128)S(1)} %pad_add_fusion.1.index, bf16[384,512]{1,0:T(8,128)(2,1)S(1)} %get-tuple-element.109.d_qk, bf16[192,512]{1,0:T(8,128)(2,1)S(1)} %get-tuple-element.110.d_v, ...), custom_call_target="tpu_custom_call" | custom-call | tf_op jit(solution)/shard_map/pallas_call | solution.py:140
  127.4 2.4 %collective-permute-start.48 = (bf16[1,96,768]{2,1,0:T(8,128)(2,1)S(1)}, bf16[1,96,768]{2,1,0:T(8,128)(2,1)S(1)}, u32[]{:S(2)}, u32[]{:S(2)}) collective-permute-start(bf16[1,96,768]{2,1,0:T(8,128)(2,1)S(1)} %copy-done.45), channel_id=1, source_target_pairs={{0,4},{1,5},{2,6},{3,7},{4,0},{5,1},{6,2},{7,3},{8,12},{9,13},{10,... | collective-permute-start | bytes 442376 | tf_op jit(solution)/shard_map/ppermute | solution.py:23
  135.6 1.6 collective-permute-done.48
  139.9 2.0 collective-permute-start.41
  142.9 8.1 %collective-permute-done.42 = bf16[4,24,384]{2,1,0:T(8,128)(2,1)S(1)} collective-permute-done((bf16[4,24,384]{2,1,0:T(8,128)(2,1)S(1)}, bf16[4,24,384]{2,1,0:T(8,128)(2,1)S(1)}, u32[]{:S(2)}, u32[]{:S(2)}) %collective-permute-start.42) | collective-permute-done | bytes 73760 | tf_op jit(solution)/shard_map/ppermute | solution.py:23
  151.0 1.6 collective-permute-done.41
  154.9 1.4 collective-permute-start.44
  156.9 2.0 collective-permute-start.50
  160.2 2.7 %collective-permute-start.46 = (bf16[4,24,384]{2,1,0:T(8,128)(2,1)S(1)}, bf16[4,24,384]{2,1,0:T(8,128)(2,1)S(1)}, u32[]{:S(2)}, u32[]{:S(2)}) collective-permute-start(bf16[4,24,384]{2,1,0:T(8,128)(2,1)S(1)} %pad_maximum_fusion.21), channel_id=1, source_target_pairs={{0,4},{1,5},{2,6},{3,7},{4,0},{5,1},{6,2},{7,3},{8,12},{9,13},{10,... | collective-permute-start | bytes 221192 | tf_op jit(solution)/shard_map/ppermute | solution.py:23
  163.0 2.9 %collective-permute-done.60 = bf16[4,24,768]{2,1,0:T(8,128)(2,1)S(1)} collective-permute-done((bf16[4,24,768]{2,1,0:T(8,128)(2,1)S(1)}, bf16[4,24,768]{2,1,0:T(8,128)(2,1)S(1)}, u32[]{:S(2)}, u32[]{:S(2)}) %collective-permute-start.60) | collective-permute-done | bytes 147488 | tf_op jit(solution)/shard_map/ppermute | solution.py:23
  166.5 6.1 %collective-permute-done.50 = bf16[1,192,768]{2,1,0:T(8,128)(2,1)S(1)} collective-permute-done((bf16[1,192,768]{2,1,0:T(8,128)(2,1)S(1)}, bf16[1,192,768]{2,1,0:T(8,128)(2,1)S(1)}, u32[]{:S(2)}, u32[]{:S(2)}) %collective-permute-start.50) | collective-permute-done | bytes 294944 | tf_op jit(solution)/shard_map/ppermute | solution.py:23
  174.3 1.5 collective-permute-start.51
  176.2 2.1 %collective-permute-start.62 = (bf16[4,96,768]{2,1,0:T(8,128)(2,1)S(1)}, bf16[4,96,768]{2,1,0:T(8,128)(2,1)S(1)}, u32[]{:S(2)}, u32[]{:S(2)}) collective-permute-start(bf16[4,96,768]{2,1,0:T(8,128)(2,1)S(1)} %pad_maximum_fusion.6.held), channel_id=1, source_target_pairs={{0,2},{1,3},{2,0},{3,1},{4,6},{5,7},{6,4},{7,5},{8,10},{9,11},{10,... | collective-permute-start | bytes 1769480 | tf_op jit(solution)/shard_map/ppermute | solution.py:23
  178.3 13.4 %collective-permute-done.51 = bf16[4,48,384]{2,1,0:T(8,128)(2,1)S(1)} collective-permute-done((bf16[4,48,384]{2,1,0:T(8,128)(2,1)S(1)}, bf16[4,48,384]{2,1,0:T(8,128)(2,1)S(1)}, u32[]{:S(2)}, u32[]{:S(2)}) %collective-permute-start.51) | collective-permute-done | bytes 147488 | tf_op jit(solution)/shard_map/ppermute | solution.py:23
  193.4 1.9 add_convert_fusion.1
  195.3 2.1 %shard_map.259 = f32[768,768]{1,0:T(8,128)} custom-call(s32[3]{0:T(128)S(1)} %pad_add_fusion.1.index, bf16[384,768]{1,0:T(8,128)(2,1)S(1)} %get-tuple-element.189.held, bf16[384,768]{1,0:T(8,128)(2,1)S(1)} %bitcast.107), custom_call_target="tpu_custom_call" | custom-call | tf_op jit(solution)/shard_map/pallas_call | solution.py:140
  197.4 2.1 %shard_map.260 = f32[192,3072]{1,0:T(8,128)} custom-call(s32[3]{0:T(128)S(1)} %pad_add_fusion.1.index, bf16[4,96,768]{2,1,0:T(8,128)(2,1)S(1)} %pad_maximum_fusion.6.held, bf16[4,96,768]{2,1,0:T(8,128)(2,1)S(1)} %collective-permute-done.62.got), custom_call_target="tpu_custom_call" | custom-call | tf_op jit(solution)/shard_map/pallas_call | solution.py:140
  201.1 2.8 %shard_map.261 = (f32[192,768]{1,0:T(8,128)}, f32[192,2304]{1,0:T(8,128)}, f32[32,384]{1,0:T(8,128)S(1)}) custom-call(s32[3]{0:T(128)S(1)} %pad_add_fusion.1.index, bf16[4,96,384]{2,1,0:T(8,128)(2,1)S(1)} %pad_maximum_fusion.9.held_one, bf16[4,96,384]{2,1,0:T(8,128)(2,1)} %collective-permute-done.52.got_one, ...), custom_call_target="tpu_custom_call" | custom-call | tf_op jit(solution)/shard_map/pallas_call | solution.py:140
  (323 shorter events, 64.9 us)
Async XLA Ops:
  0.6 9.1 %collective-permute-start = (bf16[128,768]{1,0:T(8,128)(2,1)}, bf16[128,768]{1,0:T(8,128)(2,1)S(1)}, u32[]{:S(2)}, u32[]{:S(2)}) collective-permute-start(bf16[128,768]{1,0:T(8,128)(2,1)} %bitcast.114), channel_id=1, source_target_pairs={{0,8},{8,0},{16,24},{24,16},{1,9},{9,1},{17,25},{25,17},{2,10},{10... | collective-permute-start | bytes 589832 | tf_op jit(solution)/shard_map/ppermute | solution.py:19
  1.2 8.5 %collective-permute-start.1 = (bf16[128,768]{1,0:T(8,128)(2,1)}, bf16[128,768]{1,0:T(8,128)(2,1)S(1)}, u32[]{:S(2)}, u32[]{:S(2)}) collective-permute-start(bf16[128,768]{1,0:T(8,128)(2,1)} %bitcast.115), channel_id=1, source_target_pairs={{0,16},{8,24},{16,0},{24,8},{1,17},{9,25},{17,1},{25,9},{2,18},{10... | collective-permute-start | bytes 589832 | tf_op jit(solution)/shard_map/ppermute | solution.py:19
  6.0 13.0 %collective-permute-start.3 = (bf16[192,576]{1,0:T(8,128)(2,1)S(1)}, bf16[192,576]{1,0:T(8,128)(2,1)S(1)}, u32[]{:S(2)}, u32[]{:S(2)}) collective-permute-start(bf16[192,576]{1,0:T(8,128)(2,1)S(1)} %get-tuple-element.80), channel_id=1, source_target_pairs={{0,24},{8,16},{16,8},{24,0},{1,25},{9,17},{17,9},{25,1},{2,26},{10... | collective-permute-start | bytes 663560 | tf_op jit(solution)/shard_map/ppermute | solution.py:19
  6.0 14.0 %collective-permute-start.4 = (bf16[192,576]{1,0:T(8,128)(2,1)S(1)}, bf16[192,576]{1,0:T(8,128)(2,1)S(1)}, u32[]{:S(2)}, u32[]{:S(2)}) collective-permute-start(bf16[192,576]{1,0:T(8,128)(2,1)S(1)} %get-tuple-element.81), channel_id=1, source_target_pairs={{0,16},{8,24},{16,0},{24,8},{1,17},{9,25},{17,1},{25,9},{2,18},{10... | collective-permute-start | bytes 663560 | tf_op jit(solution)/shard_map/ppermute | solution.py:19
  9.7 13.5 %collective-permute-start.2 = (bf16[128,768]{1,0:T(8,128)(2,1)S(1)}, bf16[128,768]{1,0:T(8,128)(2,1)}, u32[]{:S(2)}, u32[]{:S(2)}) collective-permute-start(bf16[128,768]{1,0:T(8,128)(2,1)S(1)} %collective-permute-done.1), channel_id=1, source_target_pairs={{0,8},{8,0},{16,24},{24,16},{1,9},{9,1},{17,25},{25,17},{2,10},{10... | collective-permute-start | bytes 589832 | tf_op jit(solution)/shard_map/ppermute | solution.py:19
  14.6 6.6 %collective-permute-start.6 = (bf16[1,1536]{1,0:T(2,128)(2,1)S(1)}, bf16[1,1536]{1,0:T(2,128)(2,1)S(1)}, u32[]{:S(2)}, u32[]{:S(2)}) collective-permute-start(bf16[1,1536]{1,0:T(2,128)(2,1)S(1)} %reshape.216), channel_id=1, source_target_pairs={{0,16},{8,24},{16,0},{24,8},{1,17},{9,25},{17,1},{25,9},{2,18},{10... | collective-permute-start | bytes 9224 | tf_op jit(solution)/shard_map/ppermute | solution.py:19
  19.0 13.1 %collective-permute-start.10 = (bf16[192,768]{1,0:T(8,128)(2,1)}, bf16[192,768]{1,0:T(8,128)(2,1)}, u32[]{:S(2)}, u32[]{:S(2)}) collective-permute-start(bf16[192,768]{1,0:T(8,128)(2,1)} %get-tuple-element.176), channel_id=1, source_target_pairs={{0,16},{8,24},{16,0},{24,8},{1,17},{9,25},{17,1},{25,9},{2,18},{10... | collective-permute-start | bytes 884744 | tf_op jit(solution)/shard_map/ppermute | solution.py:19
  20.0 14.2 %collective-permute-start.11 = (bf16[192,768]{1,0:T(8,128)(2,1)}, bf16[192,768]{1,0:T(8,128)(2,1)}, u32[]{:S(2)}, u32[]{:S(2)}) collective-permute-start(bf16[192,768]{1,0:T(8,128)(2,1)} %get-tuple-element.175), channel_id=1, source_target_pairs={{0,24},{8,16},{16,8},{24,0},{1,25},{9,17},{17,9},{25,1},{2,26},{10... | collective-permute-start | bytes 884744 | tf_op jit(solution)/shard_map/ppermute | solution.py:19
  22.2 12.0 %collective-permute-start.9 = (bf16[192,768]{1,0:T(8,128)(2,1)}, bf16[192,768]{1,0:T(8,128)(2,1)}, u32[]{:S(2)}, u32[]{:S(2)}) collective-permute-start(bf16[192,768]{1,0:T(8,128)(2,1)} %get-tuple-element.177), channel_id=1, source_target_pairs={{0,8},{8,0},{16,24},{24,16},{1,9},{9,1},{17,25},{25,17},{2,10},{10... | collective-permute-start | bytes 884744 | tf_op jit(solution)/shard_map/ppermute | solution.py:19
  37.7 7.2 %collective-permute-start.14 = (bf16[128,768]{1,0:T(8,128)(2,1)S(1)}, bf16[128,768]{1,0:T(8,128)(2,1)S(1)}, u32[]{:S(2)}, u32[]{:S(2)}) collective-permute-start(bf16[128,768]{1,0:T(8,128)(2,1)S(1)} %add_convert_fusion.4), channel_id=1, source_target_pairs={{0,16},{8,24},{16,0},{24,8},{1,17},{9,25},{17,1},{25,9},{2,18},{10... | collective-permute-start | bytes 589832 | tf_op jit(solution)/shard_map/ppermute | solution.py:19
  46.5 6.4 %collective-permute-start.16 = (bf16[128,768]{1,0:T(8,128)(2,1)S(1)}, bf16[128,768]{1,0:T(8,128)(2,1)S(1)}, u32[]{:S(2)}, u32[]{:S(2)}) collective-permute-start(bf16[128,768]{1,0:T(8,128)(2,1)S(1)} %fusion.24.own), channel_id=1, source_target_pairs={{0,16},{8,24},{16,0},{24,8},{1,17},{9,25},{17,1},{25,9},{2,18},{10... | collective-permute-start | bytes 589832 | tf_op jit(solution)/shard_map/ppermute | solution.py:19
  46.8 6.1 %collective-permute-start.15 = (bf16[128,768]{1,0:T(8,128)(2,1)S(1)}, bf16[128,768]{1,0:T(8,128)(2,1)S(1)}, u32[]{:S(2)}, u32[]{:S(2)}) collective-permute-start(bf16[128,768]{1,0:T(8,128)(2,1)S(1)} %fusion.24.own), channel_id=1, source_target_pairs={{0,8},{8,0},{16,24},{24,16},{1,9},{9,1},{17,25},{25,17},{2,10},{10... | collective-permute-start | bytes 589832 | tf_op jit(solution)/shard_map/ppermute | solution.py:19
  63.5 7.0 %collective-permute-start.20 = (bf16[128,768]{1,0:T(8,128)(2,1)S(1)}, bf16[128,768]{1,0:T(8,128)(2,1)S(1)}, u32[]{:S(2)}, u32[]{:S(2)}) collective-permute-start(bf16[128,768]{1,0:T(8,128)(2,1)S(1)} %add_convert_fusion.3), channel_id=1, source_target_pairs={{0,16},{8,24},{16,0},{24,8},{1,17},{9,25},{17,1},{25,9},{2,18},{10... | collective-permute-start | bytes 589832 | tf_op jit(solution)/shard_map/ppermute | solution.py:19
  72.7 6.2 %collective-permute-start.22 = (bf16[128,768]{1,0:T(8,128)(2,1)S(1)}, bf16[128,768]{1,0:T(8,128)(2,1)S(1)}, u32[]{:S(2)}, u32[]{:S(2)}) collective-permute-start(bf16[128,768]{1,0:T(8,128)(2,1)S(1)} %get-tuple-element.162), channel_id=1, source_target_pairs={{0,16},{8,24},{16,0},{24,8},{1,17},{9,25},{17,1},{25,9},{2,18},{10... | collective-permute-start | bytes 589832 | tf_op jit(solution)/shard_map/ppermute | solution.py:19
  73.0 5.8 %collective-permute-start.21 = (bf16[128,768]{1,0:T(8,128)(2,1)S(1)}, bf16[128,768]{1,0:T(8,128)(2,1)S(1)}, u32[]{:S(2)}, u32[]{:S(2)}) collective-permute-start(bf16[128,768]{1,0:T(8,128)(2,1)S(1)} %get-tuple-element.162), channel_id=1, source_target_pairs={{0,8},{8,0},{16,24},{24,16},{1,9},{9,1},{17,25},{25,17},{2,10},{10... | collective-permute-start | bytes 589832 | tf_op jit(solution)/shard_map/ppermute | solution.py:19
  82.6 6.3 %collective-permute-start.24 = (bf16[128,768]{1,0:T(8,128)(2,1)S(1)}, bf16[128,768]{1,0:T(8,128)(2,1)S(1)}, u32[]{:S(2)}, u32[]{:S(2)}) collective-permute-start(bf16[128,768]{1,0:T(8,128)(2,1)S(1)} %get-tuple-element.183), channel_id=1, source_target_pairs={{0,8},{8,0},{16,24},{24,16},{1,9},{9,1},{17,25},{25,17},{2,10},{10... | collective-permute-start | bytes 589832 | tf_op jit(solution)/shard_map/ppermute | solution.py:19
  83.9 15.4 %collective-permute-start.30 = (bf16[1,384,768]{2,1,0:T(8,128)(2,1)S(1)}, bf16[1,384,768]{2,1,0:T(8,128)(2,1)S(1)}, u32[]{:S(2)}, u32[]{:S(2)}) collective-permute-start(bf16[1,384,768]{2,1,0:T(8,128)(2,1)S(1)} %dynamic-slice_bitcast_fusion), channel_id=1, source_target_pairs={{0,1},{1,0},{2,3},{3,2},{4,5},{5,4},{6,7},{7,6},{8,9},{9,8},{10,11... | collective-permute-start | bytes 1769480 | tf_op jit(solution)/shard_map/ppermute | solution.py:23
  85.5 6.7 %collective-permute-start.26 = (bf16[128,768]{1,0:T(8,128)(2,1)S(1)}, bf16[128,768]{1,0:T(8,128)(2,1)S(1)}, u32[]{:S(2)}, u32[]{:S(2)}) collective-permute-start(bf16[128,768]{1,0:T(8,128)(2,1)S(1)} %fusion.21), channel_id=1, source_target_pairs={{0,16},{8,24},{16,0},{24,8},{1,17},{9,25},{17,1},{25,9},{2,18},{10... | collective-permute-start | bytes 589832 | tf_op jit(solution)/shard_map/ppermute | solution.py:19
  87.2 15.2 %collective-permute-start.31 = (bf16[4,96,768]{2,1,0:T(8,128)(2,1)S(1)}, bf16[4,96,768]{2,1,0:T(8,128)(2,1)S(1)}, u32[]{:S(2)}, u32[]{:S(2)}) collective-permute-start(bf16[4,96,768]{2,1,0:T(8,128)(2,1)S(1)} %constant_dynamic-slice_fusion.3), channel_id=1, source_target_pairs={{0,2},{1,3},{2,0},{3,1},{4,6},{5,7},{6,4},{7,5},{8,10},{9,11},{10,... | collective-permute-start | bytes 1769480 | tf_op jit(solution)/shard_map/ppermute | solution.py:23
  94.3 5.8 %collective-permute-start.28 = (bf16[128,768]{1,0:T(8,128)(2,1)S(1)}, bf16[128,768]{1,0:T(8,128)(2,1)S(1)}, u32[]{:S(2)}, u32[]{:S(2)}) collective-permute-start(bf16[128,768]{1,0:T(8,128)(2,1)S(1)} %get-tuple-element.164), channel_id=1, source_target_pairs={{0,16},{8,24},{16,0},{24,8},{1,17},{9,25},{17,1},{25,9},{2,18},{10... | collective-permute-start | bytes 589832 | tf_op jit(solution)/shard_map/ppermute | solution.py:19
  95.9 8.4 %collective-permute-start.27 = (bf16[128,768]{1,0:T(8,128)(2,1)S(1)}, bf16[128,768]{1,0:T(8,128)(2,1)S(1)}, u32[]{:S(2)}, u32[]{:S(2)}) collective-permute-start(bf16[128,768]{1,0:T(8,128)(2,1)S(1)} %get-tuple-element.164), channel_id=1, source_target_pairs={{0,8},{8,0},{16,24},{24,16},{1,9},{9,1},{17,25},{25,17},{2,10},{10... | collective-permute-start | bytes 589832 | tf_op jit(solution)/shard_map/ppermute | solution.py:19
  100.9 11.3 %collective-permute-start.36 = (bf16[1,192,768]{2,1,0:T(8,128)(2,1)}, bf16[1,192,768]{2,1,0:T(8,128)(2,1)}, u32[]{:S(2)}, u32[]{:S(2)}) collective-permute-start(bf16[1,192,768]{2,1,0:T(8,128)(2,1)} %fusion.11), channel_id=1, source_target_pairs={{0,2},{1,3},{2,0},{3,1},{4,6},{5,7},{6,4},{7,5},{8,10},{9,11},{10,... | collective-permute-start | bytes 884744 | tf_op jit(solution)/shard_map/ppermute | solution.py:23
  103.4 10.6 %collective-permute-start.37 = (bf16[4,48,768]{2,1,0:T(8,128)(2,1)}, bf16[4,48,768]{2,1,0:T(8,128)(2,1)}, u32[]{:S(2)}, u32[]{:S(2)}) collective-permute-start(bf16[4,48,768]{2,1,0:T(8,128)(2,1)} %add_convert_fusion), channel_id=1, source_target_pairs={{0,1},{1,0},{2,3},{3,2},{4,5},{5,4},{6,7},{7,6},{8,9},{9,8},{10,11... | collective-permute-start | bytes 884744 | tf_op jit(solution)/shard_map/ppermute | solution.py:23
  109.9 10.6 %collective-permute-start.34 = (bf16[4,96,384]{2,1,0:T(8,128)(2,1)}, bf16[4,96,384]{2,1,0:T(8,128)(2,1)}, u32[]{:S(2)}, u32[]{:S(2)}) collective-permute-start(bf16[4,96,384]{2,1,0:T(8,128)(2,1)} %get-tuple-element.117), channel_id=1, source_target_pairs={{0,2},{1,3},{2,0},{3,1},{4,6},{5,7},{6,4},{7,5},{8,10},{9,11},{10,... | collective-permute-start | bytes 884744 | tf_op jit(solution)/shard_map/ppermute | solution.py:23
  111.5 9.0 %collective-permute-start.35 = (bf16[4,96,384]{2,1,0:T(8,128)(2,1)S(1)}, bf16[4,96,384]{2,1,0:T(8,128)(2,1)S(1)}, u32[]{:S(2)}, u32[]{:S(2)}) collective-permute-start(bf16[4,96,384]{2,1,0:T(8,128)(2,1)S(1)} %get-tuple-element.118), channel_id=1, source_target_pairs={{0,1},{1,0},{2,3},{3,2},{4,5},{5,4},{6,7},{7,6},{8,9},{9,8},{10,11... | collective-permute-start | bytes 884744 | tf_op jit(solution)/shard_map/ppermute | solution.py:23
  115.8 11.6 %collective-permute-start.56 = (bf16[4,24,768]{2,1,0:T(8,128)(2,1)}, bf16[4,24,768]{2,1,0:T(8,128)(2,1)}, u32[]{:S(2)}, u32[]{:S(2)}) collective-permute-start(bf16[4,24,768]{2,1,0:T(8,128)(2,1)} %add_convert_fusion.8), channel_id=1, source_target_pairs={{0,4},{1,5},{2,6},{3,7},{4,0},{5,1},{6,2},{7,3},{8,12},{9,13},{10,... | collective-permute-start | bytes 442376 | tf_op jit(solution)/shard_map/ppermute | solution.py:23
  122.3 7.5 %collective-permute-start.40 = (bf16[4,48,384]{2,1,0:T(8,128)(2,1)}, bf16[4,48,384]{2,1,0:T(8,128)(2,1)}, u32[]{:S(2)}, u32[]{:S(2)}) collective-permute-start(bf16[4,48,384]{2,1,0:T(8,128)(2,1)} %add_convert_fusion.6), channel_id=1, source_target_pairs={{0,1},{1,0},{2,3},{3,2},{4,5},{5,4},{6,7},{7,6},{8,9},{9,8},{10,11... | collective-permute-start | bytes 442376 | tf_op jit(solution)/shard_map/ppermute | solution.py:23
  126.8 6.0 %collective-permute-start.33 = (bf16[144,768]{1,0:T(8,128)(2,1)S(1)}, bf16[144,768]{1,0:T(8,128)(2,1)S(1)}, u32[]{:S(2)}, u32[]{:S(2)}) collective-permute-start(bf16[144,768]{1,0:T(8,128)(2,1)S(1)} %get-tuple-element.115), channel_id=1, source_target_pairs={{0,8},{8,0},{16,24},{24,16},{1,9},{9,1},{17,25},{25,17},{2,10},{10... | collective-permute-start | bytes 663560 | tf_op jit(solution)/shard_map/ppermute | solution.py:19
  126.8 66.6 %collective-permute-start.32 = (bf16[128,768]{1,0:T(8,128)(2,1)}, bf16[128,768]{1,0:T(8,128)(2,1)}, u32[]{:S(2)}, u32[]{:S(2)}) collective-permute-start(bf16[128,768]{1,0:T(8,128)(2,1)} %get-tuple-element.112), channel_id=1, source_target_pairs={{0,8},{8,0},{16,24},{24,16},{1,9},{9,1},{17,25},{25,17},{2,10},{10... | collective-permute-start | bytes 589832 | tf_op jit(solution)/shard_map/ppermute | solution.py:19
  127.4 9.9 %collective-permute-start.48 = (bf16[1,96,768]{2,1,0:T(8,128)(2,1)S(1)}, bf16[1,96,768]{2,1,0:T(8,128)(2,1)S(1)}, u32[]{:S(2)}, u32[]{:S(2)}) collective-permute-start(bf16[1,96,768]{2,1,0:T(8,128)(2,1)S(1)} %copy-done.45), channel_id=1, source_target_pairs={{0,4},{1,5},{2,6},{3,7},{4,0},{5,1},{6,2},{7,3},{8,12},{9,13},{10,... | collective-permute-start | bytes 442376 | tf_op jit(solution)/shard_map/ppermute | solution.py:23
  131.0 7.9 %collective-permute-start.57 = (bf16[24,768]{1,0:T(8,128)(2,1)S(1)}, bf16[24,768]{1,0:T(8,128)(2,1)S(1)}, u32[]{:S(2)}, u32[]{:S(2)}) collective-permute-start(bf16[24,768]{1,0:T(8,128)(2,1)S(1)} %get-tuple-element.207), channel_id=1, source_target_pairs={{0,8},{8,0},{16,24},{24,16},{1,9},{9,1},{17,25},{25,17},{2,10},{10... | collective-permute-start | bytes 110600 | tf_op jit(solution)/shard_map/ppermute | solution.py:19
  131.1 8.8 %collective-permute-start.58 = (bf16[24,768]{1,0:T(8,128)(2,1)S(1)}, bf16[24,768]{1,0:T(8,128)(2,1)S(1)}, u32[]{:S(2)}, u32[]{:S(2)}) collective-permute-start(bf16[24,768]{1,0:T(8,128)(2,1)S(1)} %get-tuple-element.206), channel_id=1, source_target_pairs={{0,16},{8,24},{16,0},{24,8},{1,17},{9,25},{17,1},{25,9},{2,18},{10... | collective-permute-start | bytes 110600 | tf_op jit(solution)/shard_map/ppermute | solution.py:19
  132.9 9.0 %collective-permute-start.59 = (bf16[24,768]{1,0:T(8,128)(2,1)S(1)}, bf16[24,768]{1,0:T(8,128)(2,1)S(1)}, u32[]{:S(2)}, u32[]{:S(2)}) collective-permute-start(bf16[24,768]{1,0:T(8,128)(2,1)S(1)} %get-tuple-element.205), channel_id=1, source_target_pairs={{0,24},{8,16},{16,8},{24,0},{1,25},{9,17},{17,9},{25,1},{2,26},{10... | collective-permute-start | bytes 110600 | tf_op jit(solution)/shard_map/ppermute | solution.py:19
  137.2 15.3 %collective-permute-start.39 = (bf16[144,768]{1,0:T(8,128)(2,1)S(1)}, bf16[144,768]{1,0:T(8,128)(2,1)S(1)}, u32[]{:S(2)}, u32[]{:S(2)}) collective-permute-start(bf16[144,768]{1,0:T(8,128)(2,1)S(1)} %get-tuple-element.123), channel_id=1, source_target_pairs={{0,16},{8,24},{16,0},{24,8},{1,17},{9,25},{17,1},{25,9},{2,18},{10... | collective-permute-start | bytes 663560 | tf_op jit(solution)/shard_map/ppermute | solution.py:19
  138.9 12.1 %collective-permute-start.42 = (bf16[4,24,384]{2,1,0:T(8,128)(2,1)S(1)}, bf16[4,24,384]{2,1,0:T(8,128)(2,1)S(1)}, u32[]{:S(2)}, u32[]{:S(2)}) collective-permute-start(bf16[4,24,384]{2,1,0:T(8,128)(2,1)S(1)} %add_convert_fusion.11), channel_id=1, source_target_pairs={{0,4},{1,5},{2,6},{3,7},{4,0},{5,1},{6,2},{7,3},{8,12},{9,13},{10,... | collective-permute-start | bytes 221192 | tf_op jit(solution)/shard_map/ppermute | solution.py:23
  139.9 12.6 %collective-permute-start.41 = (bf16[4,24,384]{2,1,0:T(8,128)(2,1)S(1)}, bf16[4,24,384]{2,1,0:T(8,128)(2,1)S(1)}, u32[]{:S(2)}, u32[]{:S(2)}) collective-permute-start(bf16[4,24,384]{2,1,0:T(8,128)(2,1)S(1)} %add_convert_fusion.12), channel_id=1, source_target_pairs={{0,4},{1,5},{2,6},{3,7},{4,0},{5,1},{6,2},{7,3},{8,12},{9,13},{10,... | collective-permute-start | bytes 221192 | tf_op jit(solution)/shard_map/ppermute | solution.py:23
  141.9 14.8 %collective-permute-start.49 = (bf16[1,96,768]{2,1,0:T(8,128)(2,1)S(1)}, bf16[1,96,768]{2,1,0:T(8,128)(2,1)S(1)}, u32[]{:S(2)}, u32[]{:S(2)}) collective-permute-start(bf16[1,96,768]{2,1,0:T(8,128)(2,1)S(1)} %fusion.27), channel_id=1, source_target_pairs={{0,4},{1,5},{2,6},{3,7},{4,0},{5,1},{6,2},{7,3},{8,12},{9,13},{10,... | collective-permute-start | bytes 442376 | tf_op jit(solution)/shard_map/ppermute | solution.py:23
  156.7 9.1 %collective-permute-start.60 = (bf16[4,24,768]{2,1,0:T(8,128)(2,1)S(1)}, bf16[4,24,768]{2,1,0:T(8,128)(2,1)S(1)}, u32[]{:S(2)}, u32[]{:S(2)}) collective-permute-start(bf16[4,24,768]{2,1,0:T(8,128)(2,1)S(1)} %pad_maximum_fusion.16), channel_id=1, source_target_pairs={{0,4},{1,5},{2,6},{3,7},{4,0},{5,1},{6,2},{7,3},{8,12},{9,13},{10,... | collective-permute-start | bytes 442376 | tf_op jit(solution)/shard_map/ppermute | solution.py:23
  156.9 15.7 %collective-permute-start.50 = (bf16[1,192,768]{2,1,0:T(8,128)(2,1)S(1)}, bf16[1,192,768]{2,1,0:T(8,128)(2,1)S(1)}, u32[]{:S(2)}, u32[]{:S(2)}) collective-permute-start(bf16[1,192,768]{2,1,0:T(8,128)(2,1)S(1)} %pad_maximum_fusion.8), channel_id=1, source_target_pairs={{0,2},{1,3},{2,0},{3,1},{4,6},{5,7},{6,4},{7,5},{8,10},{9,11},{10,... | collective-permute-start | bytes 884744 | tf_op jit(solution)/shard_map/ppermute | solution.py:23
  159.8 14.4 %collective-permute-start.47 = (bf16[128,384]{1,0:T(8,128)(2,1)S(1)}, bf16[128,384]{1,0:T(8,128)(2,1)S(1)}, u32[]{:S(2)}, u32[]{:S(2)}) collective-permute-start(bf16[128,384]{1,0:T(8,128)(2,1)S(1)} %pad_maximum_fusion.20), channel_id=1, source_target_pairs={{0,4},{1,5},{2,6},{3,7},{4,0},{5,1},{6,2},{7,3},{8,12},{9,13},{10,... | collective-permute-start | bytes 294920 | tf_op jit(solution)/shard_map/ppermute | solution.py:23
  160.2 14.0 %collective-permute-start.46 = (bf16[4,24,384]{2,1,0:T(8,128)(2,1)S(1)}, bf16[4,24,384]{2,1,0:T(8,128)(2,1)S(1)}, u32[]{:S(2)}, u32[]{:S(2)}) collective-permute-start(bf16[4,24,384]{2,1,0:T(8,128)(2,1)S(1)} %pad_maximum_fusion.21), channel_id=1, source_target_pairs={{0,4},{1,5},{2,6},{3,7},{4,0},{5,1},{6,2},{7,3},{8,12},{9,13},{10,... | collective-permute-start | bytes 221192 | tf_op jit(solution)/shard_map/ppermute | solution.py:23
  165.9 10.2 %collective-permute-start.61 = (bf16[4,48,768]{2,1,0:T(8,128)(2,1)S(1)}, bf16[4,48,768]{2,1,0:T(8,128)(2,1)S(1)}, u32[]{:S(2)}, u32[]{:S(2)}) collective-permute-start(bf16[4,48,768]{2,1,0:T(8,128)(2,1)S(1)} %pad_maximum_fusion.11), channel_id=1, source_target_pairs={{0,1},{1,0},{2,3},{3,2},{4,5},{5,4},{6,7},{7,6},{8,9},{9,8},{10,11... | collective-permute-start | bytes 884744 | tf_op jit(solution)/shard_map/ppermute | solution.py:23
  173.6 21.8 %collective-permute-start.55 = (bf16[1,384,768]{2,1,0:T(8,128)(2,1)}, bf16[1,384,768]{2,1,0:T(8,128)(2,1)S(1)}, u32[]{:S(2)}, u32[]{:S(2)}) collective-permute-start(bf16[1,384,768]{2,1,0:T(8,128)(2,1)} %get-tuple-element.190), channel_id=1, source_target_pairs={{0,1},{1,0},{2,3},{3,2},{4,5},{5,4},{6,7},{7,6},{8,9},{9,8},{10,11... | collective-permute-start | bytes 1769480 | tf_op jit(solution)/shard_map/ppermute | solution.py:23
  174.3 17.4 %collective-permute-start.51 = (bf16[4,48,384]{2,1,0:T(8,128)(2,1)S(1)}, bf16[4,48,384]{2,1,0:T(8,128)(2,1)S(1)}, u32[]{:S(2)}, u32[]{:S(2)}) collective-permute-start(bf16[4,48,384]{2,1,0:T(8,128)(2,1)S(1)} %pad_maximum_fusion.14), channel_id=1, source_target_pairs={{0,1},{1,0},{2,3},{3,2},{4,5},{5,4},{6,7},{7,6},{8,9},{9,8},{10,11... | collective-permute-start | bytes 442376 | tf_op jit(solution)/shard_map/ppermute | solution.py:23
  176.0 15.8 %collective-permute-start.53 = (bf16[224,384]{1,0:T(8,128)(2,1)S(1)}, bf16[224,384]{1,0:T(8,128)(2,1)S(1)}, u32[]{:S(2)}, u32[]{:S(2)}) collective-permute-start(bf16[224,384]{1,0:T(8,128)(2,1)S(1)} %pad_maximum_fusion.13), channel_id=1, source_target_pairs={{0,2},{1,3},{2,0},{3,1},{4,6},{5,7},{6,4},{7,5},{8,10},{9,11},{10,... | collective-permute-start | bytes 516104 | tf_op jit(solution)/shard_map/ppermute | solution.py:23
  176.2 21.2 %collective-permute-start.62 = (bf16[4,96,768]{2,1,0:T(8,128)(2,1)S(1)}, bf16[4,96,768]{2,1,0:T(8,128)(2,1)S(1)}, u32[]{:S(2)}, u32[]{:S(2)}) collective-permute-start(bf16[4,96,768]{2,1,0:T(8,128)(2,1)S(1)} %pad_maximum_fusion.6.held), channel_id=1, source_target_pairs={{0,2},{1,3},{2,0},{3,1},{4,6},{5,7},{6,4},{7,5},{8,10},{9,11},{10,... | collective-permute-start | bytes 1769480 | tf_op jit(solution)/shard_map/ppermute | solution.py:23
  192.7 8.4 %collective-permute-start.54 = (bf16[416,384]{1,0:T(8,128)(2,1)}, bf16[416,384]{1,0:T(8,128)(2,1)}, u32[]{:S(2)}, u32[]{:S(2)}) collective-permute-start(bf16[416,384]{1,0:T(8,128)(2,1)} %pad_maximum_fusion.7), channel_id=1, source_target_pairs={{0,1},{1,0},{2,3},{3,2},{4,5},{5,4},{6,7},{7,6},{8,9},{9,8},{10,11... | collective-permute-start | bytes 958472 | tf_op jit(solution)/shard_map/ppermute | solution.py:23
  193.3 7.4 %collective-permute-start.52 = (bf16[4,96,384]{2,1,0:T(8,128)(2,1)S(1)}, bf16[4,96,384]{2,1,0:T(8,128)(2,1)}, u32[]{:S(2)}, u32[]{:S(2)}) collective-permute-start(bf16[4,96,384]{2,1,0:T(8,128)(2,1)S(1)} %pad_maximum_fusion.9.held_one), channel_id=1, source_target_pairs={{0,2},{1,3},{2,0},{3,1},{4,6},{5,7},{6,4},{7,5},{8,10},{9,11},{10,... | collective-permute-start | bytes 884744 | tf_op jit(solution)/shard_map/ppermute | solution.py:23
  (63 other events, 304.1 us)

commit v5 on v4

--- a/solution.py
+++ b/solution.py
@@ -177,7 +177,7 @@
         out[pl.ds(pl.multiple_of((1 - mine) * rows, rows), rows), where] = got[k].astype(F32)
 
 
-def join_tail_kernel(index, held_one, got_one, held_two, got_two, vecs, out, qkv, sums):
+def join_tail_kernel(index, held_one, got_one, held_two, got_two, vecs, out, qkv, ups, qvs, *six):
     rows, part = held_one.shape[1], held_one.shape[2] // 2
 
     def in_order(pieces):
@@ -207,7 +207,25 @@
                 qkv[where, (j * G + i) * part : (j * G + i + 1) * part] = piece[
                     :, j * part : (j + 1) * part
                 ]
-    sums[...] = vecs[...] + got_two[G * held_two.shape[1] :, :].astype(F32)
+    sums = vecs[...] + got_two[G * held_two.shape[1] :, :].astype(F32)
+    half = 2 * part
+
+    def own(pieces):
+        value = pieces[0]
+        for i in range(1, G):
+            value = jnp.where(index[0] == i, pieces[i], value)
+        return value
+
+    def line(row, start, size):
+        at = 2 * row + start // half
+        return sums[at : at + 1, start % half : start % half + size]
+
+    for j in range(6):
+        six[j][...] = own([line(j, i * part, part) for i in range(G)]).reshape(part)
+    whole = [jnp.concatenate([line(6 + i, 0, half), line(6 + i, half, half)], axis=1) for i in range(G)]
+    ups[...] = own(whole).reshape(2 * half)
+    row = 6 + G
+    qvs[...] = own([line(row + 2 * (i // 2), (i % 2) * half, half) for i in range(G)]).reshape(half)
 
 
 def hidden_kernel(index, own, near, far, last, up, bias, down, act, slope, *outs):
@@ -563,21 +581,18 @@
         [index, up.value, after(up_got, one.value)],
     )
     one_got, two_got = after((one_got, two_got), grad_down, grad_up, grad_tokens)
-    grad_out, grad_qkv, vecs = call(
+    grad_out, grad_qkv, vec_up, vec_qv, *six = call(
         join_tail_kernel,
         [
             jax.ShapeDtypeStruct((part, width), F32),
             jax.ShapeDtypeStruct((part, 3 * width), F32),
-            jax.ShapeDtypeStruct((2 * VECS, 2 * part), F32),
-        ],
+            jax.ShapeDtypeStruct((hidden,), F32),
+            jax.ShapeDtypeStruct((2 * part,), F32),
+        ]
+        + [jax.ShapeDtypeStruct((part,), F32)] * 6,
         [index, one.value, one_got, two.value, two_got, two.vecs],
     )
-    vecs = vecs.reshape(VECS, width)
-
-    six = lax.dynamic_slice_in_dim(vecs[:6], place * part, part, 1)
-    vec_up = lax.dynamic_slice_in_dim(vecs[6 : 6 + G].reshape(-1), place * hidden, hidden, 0)
-    qvs = jnp.concatenate([vecs[6 + G], vecs[8 + G]])
-    vec_qv = lax.dynamic_slice_in_dim(qvs, place * 2 * part, 2 * part, 0)
+
     return (
         output[None],
         grad_tokens[None],

time: 207 us -> 202 us (0.976)
  other arithmetic: 32 us -> 28.4 us
  transfers between devices with their start and end apart: 63 -> 63, of which waited for: 25 -> 25; matrix products, arithmetic and copies ran while one was open for 22% -> 21% of each run, Pallas kernels for 6% -> 6%
where the time goes in v5:
time: 202 us; the launch traced here: 201 us
  waiting for transfers between devices  78.2 us (39%)
  starting transfers between devices  47.5 us (24%)
  other arithmetic  28.4 us (14%)
  Pallas kernels  18.3 us (9%)
  local copies, waits for them, and re-layouts  17.2 us (9%)
  matrix products  9.5 us (5%)
    ppermute x24, waiting for transfers between devices, rx(): return lax.ppermute(value, 'replica', [(i, i ^ bits) for i in range(count)])  41.3 us
    ppermute x39, waiting for transfers between devices, gx(): return lax.ppermute(value, 'group', [(i, i ^ bits) for i in range(G)])  36.9 us
    ppermute x24, starting transfers between devices, rx(): return lax.ppermute(value, 'replica', [(i, i ^ bits) for i in range(count)])  28.4 us
    ppermute x39, starting transfers between devices, gx(): return lax.ppermute(value, 'group', [(i, i ^ bits) for i in range(G)])  19.1 us
    pallas_call x8, Pallas kernels, call(): pl.pallas_call(kernel, out_shape=outs, in_specs=[index_spec()] + [whole_s...  18.3 us
    convert_element_type x8, other arithmetic, send(): self.sent = self.total(1 - self.mine).astype(BF)  8.34 us
    unnamed x96, local copies, waits for them, and re-layouts  6.85 us
    concatenate x1, local copies, waits for them, and re-layouts, on_device(): small = jnp.concatenate(smalls).reshape(1, -1)  4.83 us
  transfers between devices with their start and end apart: 63, of which 25 were waited for; matrix products, arithmetic and copies ran while one was open for 21% of the time, Pallas kernels for 6%

profile of v5, /device:TPU:0, one launch (start us, length us, event | category | flops | bytes accessed | tf_op | source)
XLA Modules:
  0.0 201.1 jit_solution(4243755686161272067)
XLA Ops:
  1.2 2.6 %collective-permute-start.1 = (bf16[128,768]{1,0:T(8,128)(2,1)}, bf16[128,768]{1,0:T(8,128)(2,1)}, u32[]{:S(2)}, u32[]{:S(2)}) collective-permute-start(bf16[128,768]{1,0:T(8,128)(2,1)} %bitcast.109), channel_id=1, source_target_pairs={{0,16},{8,24},{16,0},{24,8},{1,17},{9,25},{17,1},{25,9},{2,18},{10... | collective-permute-start | bytes 589832 | tf_op jit(solution)/shard_map/ppermute | solution.py:19
  6.0 2.0 collective-permute-start.4
  9.8 4.8 %concatenate.78 = bf16[1536]{0:T(1024)(128)(2,1)S(1)} concatenate(bf16[384]{0:T(512)(128)(2,1)} %param.19, bf16[192]{0:T(256)(128)(2,1)} %param.21, bf16[192]{0:T(256)(128)(2,1)} %param.22, bf16[192]{0:T(256)(128)(2,1)} %param.23, bf16[192]{0:T(256)(128)(2,1)} %param.27, bf16[192]{0:T(256)(128)(2,1)} %param.28, bf16[192]{0:T(256)(128)(2,1)} %param.29), dimensions={0} | concatenate | bytes 6144 | tf_op jit(solution)/shard_map/concatenate | solution.py:375
  14.7 2.0 collective-permute-start.6
  16.9 2.3 %constant_dynamic-slice_fusion.3 = (bf16[192,768]{1,0:T(8,128)(2,1)}, bf16[192,768]{1,0:T(8,128)(2,1)}, bf16[192,768]{1,0:T(8,128)(2,1)}, bf16[192,768]{1,0:T(8,128)(2,1)}) fusion(bf16[192,3072]{1,0:T(8,128)(2,1)} %param.24, s32[]{:T(128)S(6)} %select_n.351, s32[]{:T(128)S(6)} %select_n.350, s32[]{:T(128)S(6)} %select_n.349, s32[]{:T(128)S(6)} %select_n.348), kind=kLoop, calls=%fused_computation.171 | loop fusion | bytes 2359312 | tf_op jit(solution)/shard_map/dynamic_slice | solution.py:384
  23.2 1.7 fusion
  25.3 1.3 fusion.68
  27.6 1.4 fusion.2
  29.0 1.5 convolution_convert_fusion.3
  32.2 2.2 %collective-permute-done.11 = bf16[192,768]{1,0:T(8,128)(2,1)} collective-permute-done((bf16[192,768]{1,0:T(8,128)(2,1)}, bf16[192,768]{1,0:T(8,128)(2,1)}, u32[]{:S(2)}, u32[]{:S(2)}) %collective-permute-start.11) | collective-permute-done | bytes 294944 | tf_op jit(solution)/shard_map/ppermute | solution.py:19
  40.5 4.5 %collective-permute-done.14 = bf16[128,768]{1,0:T(8,128)(2,1)S(1)} collective-permute-done((bf16[128,768]{1,0:T(8,128)(2,1)S(1)}, bf16[128,768]{1,0:T(8,128)(2,1)S(1)}, u32[]{:S(2)}, u32[]{:S(2)}) %collective-permute-start.14) | collective-permute-done | bytes 196640 | tf_op jit(solution)/shard_map/ppermute | solution.py:19
  46.9 6.1 %collective-permute-done.16.far = bf16[128,768]{1,0:T(8,128)(2,1)S(1)} collective-permute-done((bf16[128,768]{1,0:T(8,128)(2,1)S(1)}, bf16[128,768]{1,0:T(8,128)(2,1)S(1)}, u32[]{:S(2)}, u32[]{:S(2)}) %collective-permute-start.16) | collective-permute-done | bytes 196640 | tf_op jit(solution)/shard_map/ppermute | solution.py:19
  53.1 1.4 collective-permute-done.17.last
  54.5 3.2 %shard_map.255 = (bf16[512,768]{1,0:T(8,128)(2,1)S(1)}, f32[512,768]{1,0:T(8,128)}, f32[128,768]{1,0:T(8,128)S(1)}, bf16[128,768]{1,0:T(8,128)(2,1)S(1)}, f32[12...) custom-call(s32[3]{0:T(128)S(1)} %pad_add_fusion.1.index, bf16[128,768]{1,0:T(8,128)(2,1)S(1)} %fusion.24.own, ...), custom_call_target="tpu_custom_call" | custom-call | tf_op jit(solution)/shard_map/pallas_call | solution.py:140
  64.0 6.7 %collective-permute-done.20 = bf16[128,768]{1,0:T(8,128)(2,1)S(1)} collective-permute-done((bf16[128,768]{1,0:T(8,128)(2,1)S(1)}, bf16[128,768]{1,0:T(8,128)(2,1)S(1)}, u32[]{:S(2)}, u32[]{:S(2)}) %collective-permute-start.20) | collective-permute-done | bytes 196640 | tf_op jit(solution)/shard_map/ppermute | solution.py:19
  70.6 1.5 fusion.62
  73.1 5.8 %collective-permute-done.22 = bf16[128,768]{1,0:T(8,128)(2,1)S(1)} collective-permute-done((bf16[128,768]{1,0:T(8,128)(2,1)S(1)}, bf16[128,768]{1,0:T(8,128)(2,1)S(1)}, u32[]{:S(2)}, u32[]{:S(2)}) %collective-permute-start.22) | collective-permute-done | bytes 196640 | tf_op jit(solution)/shard_map/ppermute | solution.py:19
  79.0 1.4 collective-permute-done.23
  84.0 1.6 collective-permute-start.30
  87.4 1.6 collective-permute-start.31
  89.0 3.4 %collective-permute-done.26 = bf16[128,768]{1,0:T(8,128)(2,1)S(1)} collective-permute-done((bf16[128,768]{1,0:T(8,128)(2,1)S(1)}, bf16[128,768]{1,0:T(8,128)(2,1)S(1)}, u32[]{:S(2)}, u32[]{:S(2)}) %collective-permute-start.26) | collective-permute-done | bytes 196640 | tf_op jit(solution)/shard_map/ppermute | solution.py:19
  96.2 3.3 %collective-permute-done.30 = bf16[1,384,768]{2,1,0:T(8,128)(2,1)S(1)} collective-permute-done((bf16[1,384,768]{2,1,0:T(8,128)(2,1)S(1)}, bf16[1,384,768]{2,1,0:T(8,128)(2,1)S(1)}, u32[]{:S(2)}, u32[]{:S(2)}) %collective-permute-start.30) | collective-permute-done | bytes 589856 | tf_op jit(solution)/shard_map/ppermute | solution.py:23
  101.0 1.6 collective-permute-start.36
  104.5 4.7 %shard_map.256 = (bf16[384,512]{1,0:T(8,128)(2,1)S(1)}, bf16[192,512]{1,0:T(8,128)(2,1)S(1)}, bf16[4,192,384]{2,1,0:T(8,128)(2,1)S(1)}, bf16[4,192,384]{2,1,0:T(...) custom-call(s32[3]{0:T(128)S(1)} %pad_add_fusion.1.index, ...), custom_call_target="tpu_custom_call" | custom-call | tf_op jit(solution)/shard_map/pallas_call | solution.py:140
  110.0 1.6 collective-permute-start.34
  112.3 1.8 fusion.29
  114.1 1.8 add_convert_fusion.8
  115.9 2.6 %collective-permute-start.56 = (bf16[4,24,768]{2,1,0:T(8,128)(2,1)}, bf16[4,24,768]{2,1,0:T(8,128)(2,1)S(1)}, u32[]{:S(2)}, u32[]{:S(2)}) collective-permute-start(bf16[4,24,768]{2,1,0:T(8,128)(2,1)} %add_convert_fusion.8), channel_id=1, source_target_pairs={{0,4},{1,5},{2,6},{3,7},{4,0},{5,1},{6,2},{7,3},{8,12},{9,13},{10,... | collective-permute-start | bytes 442376 | tf_op jit(solution)/shard_map/ppermute | solution.py:23
  118.5 2.2 %collective-permute-done.34 = bf16[4,96,384]{2,1,0:T(8,128)(2,1)} collective-permute-done((bf16[4,96,384]{2,1,0:T(8,128)(2,1)}, bf16[4,96,384]{2,1,0:T(8,128)(2,1)}, u32[]{:S(2)}, u32[]{:S(2)}) %collective-permute-start.34) | collective-permute-done | bytes 294944 | tf_op jit(solution)/shard_map/ppermute | solution.py:23
  123.4 2.4 %shard_map.257 = (bf16[128,768]{1,0:T(8,128)(2,1)}, bf16[144,768]{1,0:T(8,128)(2,1)S(1)}, f32[128,768]{1,0:T(8,128)S(1)}, f32[128,768]{1,0:T(8,128)S(1)}, f32[16,768]{1,0:T(8,128)S(1)}) custom-call(s32[3]{0:T(128)S(1)} %pad_add_fusion.1.index, bf16[384,512]{1,0:T(8,128)(2,1)S(1)} %get-tuple-element.116.d_qk, bf16[192,512]{1,0:T(8,128)(2,1)S(1)} %get-tuple-element.117.d_v, ...), custom_call_target="tpu_custom_call" | custom-call | tf_op jit(solution)/shard_map/pallas_call | solution.py:140
  126.3 2.4 %collective-permute-start.48 = (bf16[1,96,768]{2,1,0:T(8,128)(2,1)S(1)}, bf16[1,96,768]{2,1,0:T(8,128)(2,1)S(1)}, u32[]{:S(2)}, u32[]{:S(2)}) collective-permute-start(bf16[1,96,768]{2,1,0:T(8,128)(2,1)S(1)} %copy-done.45), channel_id=1, source_target_pairs={{0,4},{1,5},{2,6},{3,7},{4,0},{5,1},{6,2},{7,3},{8,12},{9,13},{10,... | collective-permute-start | bytes 442376 | tf_op jit(solution)/shard_map/ppermute | solution.py:23
  134.4 1.8 collective-permute-done.48
  138.6 2.3 %collective-permute-start.41 = (bf16[4,24,384]{2,1,0:T(8,128)(2,1)S(1)}, bf16[4,24,384]{2,1,0:T(8,128)(2,1)S(1)}, u32[]{:S(2)}, u32[]{:S(2)}) collective-permute-start(bf16[4,24,384]{2,1,0:T(8,128)(2,1)S(1)} %add_convert_fusion.12), channel_id=1, source_target_pairs={{0,4},{1,5},{2,6},{3,7},{4,0},{5,1},{6,2},{7,3},{8,12},{9,13},{10,... | collective-permute-start | bytes 221192 | tf_op jit(solution)/shard_map/ppermute | solution.py:23
  141.5 8.5 %collective-permute-done.42 = bf16[4,24,384]{2,1,0:T(8,128)(2,1)S(1)} collective-permute-done((bf16[4,24,384]{2,1,0:T(8,128)(2,1)S(1)}, bf16[4,24,384]{2,1,0:T(8,128)(2,1)S(1)}, u32[]{:S(2)}, u32[]{:S(2)}) %collective-permute-start.42) | collective-permute-done | bytes 73760 | tf_op jit(solution)/shard_map/ppermute | solution.py:23
  150.0 1.6 collective-permute-done.41
  153.9 1.4 collective-permute-start.44
  155.9 1.7 collective-permute-start.50
  159.3 2.7 %collective-permute-start.46 = (bf16[4,24,384]{2,1,0:T(8,128)(2,1)S(1)}, bf16[4,24,384]{2,1,0:T(8,128)(2,1)S(1)}, u32[]{:S(2)}, u32[]{:S(2)}) collective-permute-start(bf16[4,24,384]{2,1,0:T(8,128)(2,1)S(1)} %pad_maximum_fusion.21), channel_id=1, source_target_pairs={{0,4},{1,5},{2,6},{3,7},{4,0},{5,1},{6,2},{7,3},{8,12},{9,13},{10,... | collective-permute-start | bytes 221192 | tf_op jit(solution)/shard_map/ppermute | solution.py:23
  161.9 2.7 %collective-permute-done.60 = bf16[4,24,768]{2,1,0:T(8,128)(2,1)S(1)} collective-permute-done((bf16[4,24,768]{2,1,0:T(8,128)(2,1)S(1)}, bf16[4,24,768]{2,1,0:T(8,128)(2,1)S(1)}, u32[]{:S(2)}, u32[]{:S(2)}) %collective-permute-start.60) | collective-permute-done | bytes 147488 | tf_op jit(solution)/shard_map/ppermute | solution.py:23
  165.3 6.8 %collective-permute-done.50 = bf16[1,192,768]{2,1,0:T(8,128)(2,1)S(1)} collective-permute-done((bf16[1,192,768]{2,1,0:T(8,128)(2,1)S(1)}, bf16[1,192,768]{2,1,0:T(8,128)(2,1)S(1)}, u32[]{:S(2)}, u32[]{:S(2)}) %collective-permute-start.50) | collective-permute-done | bytes 294944 | tf_op jit(solution)/shard_map/ppermute | solution.py:23
  173.1 1.5 collective-permute-start.51
  175.0 2.1 %collective-permute-start.62 = (bf16[4,96,768]{2,1,0:T(8,128)(2,1)S(1)}, bf16[4,96,768]{2,1,0:T(8,128)(2,1)S(1)}, u32[]{:S(2)}, u32[]{:S(2)}) collective-permute-start(bf16[4,96,768]{2,1,0:T(8,128)(2,1)S(1)} %pad_maximum_fusion.6.held), channel_id=1, source_target_pairs={{0,2},{1,3},{2,0},{3,1},{4,6},{5,7},{6,4},{7,5},{8,10},{9,11},{10,... | collective-permute-start | bytes 1769480 | tf_op jit(solution)/shard_map/ppermute | solution.py:23
  177.1 12.7 %collective-permute-done.51 = bf16[4,48,384]{2,1,0:T(8,128)(2,1)S(1)} collective-permute-done((bf16[4,48,384]{2,1,0:T(8,128)(2,1)S(1)}, bf16[4,48,384]{2,1,0:T(8,128)(2,1)S(1)}, u32[]{:S(2)}, u32[]{:S(2)}) %collective-permute-start.51) | collective-permute-done | bytes 147488 | tf_op jit(solution)/shard_map/ppermute | solution.py:23
  190.9 1.7 add_convert_fusion.1
  192.6 2.1 %shard_map.259 = f32[768,768]{1,0:T(8,128)} custom-call(s32[3]{0:T(128)S(1)} %pad_add_fusion.1.index, bf16[384,768]{1,0:T(8,128)(2,1)S(1)} %get-tuple-element.203.held, bf16[384,768]{1,0:T(8,128)(2,1)S(1)} %bitcast.101), custom_call_target="tpu_custom_call" | custom-call | tf_op jit(solution)/shard_map/pallas_call | solution.py:140
  194.7 2.1 %shard_map.260 = f32[192,3072]{1,0:T(8,128)} custom-call(s32[3]{0:T(128)S(1)} %pad_add_fusion.1.index, bf16[4,96,768]{2,1,0:T(8,128)(2,1)S(1)} %pad_maximum_fusion.6.held, bf16[4,96,768]{2,1,0:T(8,128)(2,1)S(1)} %collective-permute-done.62.got), custom_call_target="tpu_custom_call" | custom-call | tf_op jit(solution)/shard_map/pallas_call | solution.py:140
  196.8 1.8 collective-permute-done.52.got_one
  198.6 2.5 %shard_map.261 = (f32[192,768]{1,0:T(8,128)}, f32[192,2304]{1,0:T(8,128)}, f32[768]{0:T(1024)}, f32[384]{0:T(512)}, f32[192]{0:T(256)}, /*index=5*/f32[192]{0:T(...) custom-call(s32[3]{0:T(128)S(1)} %pad_add_fusion.1.index, bf16[4,96,384]{2,1,0:T(8,128)(2,1)S(1)} %pad_maximum_fusion.9.held_one, ...), custom_call_target="tpu_custom_call" | custom-call | tf_op jit(solution)/shard_map/pallas_call | solution.py:140
  (313 shorter events, 60.2 us)
Async XLA Ops:
  0.6 9.2 %collective-permute-start = (bf16[128,768]{1,0:T(8,128)(2,1)}, bf16[128,768]{1,0:T(8,128)(2,1)S(1)}, u32[]{:S(2)}, u32[]{:S(2)}) collective-permute-start(bf16[128,768]{1,0:T(8,128)(2,1)} %bitcast.108), channel_id=1, source_target_pairs={{0,8},{8,0},{16,24},{24,16},{1,9},{9,1},{17,25},{25,17},{2,10},{10... | collective-permute-start | bytes 589832 | tf_op jit(solution)/shard_map/ppermute | solution.py:19
  1.2 8.6 %collective-permute-start.1 = (bf16[128,768]{1,0:T(8,128)(2,1)}, bf16[128,768]{1,0:T(8,128)(2,1)}, u32[]{:S(2)}, u32[]{:S(2)}) collective-permute-start(bf16[128,768]{1,0:T(8,128)(2,1)} %bitcast.109), channel_id=1, source_target_pairs={{0,16},{8,24},{16,0},{24,8},{1,17},{9,25},{17,1},{25,9},{2,18},{10... | collective-permute-start | bytes 589832 | tf_op jit(solution)/shard_map/ppermute | solution.py:19
  6.0 13.1 %collective-permute-start.3 = (bf16[192,576]{1,0:T(8,128)(2,1)S(1)}, bf16[192,576]{1,0:T(8,128)(2,1)S(1)}, u32[]{:S(2)}, u32[]{:S(2)}) collective-permute-start(bf16[192,576]{1,0:T(8,128)(2,1)S(1)} %get-tuple-element.87), channel_id=1, source_target_pairs={{0,24},{8,16},{16,8},{24,0},{1,25},{9,17},{17,9},{25,1},{2,26},{10... | collective-permute-start | bytes 663560 | tf_op jit(solution)/shard_map/ppermute | solution.py:19
  6.0 14.0 %collective-permute-start.4 = (bf16[192,576]{1,0:T(8,128)(2,1)S(1)}, bf16[192,576]{1,0:T(8,128)(2,1)S(1)}, u32[]{:S(2)}, u32[]{:S(2)}) collective-permute-start(bf16[192,576]{1,0:T(8,128)(2,1)S(1)} %get-tuple-element.88), channel_id=1, source_target_pairs={{0,16},{8,24},{16,0},{24,8},{1,17},{9,25},{17,1},{25,9},{2,18},{10... | collective-permute-start | bytes 663560 | tf_op jit(solution)/shard_map/ppermute | solution.py:19
  9.8 13.4 %collective-permute-start.2 = (bf16[128,768]{1,0:T(8,128)(2,1)}, bf16[128,768]{1,0:T(8,128)(2,1)}, u32[]{:S(2)}, u32[]{:S(2)}) collective-permute-start(bf16[128,768]{1,0:T(8,128)(2,1)} %collective-permute-done.1), channel_id=1, source_target_pairs={{0,8},{8,0},{16,24},{24,16},{1,9},{9,1},{17,25},{25,17},{2,10},{10... | collective-permute-start | bytes 589832 | tf_op jit(solution)/shard_map/ppermute | solution.py:19
  14.7 6.5 %collective-permute-start.6 = (bf16[1,1536]{1,0:T(2,128)(2,1)S(1)}, bf16[1,1536]{1,0:T(2,128)(2,1)S(1)}, u32[]{:S(2)}, u32[]{:S(2)}) collective-permute-start(bf16[1,1536]{1,0:T(2,128)(2,1)S(1)} %reshape.205), channel_id=1, source_target_pairs={{0,16},{8,24},{16,0},{24,8},{1,17},{9,25},{17,1},{25,9},{2,18},{10... | collective-permute-start | bytes 9224 | tf_op jit(solution)/shard_map/ppermute | solution.py:19
  19.1 13.1 %collective-permute-start.10 = (bf16[192,768]{1,0:T(8,128)(2,1)}, bf16[192,768]{1,0:T(8,128)(2,1)}, u32[]{:S(2)}, u32[]{:S(2)}) collective-permute-start(bf16[192,768]{1,0:T(8,128)(2,1)} %get-tuple-element.190), channel_id=1, source_target_pairs={{0,16},{8,24},{16,0},{24,8},{1,17},{9,25},{17,1},{25,9},{2,18},{10... | collective-permute-start | bytes 884744 | tf_op jit(solution)/shard_map/ppermute | solution.py:19
  20.0 14.4 %collective-permute-start.11 = (bf16[192,768]{1,0:T(8,128)(2,1)}, bf16[192,768]{1,0:T(8,128)(2,1)}, u32[]{:S(2)}, u32[]{:S(2)}) collective-permute-start(bf16[192,768]{1,0:T(8,128)(2,1)} %get-tuple-element.189), channel_id=1, source_target_pairs={{0,24},{8,16},{16,8},{24,0},{1,25},{9,17},{17,9},{25,1},{2,26},{10... | collective-permute-start | bytes 884744 | tf_op jit(solution)/shard_map/ppermute | solution.py:19
  22.2 12.2 %collective-permute-start.9 = (bf16[192,768]{1,0:T(8,128)(2,1)}, bf16[192,768]{1,0:T(8,128)(2,1)}, u32[]{:S(2)}, u32[]{:S(2)}) collective-permute-start(bf16[192,768]{1,0:T(8,128)(2,1)} %get-tuple-element.191), channel_id=1, source_target_pairs={{0,8},{8,0},{16,24},{24,16},{1,9},{9,1},{17,25},{25,17},{2,10},{10... | collective-permute-start | bytes 884744 | tf_op jit(solution)/shard_map/ppermute | solution.py:19
  37.8 7.2 %collective-permute-start.14 = (bf16[128,768]{1,0:T(8,128)(2,1)S(1)}, bf16[128,768]{1,0:T(8,128)(2,1)S(1)}, u32[]{:S(2)}, u32[]{:S(2)}) collective-permute-start(bf16[128,768]{1,0:T(8,128)(2,1)S(1)} %add_convert_fusion.4), channel_id=1, source_target_pairs={{0,16},{8,24},{16,0},{24,8},{1,17},{9,25},{17,1},{25,9},{2,18},{10... | collective-permute-start | bytes 589832 | tf_op jit(solution)/shard_map/ppermute | solution.py:19
  46.6 6.4 %collective-permute-start.16 = (bf16[128,768]{1,0:T(8,128)(2,1)S(1)}, bf16[128,768]{1,0:T(8,128)(2,1)S(1)}, u32[]{:S(2)}, u32[]{:S(2)}) collective-permute-start(bf16[128,768]{1,0:T(8,128)(2,1)S(1)} %fusion.24.own), channel_id=1, source_target_pairs={{0,16},{8,24},{16,0},{24,8},{1,17},{9,25},{17,1},{25,9},{2,18},{10... | collective-permute-start | bytes 589832 | tf_op jit(solution)/shard_map/ppermute | solution.py:19
  46.9 6.1 %collective-permute-start.15 = (bf16[128,768]{1,0:T(8,128)(2,1)S(1)}, bf16[128,768]{1,0:T(8,128)(2,1)S(1)}, u32[]{:S(2)}, u32[]{:S(2)}) collective-permute-start(bf16[128,768]{1,0:T(8,128)(2,1)S(1)} %fusion.24.own), channel_id=1, source_target_pairs={{0,8},{8,0},{16,24},{24,16},{1,9},{9,1},{17,25},{25,17},{2,10},{10... | collective-permute-start | bytes 589832 | tf_op jit(solution)/shard_map/ppermute | solution.py:19
  63.6 7.0 %collective-permute-start.20 = (bf16[128,768]{1,0:T(8,128)(2,1)S(1)}, bf16[128,768]{1,0:T(8,128)(2,1)S(1)}, u32[]{:S(2)}, u32[]{:S(2)}) collective-permute-start(bf16[128,768]{1,0:T(8,128)(2,1)S(1)} %add_convert_fusion.3), channel_id=1, source_target_pairs={{0,16},{8,24},{16,0},{24,8},{1,17},{9,25},{17,1},{25,9},{2,18},{10... | collective-permute-start | bytes 589832 | tf_op jit(solution)/shard_map/ppermute | solution.py:19
  72.8 6.2 %collective-permute-start.22 = (bf16[128,768]{1,0:T(8,128)(2,1)S(1)}, bf16[128,768]{1,0:T(8,128)(2,1)S(1)}, u32[]{:S(2)}, u32[]{:S(2)}) collective-permute-start(bf16[128,768]{1,0:T(8,128)(2,1)S(1)} %get-tuple-element.176), channel_id=1, source_target_pairs={{0,16},{8,24},{16,0},{24,8},{1,17},{9,25},{17,1},{25,9},{2,18},{10... | collective-permute-start | bytes 589832 | tf_op jit(solution)/shard_map/ppermute | solution.py:19
  73.1 5.8 %collective-permute-start.21 = (bf16[128,768]{1,0:T(8,128)(2,1)S(1)}, bf16[128,768]{1,0:T(8,128)(2,1)S(1)}, u32[]{:S(2)}, u32[]{:S(2)}) collective-permute-start(bf16[128,768]{1,0:T(8,128)(2,1)S(1)} %get-tuple-element.176), channel_id=1, source_target_pairs={{0,8},{8,0},{16,24},{24,16},{1,9},{9,1},{17,25},{25,17},{2,10},{10... | collective-permute-start | bytes 589832 | tf_op jit(solution)/shard_map/ppermute | solution.py:19
  82.7 6.3 %collective-permute-start.24 = (bf16[128,768]{1,0:T(8,128)(2,1)S(1)}, bf16[128,768]{1,0:T(8,128)(2,1)S(1)}, u32[]{:S(2)}, u32[]{:S(2)}) collective-permute-start(bf16[128,768]{1,0:T(8,128)(2,1)S(1)} %get-tuple-element.197), channel_id=1, source_target_pairs={{0,8},{8,0},{16,24},{24,16},{1,9},{9,1},{17,25},{25,17},{2,10},{10... | collective-permute-start | bytes 589832 | tf_op jit(solution)/shard_map/ppermute | solution.py:19
  84.0 15.4 %collective-permute-start.30 = (bf16[1,384,768]{2,1,0:T(8,128)(2,1)S(1)}, bf16[1,384,768]{2,1,0:T(8,128)(2,1)S(1)}, u32[]{:S(2)}, u32[]{:S(2)}) collective-permute-start(bf16[1,384,768]{2,1,0:T(8,128)(2,1)S(1)} %dynamic-slice_bitcast_fusion), channel_id=1, source_target_pairs={{0,1},{1,0},{2,3},{3,2},{4,5},{5,4},{6,7},{7,6},{8,9},{9,8},{10,11... | collective-permute-start | bytes 1769480 | tf_op jit(solution)/shard_map/ppermute | solution.py:23
  85.7 6.7 %collective-permute-start.26 = (bf16[128,768]{1,0:T(8,128)(2,1)S(1)}, bf16[128,768]{1,0:T(8,128)(2,1)S(1)}, u32[]{:S(2)}, u32[]{:S(2)}) collective-permute-start(bf16[128,768]{1,0:T(8,128)(2,1)S(1)} %fusion.21), channel_id=1, source_target_pairs={{0,16},{8,24},{16,0},{24,8},{1,17},{9,25},{17,1},{25,9},{2,18},{10... | collective-permute-start | bytes 589832 | tf_op jit(solution)/shard_map/ppermute | solution.py:19
  87.4 15.2 %collective-permute-start.31 = (bf16[4,96,768]{2,1,0:T(8,128)(2,1)S(1)}, bf16[4,96,768]{2,1,0:T(8,128)(2,1)S(1)}, u32[]{:S(2)}, u32[]{:S(2)}) collective-permute-start(bf16[4,96,768]{2,1,0:T(8,128)(2,1)S(1)} %constant_dynamic-slice_fusion.2), channel_id=1, source_target_pairs={{0,2},{1,3},{2,0},{3,1},{4,6},{5,7},{6,4},{7,5},{8,10},{9,11},{10,... | collective-permute-start | bytes 1769480 | tf_op jit(solution)/shard_map/ppermute | solution.py:23
  94.4 5.8 %collective-permute-start.28 = (bf16[128,768]{1,0:T(8,128)(2,1)S(1)}, bf16[128,768]{1,0:T(8,128)(2,1)S(1)}, u32[]{:S(2)}, u32[]{:S(2)}) collective-permute-start(bf16[128,768]{1,0:T(8,128)(2,1)S(1)} %get-tuple-element.178), channel_id=1, source_target_pairs={{0,16},{8,24},{16,0},{24,8},{1,17},{9,25},{17,1},{25,9},{2,18},{10... | collective-permute-start | bytes 589832 | tf_op jit(solution)/shard_map/ppermute | solution.py:19
  96.1 8.3 %collective-permute-start.27 = (bf16[128,768]{1,0:T(8,128)(2,1)S(1)}, bf16[128,768]{1,0:T(8,128)(2,1)S(1)}, u32[]{:S(2)}, u32[]{:S(2)}) collective-permute-start(bf16[128,768]{1,0:T(8,128)(2,1)S(1)} %get-tuple-element.178), channel_id=1, source_target_pairs={{0,8},{8,0},{16,24},{24,16},{1,9},{9,1},{17,25},{25,17},{2,10},{10... | collective-permute-start | bytes 589832 | tf_op jit(solution)/shard_map/ppermute | solution.py:19
  101.0 11.3 %collective-permute-start.36 = (bf16[1,192,768]{2,1,0:T(8,128)(2,1)}, bf16[1,192,768]{2,1,0:T(8,128)(2,1)}, u32[]{:S(2)}, u32[]{:S(2)}) collective-permute-start(bf16[1,192,768]{2,1,0:T(8,128)(2,1)} %fusion.11), channel_id=1, source_target_pairs={{0,2},{1,3},{2,0},{3,1},{4,6},{5,7},{6,4},{7,5},{8,10},{9,11},{10,... | collective-permute-start | bytes 884744 | tf_op jit(solution)/shard_map/ppermute | solution.py:23
  103.5 10.6 %collective-permute-start.37 = (bf16[4,48,768]{2,1,0:T(8,128)(2,1)}, bf16[4,48,768]{2,1,0:T(8,128)(2,1)}, u32[]{:S(2)}, u32[]{:S(2)}) collective-permute-start(bf16[4,48,768]{2,1,0:T(8,128)(2,1)} %add_convert_fusion), channel_id=1, source_target_pairs={{0,1},{1,0},{2,3},{3,2},{4,5},{5,4},{6,7},{7,6},{8,9},{9,8},{10,11... | collective-permute-start | bytes 884744 | tf_op jit(solution)/shard_map/ppermute | solution.py:23
  110.0 10.6 %collective-permute-start.34 = (bf16[4,96,384]{2,1,0:T(8,128)(2,1)}, bf16[4,96,384]{2,1,0:T(8,128)(2,1)}, u32[]{:S(2)}, u32[]{:S(2)}) collective-permute-start(bf16[4,96,384]{2,1,0:T(8,128)(2,1)} %get-tuple-element.124), channel_id=1, source_target_pairs={{0,2},{1,3},{2,0},{3,1},{4,6},{5,7},{6,4},{7,5},{8,10},{9,11},{10,... | collective-permute-start | bytes 884744 | tf_op jit(solution)/shard_map/ppermute | solution.py:23
  111.6 9.1 %collective-permute-start.35 = (bf16[4,96,384]{2,1,0:T(8,128)(2,1)S(1)}, bf16[4,96,384]{2,1,0:T(8,128)(2,1)S(1)}, u32[]{:S(2)}, u32[]{:S(2)}) collective-permute-start(bf16[4,96,384]{2,1,0:T(8,128)(2,1)S(1)} %get-tuple-element.125), channel_id=1, source_target_pairs={{0,1},{1,0},{2,3},{3,2},{4,5},{5,4},{6,7},{7,6},{8,9},{9,8},{10,11... | collective-permute-start | bytes 884744 | tf_op jit(solution)/shard_map/ppermute | solution.py:23
  115.9 10.5 %collective-permute-start.56 = (bf16[4,24,768]{2,1,0:T(8,128)(2,1)}, bf16[4,24,768]{2,1,0:T(8,128)(2,1)S(1)}, u32[]{:S(2)}, u32[]{:S(2)}) collective-permute-start(bf16[4,24,768]{2,1,0:T(8,128)(2,1)} %add_convert_fusion.8), channel_id=1, source_target_pairs={{0,4},{1,5},{2,6},{3,7},{4,0},{5,1},{6,2},{7,3},{8,12},{9,13},{10,... | collective-permute-start | bytes 442376 | tf_op jit(solution)/shard_map/ppermute | solution.py:23
  121.8 6.9 %collective-permute-start.40 = (bf16[4,48,384]{2,1,0:T(8,128)(2,1)S(1)}, bf16[4,48,384]{2,1,0:T(8,128)(2,1)}, u32[]{:S(2)}, u32[]{:S(2)}) collective-permute-start(bf16[4,48,384]{2,1,0:T(8,128)(2,1)S(1)} %add_convert_fusion.6), channel_id=1, source_target_pairs={{0,1},{1,0},{2,3},{3,2},{4,5},{5,4},{6,7},{7,6},{8,9},{9,8},{10,11... | collective-permute-start | bytes 442376 | tf_op jit(solution)/shard_map/ppermute | solution.py:23
  125.8 6.0 %collective-permute-start.33 = (bf16[144,768]{1,0:T(8,128)(2,1)S(1)}, bf16[144,768]{1,0:T(8,128)(2,1)S(1)}, u32[]{:S(2)}, u32[]{:S(2)}) collective-permute-start(bf16[144,768]{1,0:T(8,128)(2,1)S(1)} %get-tuple-element.122), channel_id=1, source_target_pairs={{0,8},{8,0},{16,24},{24,16},{1,9},{9,1},{17,25},{25,17},{2,10},{10... | collective-permute-start | bytes 663560 | tf_op jit(solution)/shard_map/ppermute | solution.py:19
  125.8 65.1 %collective-permute-start.32 = (bf16[128,768]{1,0:T(8,128)(2,1)}, bf16[128,768]{1,0:T(8,128)(2,1)}, u32[]{:S(2)}, u32[]{:S(2)}) collective-permute-start(bf16[128,768]{1,0:T(8,128)(2,1)} %get-tuple-element.119), channel_id=1, source_target_pairs={{0,8},{8,0},{16,24},{24,16},{1,9},{9,1},{17,25},{25,17},{2,10},{10... | collective-permute-start | bytes 589832 | tf_op jit(solution)/shard_map/ppermute | solution.py:19
  126.3 9.9 %collective-permute-start.48 = (bf16[1,96,768]{2,1,0:T(8,128)(2,1)S(1)}, bf16[1,96,768]{2,1,0:T(8,128)(2,1)S(1)}, u32[]{:S(2)}, u32[]{:S(2)}) collective-permute-start(bf16[1,96,768]{2,1,0:T(8,128)(2,1)S(1)} %copy-done.45), channel_id=1, source_target_pairs={{0,4},{1,5},{2,6},{3,7},{4,0},{5,1},{6,2},{7,3},{8,12},{9,13},{10,... | collective-permute-start | bytes 442376 | tf_op jit(solution)/shard_map/ppermute | solution.py:23
  129.9 8.0 %collective-permute-start.57 = (bf16[24,768]{1,0:T(8,128)(2,1)S(1)}, bf16[24,768]{1,0:T(8,128)(2,1)S(1)}, u32[]{:S(2)}, u32[]{:S(2)}) collective-permute-start(bf16[24,768]{1,0:T(8,128)(2,1)S(1)} %get-tuple-element.221), channel_id=1, source_target_pairs={{0,8},{8,0},{16,24},{24,16},{1,9},{9,1},{17,25},{25,17},{2,10},{10... | collective-permute-start | bytes 110600 | tf_op jit(solution)/shard_map/ppermute | solution.py:19
  130.0 8.6 %collective-permute-start.58 = (bf16[24,768]{1,0:T(8,128)(2,1)S(1)}, bf16[24,768]{1,0:T(8,128)(2,1)S(1)}, u32[]{:S(2)}, u32[]{:S(2)}) collective-permute-start(bf16[24,768]{1,0:T(8,128)(2,1)S(1)} %get-tuple-element.220), channel_id=1, source_target_pairs={{0,16},{8,24},{16,0},{24,8},{1,17},{9,25},{17,1},{25,9},{2,18},{10... | collective-permute-start | bytes 110600 | tf_op jit(solution)/shard_map/ppermute | solution.py:19
  131.8 9.1 %collective-permute-start.59 = (bf16[24,768]{1,0:T(8,128)(2,1)S(1)}, bf16[24,768]{1,0:T(8,128)(2,1)S(1)}, u32[]{:S(2)}, u32[]{:S(2)}) collective-permute-start(bf16[24,768]{1,0:T(8,128)(2,1)S(1)} %get-tuple-element.219), channel_id=1, source_target_pairs={{0,24},{8,16},{16,8},{24,0},{1,25},{9,17},{17,9},{25,1},{2,26},{10... | collective-permute-start | bytes 110600 | tf_op jit(solution)/shard_map/ppermute | solution.py:19
  136.2 15.4 %collective-permute-start.39 = (bf16[144,768]{1,0:T(8,128)(2,1)S(1)}, bf16[144,768]{1,0:T(8,128)(2,1)S(1)}, u32[]{:S(2)}, u32[]{:S(2)}) collective-permute-start(bf16[144,768]{1,0:T(8,128)(2,1)S(1)} %get-tuple-element.130), channel_id=1, source_target_pairs={{0,16},{8,24},{16,0},{24,8},{1,17},{9,25},{17,1},{25,9},{2,18},{10... | collective-permute-start | bytes 663560 | tf_op jit(solution)/shard_map/ppermute | solution.py:19
  137.9 12.1 %collective-permute-start.42 = (bf16[4,24,384]{2,1,0:T(8,128)(2,1)S(1)}, bf16[4,24,384]{2,1,0:T(8,128)(2,1)S(1)}, u32[]{:S(2)}, u32[]{:S(2)}) collective-permute-start(bf16[4,24,384]{2,1,0:T(8,128)(2,1)S(1)} %add_convert_fusion.11), channel_id=1, source_target_pairs={{0,4},{1,5},{2,6},{3,7},{4,0},{5,1},{6,2},{7,3},{8,12},{9,13},{10,... | collective-permute-start | bytes 221192 | tf_op jit(solution)/shard_map/ppermute | solution.py:23
  138.6 13.0 %collective-permute-start.41 = (bf16[4,24,384]{2,1,0:T(8,128)(2,1)S(1)}, bf16[4,24,384]{2,1,0:T(8,128)(2,1)S(1)}, u32[]{:S(2)}, u32[]{:S(2)}) collective-permute-start(bf16[4,24,384]{2,1,0:T(8,128)(2,1)S(1)} %add_convert_fusion.12), channel_id=1, source_target_pairs={{0,4},{1,5},{2,6},{3,7},{4,0},{5,1},{6,2},{7,3},{8,12},{9,13},{10,... | collective-permute-start | bytes 221192 | tf_op jit(solution)/shard_map/ppermute | solution.py:23
  140.9 14.9 %collective-permute-start.49 = (bf16[1,96,768]{2,1,0:T(8,128)(2,1)S(1)}, bf16[1,96,768]{2,1,0:T(8,128)(2,1)S(1)}, u32[]{:S(2)}, u32[]{:S(2)}) collective-permute-start(bf16[1,96,768]{2,1,0:T(8,128)(2,1)S(1)} %fusion.27), channel_id=1, source_target_pairs={{0,4},{1,5},{2,6},{3,7},{4,0},{5,1},{6,2},{7,3},{8,12},{9,13},{10,... | collective-permute-start | bytes 442376 | tf_op jit(solution)/shard_map/ppermute | solution.py:23
  155.8 8.8 %collective-permute-start.60 = (bf16[4,24,768]{2,1,0:T(8,128)(2,1)S(1)}, bf16[4,24,768]{2,1,0:T(8,128)(2,1)S(1)}, u32[]{:S(2)}, u32[]{:S(2)}) collective-permute-start(bf16[4,24,768]{2,1,0:T(8,128)(2,1)S(1)} %pad_maximum_fusion.16), channel_id=1, source_target_pairs={{0,4},{1,5},{2,6},{3,7},{4,0},{5,1},{6,2},{7,3},{8,12},{9,13},{10,... | collective-permute-start | bytes 442376 | tf_op jit(solution)/shard_map/ppermute | solution.py:23
  155.9 16.2 %collective-permute-start.50 = (bf16[1,192,768]{2,1,0:T(8,128)(2,1)S(1)}, bf16[1,192,768]{2,1,0:T(8,128)(2,1)S(1)}, u32[]{:S(2)}, u32[]{:S(2)}) collective-permute-start(bf16[1,192,768]{2,1,0:T(8,128)(2,1)S(1)} %pad_maximum_fusion.8), channel_id=1, source_target_pairs={{0,2},{1,3},{2,0},{3,1},{4,6},{5,7},{6,4},{7,5},{8,10},{9,11},{10,... | collective-permute-start | bytes 884744 | tf_op jit(solution)/shard_map/ppermute | solution.py:23
  158.8 14.2 %collective-permute-start.47 = (bf16[128,384]{1,0:T(8,128)(2,1)S(1)}, bf16[128,384]{1,0:T(8,128)(2,1)S(1)}, u32[]{:S(2)}, u32[]{:S(2)}) collective-permute-start(bf16[128,384]{1,0:T(8,128)(2,1)S(1)} %pad_maximum_fusion.20), channel_id=1, source_target_pairs={{0,4},{1,5},{2,6},{3,7},{4,0},{5,1},{6,2},{7,3},{8,12},{9,13},{10,... | collective-permute-start | bytes 294920 | tf_op jit(solution)/shard_map/ppermute | solution.py:23
  159.3 13.7 %collective-permute-start.46 = (bf16[4,24,384]{2,1,0:T(8,128)(2,1)S(1)}, bf16[4,24,384]{2,1,0:T(8,128)(2,1)S(1)}, u32[]{:S(2)}, u32[]{:S(2)}) collective-permute-start(bf16[4,24,384]{2,1,0:T(8,128)(2,1)S(1)} %pad_maximum_fusion.21), channel_id=1, source_target_pairs={{0,4},{1,5},{2,6},{3,7},{4,0},{5,1},{6,2},{7,3},{8,12},{9,13},{10,... | collective-permute-start | bytes 221192 | tf_op jit(solution)/shard_map/ppermute | solution.py:23
  164.6 10.2 %collective-permute-start.61 = (bf16[4,48,768]{2,1,0:T(8,128)(2,1)S(1)}, bf16[4,48,768]{2,1,0:T(8,128)(2,1)S(1)}, u32[]{:S(2)}, u32[]{:S(2)}) collective-permute-start(bf16[4,48,768]{2,1,0:T(8,128)(2,1)S(1)} %pad_maximum_fusion.11), channel_id=1, source_target_pairs={{0,1},{1,0},{2,3},{3,2},{4,5},{5,4},{6,7},{7,6},{8,9},{9,8},{10,11... | collective-permute-start | bytes 884744 | tf_op jit(solution)/shard_map/ppermute | solution.py:23
  172.3 20.3 %collective-permute-start.55 = (bf16[1,384,768]{2,1,0:T(8,128)(2,1)S(1)}, bf16[1,384,768]{2,1,0:T(8,128)(2,1)S(1)}, u32[]{:S(2)}, u32[]{:S(2)}) collective-permute-start(bf16[1,384,768]{2,1,0:T(8,128)(2,1)S(1)} %get-tuple-element.204), channel_id=1, source_target_pairs={{0,1},{1,0},{2,3},{3,2},{4,5},{5,4},{6,7},{7,6},{8,9},{9,8},{10,11... | collective-permute-start | bytes 1769480 | tf_op jit(solution)/shard_map/ppermute | solution.py:23
  173.1 16.8 %collective-permute-start.51 = (bf16[4,48,384]{2,1,0:T(8,128)(2,1)S(1)}, bf16[4,48,384]{2,1,0:T(8,128)(2,1)S(1)}, u32[]{:S(2)}, u32[]{:S(2)}) collective-permute-start(bf16[4,48,384]{2,1,0:T(8,128)(2,1)S(1)} %pad_maximum_fusion.14), channel_id=1, source_target_pairs={{0,1},{1,0},{2,3},{3,2},{4,5},{5,4},{6,7},{7,6},{8,9},{9,8},{10,11... | collective-permute-start | bytes 442376 | tf_op jit(solution)/shard_map/ppermute | solution.py:23
  174.8 15.1 %collective-permute-start.53 = (bf16[224,384]{1,0:T(8,128)(2,1)S(1)}, bf16[224,384]{1,0:T(8,128)(2,1)S(1)}, u32[]{:S(2)}, u32[]{:S(2)}) collective-permute-start(bf16[224,384]{1,0:T(8,128)(2,1)S(1)} %pad_maximum_fusion.13), channel_id=1, source_target_pairs={{0,2},{1,3},{2,0},{3,1},{4,6},{5,7},{6,4},{7,5},{8,10},{9,11},{10,... | collective-permute-start | bytes 516104 | tf_op jit(solution)/shard_map/ppermute | solution.py:23
  175.0 19.7 %collective-permute-start.62 = (bf16[4,96,768]{2,1,0:T(8,128)(2,1)S(1)}, bf16[4,96,768]{2,1,0:T(8,128)(2,1)S(1)}, u32[]{:S(2)}, u32[]{:S(2)}) collective-permute-start(bf16[4,96,768]{2,1,0:T(8,128)(2,1)S(1)} %pad_maximum_fusion.6.held), channel_id=1, source_target_pairs={{0,2},{1,3},{2,0},{3,1},{4,6},{5,7},{6,4},{7,5},{8,10},{9,11},{10,... | collective-permute-start | bytes 1769480 | tf_op jit(solution)/shard_map/ppermute | solution.py:23
  190.1 8.5 %collective-permute-start.54 = (bf16[416,384]{1,0:T(8,128)(2,1)S(1)}, bf16[416,384]{1,0:T(8,128)(2,1)S(1)}, u32[]{:S(2)}, u32[]{:S(2)}) collective-permute-start(bf16[416,384]{1,0:T(8,128)(2,1)S(1)} %pad_maximum_fusion.7), channel_id=1, source_target_pairs={{0,1},{1,0},{2,3},{3,2},{4,5},{5,4},{6,7},{7,6},{8,9},{9,8},{10,11... | collective-permute-start | bytes 958472 | tf_op jit(solution)/shard_map/ppermute | solution.py:23
  190.8 7.8 %collective-permute-start.52 = (bf16[4,96,384]{2,1,0:T(8,128)(2,1)S(1)}, bf16[4,96,384]{2,1,0:T(8,128)(2,1)S(1)}, u32[]{:S(2)}, u32[]{:S(2)}) collective-permute-start(bf16[4,96,384]{2,1,0:T(8,128)(2,1)S(1)} %pad_maximum_fusion.9.held_one), channel_id=1, source_target_pairs={{0,2},{1,3},{2,0},{3,1},{4,6},{5,7},{6,4},{7,5},{8,10},{9,11},{10,... | collective-permute-start | bytes 884744 | tf_op jit(solution)/shard_map/ppermute | solution.py:23
  (63 other events, 279.7 us)

commit v6 on v5

--- a/solution.py
+++ b/solution.py
@@ -235,7 +235,8 @@
         pre = dot(ref[...], up[...]) + bias[...]
         cdf = 0.5 * (1.0 + lax.erf(pre * (0.5**0.5)))
         act[where, :] = (pre * cdf).astype(BF)
-        slope[where, :] = cdf + pre * jnp.exp(-0.5 * pre * pre) * ((2 * jnp.pi) ** -0.5)
+        value = cdf + pre * jnp.exp(-0.5 * pre * pre) * ((2 * jnp.pi) ** -0.5)
+        slope[where, :] = value.astype(BF)
     for block, out in enumerate(outs):
         where = pl.ds(block * rows, rows)
         out[...] = dot(act[where, :], down[...]).astype(out.dtype)
@@ -422,7 +423,7 @@
         hidden_kernel,
         [
             jax.ShapeDtypeStruct((G * rows, hidden), BF),
-            jax.ShapeDtypeStruct((G * rows, hidden), F32),
+            jax.ShapeDtypeStruct((G * rows, hidden), BF),
             block,
             block_low,
             block,
@@ -445,7 +446,7 @@
     d_second_all = jnp.concatenate(gather_rows(d_second), axis=0)
     down = Scatter(t_dot(act, d_second_all).astype(BF)[None], first_y, me, replicas)
     down_got = down.swap(down.send())
-    d_pre = (dot_t(d_second_all, down_weight) * slope).astype(BF)
+    d_pre = (dot_t(d_second_all, down_weight) * slope.astype(F32)).astype(BF)
     vec_up = jnp.sum(d_pre.astype(F32), axis=0, keepdims=True)
     d_normed = dot_t(d_pre, up_local)
     far = d_normed[2 * rows : 3 * rows] + gx(d_normed[3 * rows :].astype(BF), 1).astype(F32)

time: 202 us -> 203 us (level)
    unnamed x96 -> x98, local copies, waits for them, and re-layouts: 6.85 us -> 7.74 us
where the time goes in v6:
time: 203 us; the launch traced here: 202 us
  waiting for transfers between devices  78.2 us (39%)
  starting transfers between devices  47.6 us (23%)
  other arithmetic  28.3 us (14%)
  local copies, waits for them, and re-layouts  18 us (9%)
  Pallas kernels  18 us (9%)
  matrix products  9.68 us (5%)
    ppermute x24, waiting for transfers between devices, rx(): return lax.ppermute(value, 'replica', [(i, i ^ bits) for i in range(count)])  41.3 us
    ppermute x39, waiting for transfers between devices, gx(): return lax.ppermute(value, 'group', [(i, i ^ bits) for i in range(G)])  36.9 us
    ppermute x24, starting transfers between devices, rx(): return lax.ppermute(value, 'replica', [(i, i ^ bits) for i in range(count)])  28.5 us
    ppermute x39, starting transfers between devices, gx(): return lax.ppermute(value, 'group', [(i, i ^ bits) for i in range(G)])  19.1 us
    pallas_call x8, Pallas kernels, call(): pl.pallas_call(kernel, out_shape=outs, in_specs=[index_spec()] + [whole_s...  18 us
    convert_element_type x8, other arithmetic, send(): self.sent = self.total(1 - self.mine).astype(BF)  8.32 us
    unnamed x98, local copies, waits for them, and re-layouts  7.74 us
    concatenate x1, local copies, waits for them, and re-layouts, on_device(): small = jnp.concatenate(smalls).reshape(1, -1)  4.83 us
  transfers between devices with their start and end apart: 63, of which 25 were waited for; matrix products, arithmetic and copies ran while one was open for 21% of the time, Pallas kernels for 6%

profile of v6, /device:TPU:0, one launch (start us, length us, event | category | flops | bytes accessed | tf_op | source)
XLA Modules:
  0.0 201.6 jit_solution(4581244470772882852)
XLA Ops:
  1.2 2.6 %collective-permute-start.1 = (bf16[128,768]{1,0:T(8,128)(2,1)}, bf16[128,768]{1,0:T(8,128)(2,1)}, u32[]{:S(2)}, u32[]{:S(2)}) collective-permute-start(bf16[128,768]{1,0:T(8,128)(2,1)} %bitcast.109), channel_id=1, source_target_pairs={{0,16},{8,24},{16,0},{24,8},{1,17},{9,25},{17,1},{25,9},{2,18},{10... | collective-permute-start | bytes 589832 | tf_op jit(solution)/shard_map/ppermute | solution.py:19
  6.0 2.0 collective-permute-start.4
  9.8 4.8 %concatenate.78 = bf16[1536]{0:T(1024)(128)(2,1)S(1)} concatenate(bf16[384]{0:T(512)(128)(2,1)} %param.19, bf16[192]{0:T(256)(128)(2,1)} %param.21, bf16[192]{0:T(256)(128)(2,1)} %param.22, bf16[192]{0:T(256)(128)(2,1)} %param.23, bf16[192]{0:T(256)(128)(2,1)} %param.27, bf16[192]{0:T(256)(128)(2,1)} %param.28, bf16[192]{0:T(256)(128)(2,1)} %param.29), dimensions={0} | concatenate | bytes 6144 | tf_op jit(solution)/shard_map/concatenate | solution.py:376
  14.7 2.0 collective-permute-start.6
  16.9 2.3 %constant_dynamic-slice_fusion.3 = (bf16[192,768]{1,0:T(8,128)(2,1)}, bf16[192,768]{1,0:T(8,128)(2,1)}, bf16[192,768]{1,0:T(8,128)(2,1)}, bf16[192,768]{1,0:T(8,128)(2,1)}) fusion(bf16[192,3072]{1,0:T(8,128)(2,1)} %param.24, s32[]{:T(128)S(6)} %select_n.351, s32[]{:T(128)S(6)} %select_n.350, s32[]{:T(128)S(6)} %select_n.349, s32[]{:T(128)S(6)} %select_n.348), kind=kLoop, calls=%fused_computation.171 | loop fusion | bytes 2359312 | tf_op jit(solution)/shard_map/dynamic_slice | solution.py:385
  23.2 1.7 fusion
  27.6 1.4 fusion.2
  29.0 1.5 convolution_convert_fusion.3
  32.2 2.1 %collective-permute-done.11 = bf16[192,768]{1,0:T(8,128)(2,1)} collective-permute-done((bf16[192,768]{1,0:T(8,128)(2,1)}, bf16[192,768]{1,0:T(8,128)(2,1)}, u32[]{:S(2)}, u32[]{:S(2)}) %collective-permute-start.11) | collective-permute-done | bytes 294944 | tf_op jit(solution)/shard_map/ppermute | solution.py:19
  40.5 4.5 %collective-permute-done.14 = bf16[128,768]{1,0:T(8,128)(2,1)S(1)} collective-permute-done((bf16[128,768]{1,0:T(8,128)(2,1)S(1)}, bf16[128,768]{1,0:T(8,128)(2,1)S(1)}, u32[]{:S(2)}, u32[]{:S(2)}) %collective-permute-start.14) | collective-permute-done | bytes 196640 | tf_op jit(solution)/shard_map/ppermute | solution.py:19
  46.9 6.1 %collective-permute-done.16.far = bf16[128,768]{1,0:T(8,128)(2,1)S(1)} collective-permute-done((bf16[128,768]{1,0:T(8,128)(2,1)S(1)}, bf16[128,768]{1,0:T(8,128)(2,1)S(1)}, u32[]{:S(2)}, u32[]{:S(2)}) %collective-permute-start.16) | collective-permute-done | bytes 196640 | tf_op jit(solution)/shard_map/ppermute | solution.py:19
  53.1 1.4 collective-permute-done.17.last
  54.5 2.9 %shard_map.255 = (bf16[512,768]{1,0:T(8,128)(2,1)S(1)}, bf16[512,768]{1,0:T(8,128)(2,1)S(1)}, f32[128,768]{1,0:T(8,128)S(1)}, bf16[128,768]{1,0:T(8,128)(2,1)S(1...) custom-call(s32[3]{0:T(128)S(1)} %pad_add_fusion.1.index, bf16[128,768]{1,0:T(8,128)(2,1)S(1)} %fusion.24.own, ...), custom_call_target="tpu_custom_call" | custom-call | tf_op jit(solution)/shard_map/pallas_call | solution.py:140
  64.5 6.6 %collective-permute-done.20 = bf16[128,768]{1,0:T(8,128)(2,1)S(1)} collective-permute-done((bf16[128,768]{1,0:T(8,128)(2,1)S(1)}, bf16[128,768]{1,0:T(8,128)(2,1)S(1)}, u32[]{:S(2)}, u32[]{:S(2)}) %collective-permute-start.20) | collective-permute-done | bytes 196640 | tf_op jit(solution)/shard_map/ppermute | solution.py:19
  71.2 1.4 fusion.62
  73.7 5.8 %collective-permute-done.22 = bf16[128,768]{1,0:T(8,128)(2,1)S(1)} collective-permute-done((bf16[128,768]{1,0:T(8,128)(2,1)S(1)}, bf16[128,768]{1,0:T(8,128)(2,1)S(1)}, u32[]{:S(2)}, u32[]{:S(2)}) %collective-permute-start.22) | collective-permute-done | bytes 196640 | tf_op jit(solution)/shard_map/ppermute | solution.py:19
  79.5 1.4 collective-permute-done.23
  84.5 1.6 collective-permute-start.30
  87.9 1.6 collective-permute-start.31
  89.5 3.4 %collective-permute-done.26 = bf16[128,768]{1,0:T(8,128)(2,1)S(1)} collective-permute-done((bf16[128,768]{1,0:T(8,128)(2,1)S(1)}, bf16[128,768]{1,0:T(8,128)(2,1)S(1)}, u32[]{:S(2)}, u32[]{:S(2)}) %collective-permute-start.26) | collective-permute-done | bytes 196640 | tf_op jit(solution)/shard_map/ppermute | solution.py:19
  96.7 3.3 %collective-permute-done.30 = bf16[1,384,768]{2,1,0:T(8,128)(2,1)S(1)} collective-permute-done((bf16[1,384,768]{2,1,0:T(8,128)(2,1)S(1)}, bf16[1,384,768]{2,1,0:T(8,128)(2,1)S(1)}, u32[]{:S(2)}, u32[]{:S(2)}) %collective-permute-start.30) | collective-permute-done | bytes 589856 | tf_op jit(solution)/shard_map/ppermute | solution.py:23
  101.5 1.6 collective-permute-start.36
  105.0 4.7 %shard_map.256 = (bf16[384,512]{1,0:T(8,128)(2,1)S(1)}, bf16[192,512]{1,0:T(8,128)(2,1)S(1)}, bf16[4,192,384]{2,1,0:T(8,128)(2,1)S(1)}, bf16[4,192,384]{2,1,0:T(...) custom-call(s32[3]{0:T(128)S(1)} %pad_add_fusion.1.index, ...), custom_call_target="tpu_custom_call" | custom-call | tf_op jit(solution)/shard_map/pallas_call | solution.py:140
  110.5 1.6 collective-permute-start.34
  112.8 1.8 fusion.29
  114.6 1.8 add_convert_fusion.8
  116.4 2.6 %collective-permute-start.56 = (bf16[4,24,768]{2,1,0:T(8,128)(2,1)}, bf16[4,24,768]{2,1,0:T(8,128)(2,1)S(1)}, u32[]{:S(2)}, u32[]{:S(2)}) collective-permute-start(bf16[4,24,768]{2,1,0:T(8,128)(2,1)} %add_convert_fusion.8), channel_id=1, source_target_pairs={{0,4},{1,5},{2,6},{3,7},{4,0},{5,1},{6,2},{7,3},{8,12},{9,13},{10,... | collective-permute-start | bytes 442376 | tf_op jit(solution)/shard_map/ppermute | solution.py:23
  119.0 2.1 %collective-permute-done.34 = bf16[4,96,384]{2,1,0:T(8,128)(2,1)} collective-permute-done((bf16[4,96,384]{2,1,0:T(8,128)(2,1)}, bf16[4,96,384]{2,1,0:T(8,128)(2,1)}, u32[]{:S(2)}, u32[]{:S(2)}) %collective-permute-start.34) | collective-permute-done | bytes 294944 | tf_op jit(solution)/shard_map/ppermute | solution.py:23
  122.2 1.3 collective-permute-start.40
  123.9 2.4 %shard_map.257 = (bf16[128,768]{1,0:T(8,128)(2,1)}, bf16[144,768]{1,0:T(8,128)(2,1)S(1)}, f32[128,768]{1,0:T(8,128)S(1)}, f32[128,768]{1,0:T(8,128)S(1)}, f32[16,768]{1,0:T(8,128)S(1)}) custom-call(s32[3]{0:T(128)S(1)} %pad_add_fusion.1.index, bf16[384,512]{1,0:T(8,128)(2,1)S(1)} %get-tuple-element.116.d_qk, bf16[192,512]{1,0:T(8,128)(2,1)S(1)} %get-tuple-element.117.d_v, ...), custom_call_target="tpu_custom_call" | custom-call | tf_op jit(solution)/shard_map/pallas_call | solution.py:140
  126.8 2.4 %collective-permute-start.48 = (bf16[1,96,768]{2,1,0:T(8,128)(2,1)S(1)}, bf16[1,96,768]{2,1,0:T(8,128)(2,1)S(1)}, u32[]{:S(2)}, u32[]{:S(2)}) collective-permute-start(bf16[1,96,768]{2,1,0:T(8,128)(2,1)S(1)} %copy-done.47), channel_id=1, source_target_pairs={{0,4},{1,5},{2,6},{3,7},{4,0},{5,1},{6,2},{7,3},{8,12},{9,13},{10,... | collective-permute-start | bytes 442376 | tf_op jit(solution)/shard_map/ppermute | solution.py:23
  134.9 1.8 collective-permute-done.48
  139.1 2.3 %collective-permute-start.41 = (bf16[4,24,384]{2,1,0:T(8,128)(2,1)S(1)}, bf16[4,24,384]{2,1,0:T(8,128)(2,1)S(1)}, u32[]{:S(2)}, u32[]{:S(2)}) collective-permute-start(bf16[4,24,384]{2,1,0:T(8,128)(2,1)S(1)} %add_convert_fusion.12), channel_id=1, source_target_pairs={{0,4},{1,5},{2,6},{3,7},{4,0},{5,1},{6,2},{7,3},{8,12},{9,13},{10,... | collective-permute-start | bytes 221192 | tf_op jit(solution)/shard_map/ppermute | solution.py:23
  142.0 8.5 %collective-permute-done.42 = bf16[4,24,384]{2,1,0:T(8,128)(2,1)S(1)} collective-permute-done((bf16[4,24,384]{2,1,0:T(8,128)(2,1)S(1)}, bf16[4,24,384]{2,1,0:T(8,128)(2,1)S(1)}, u32[]{:S(2)}, u32[]{:S(2)}) %collective-permute-start.42) | collective-permute-done | bytes 73760 | tf_op jit(solution)/shard_map/ppermute | solution.py:23
  150.5 1.6 collective-permute-done.41
  154.4 1.3 collective-permute-start.44
  156.4 1.7 collective-permute-start.50
  159.8 2.6 %collective-permute-start.46 = (bf16[4,24,384]{2,1,0:T(8,128)(2,1)S(1)}, bf16[4,24,384]{2,1,0:T(8,128)(2,1)S(1)}, u32[]{:S(2)}, u32[]{:S(2)}) collective-permute-start(bf16[4,24,384]{2,1,0:T(8,128)(2,1)S(1)} %pad_maximum_fusion.21), channel_id=1, source_target_pairs={{0,4},{1,5},{2,6},{3,7},{4,0},{5,1},{6,2},{7,3},{8,12},{9,13},{10,... | collective-permute-start | bytes 221192 | tf_op jit(solution)/shard_map/ppermute | solution.py:23
  162.4 2.7 %collective-permute-done.60 = bf16[4,24,768]{2,1,0:T(8,128)(2,1)S(1)} collective-permute-done((bf16[4,24,768]{2,1,0:T(8,128)(2,1)S(1)}, bf16[4,24,768]{2,1,0:T(8,128)(2,1)S(1)}, u32[]{:S(2)}, u32[]{:S(2)}) %collective-permute-start.60) | collective-permute-done | bytes 147488 | tf_op jit(solution)/shard_map/ppermute | solution.py:23
  165.8 6.8 %collective-permute-done.50 = bf16[1,192,768]{2,1,0:T(8,128)(2,1)S(1)} collective-permute-done((bf16[1,192,768]{2,1,0:T(8,128)(2,1)S(1)}, bf16[1,192,768]{2,1,0:T(8,128)(2,1)S(1)}, u32[]{:S(2)}, u32[]{:S(2)}) %collective-permute-start.50) | collective-permute-done | bytes 294944 | tf_op jit(solution)/shard_map/ppermute | solution.py:23
  173.6 1.5 collective-permute-start.51
  175.5 2.1 %collective-permute-start.62 = (bf16[4,96,768]{2,1,0:T(8,128)(2,1)S(1)}, bf16[4,96,768]{2,1,0:T(8,128)(2,1)S(1)}, u32[]{:S(2)}, u32[]{:S(2)}) collective-permute-start(bf16[4,96,768]{2,1,0:T(8,128)(2,1)S(1)} %pad_maximum_fusion.6.held), channel_id=1, source_target_pairs={{0,2},{1,3},{2,0},{3,1},{4,6},{5,7},{6,4},{7,5},{8,10},{9,11},{10,... | collective-permute-start | bytes 1769480 | tf_op jit(solution)/shard_map/ppermute | solution.py:23
  177.6 12.8 %collective-permute-done.51 = bf16[4,48,384]{2,1,0:T(8,128)(2,1)S(1)} collective-permute-done((bf16[4,48,384]{2,1,0:T(8,128)(2,1)S(1)}, bf16[4,48,384]{2,1,0:T(8,128)(2,1)S(1)}, u32[]{:S(2)}, u32[]{:S(2)}) %collective-permute-start.51) | collective-permute-done | bytes 147488 | tf_op jit(solution)/shard_map/ppermute | solution.py:23
  191.4 1.7 add_convert_fusion.1
  193.1 2.1 %shard_map.259 = f32[768,768]{1,0:T(8,128)} custom-call(s32[3]{0:T(128)S(1)} %pad_add_fusion.1.index, bf16[384,768]{1,0:T(8,128)(2,1)S(1)} %get-tuple-element.203.held, bf16[384,768]{1,0:T(8,128)(2,1)S(1)} %bitcast.101), custom_call_target="tpu_custom_call" | custom-call | tf_op jit(solution)/shard_map/pallas_call | solution.py:140
  195.2 2.1 %shard_map.260 = f32[192,3072]{1,0:T(8,128)} custom-call(s32[3]{0:T(128)S(1)} %pad_add_fusion.1.index, bf16[4,96,768]{2,1,0:T(8,128)(2,1)S(1)} %pad_maximum_fusion.6.held, bf16[4,96,768]{2,1,0:T(8,128)(2,1)S(1)} %collective-permute-done.62.got), custom_call_target="tpu_custom_call" | custom-call | tf_op jit(solution)/shard_map/pallas_call | solution.py:140
  197.3 1.8 collective-permute-done.52.got_one
  199.1 2.5 %shard_map.261 = (f32[192,768]{1,0:T(8,128)}, f32[192,2304]{1,0:T(8,128)}, f32[768]{0:T(1024)}, f32[384]{0:T(512)}, f32[192]{0:T(256)}, /*index=5*/f32[192]{0:T(...) custom-call(s32[3]{0:T(128)S(1)} %pad_add_fusion.1.index, bf16[4,96,384]{2,1,0:T(8,128)(2,1)S(1)} %pad_maximum_fusion.9.held_one, ...), custom_call_target="tpu_custom_call" | custom-call | tf_op jit(solution)/shard_map/pallas_call | solution.py:140
  (315 shorter events, 61.3 us)
Async XLA Ops:
  0.6 9.2 %collective-permute-start = (bf16[128,768]{1,0:T(8,128)(2,1)}, bf16[128,768]{1,0:T(8,128)(2,1)S(1)}, u32[]{:S(2)}, u32[]{:S(2)}) collective-permute-start(bf16[128,768]{1,0:T(8,128)(2,1)} %bitcast.108), channel_id=1, source_target_pairs={{0,8},{8,0},{16,24},{24,16},{1,9},{9,1},{17,25},{25,17},{2,10},{10... | collective-permute-start | bytes 589832 | tf_op jit(solution)/shard_map/ppermute | solution.py:19
  1.2 8.6 %collective-permute-start.1 = (bf16[128,768]{1,0:T(8,128)(2,1)}, bf16[128,768]{1,0:T(8,128)(2,1)}, u32[]{:S(2)}, u32[]{:S(2)}) collective-permute-start(bf16[128,768]{1,0:T(8,128)(2,1)} %bitcast.109), channel_id=1, source_target_pairs={{0,16},{8,24},{16,0},{24,8},{1,17},{9,25},{17,1},{25,9},{2,18},{10... | collective-permute-start | bytes 589832 | tf_op jit(solution)/shard_map/ppermute | solution.py:19
  6.0 13.1 %collective-permute-start.3 = (bf16[192,576]{1,0:T(8,128)(2,1)S(1)}, bf16[192,576]{1,0:T(8,128)(2,1)S(1)}, u32[]{:S(2)}, u32[]{:S(2)}) collective-permute-start(bf16[192,576]{1,0:T(8,128)(2,1)S(1)} %get-tuple-element.87), channel_id=1, source_target_pairs={{0,24},{8,16},{16,8},{24,0},{1,25},{9,17},{17,9},{25,1},{2,26},{10... | collective-permute-start | bytes 663560 | tf_op jit(solution)/shard_map/ppermute | solution.py:19
  6.0 14.0 %collective-permute-start.4 = (bf16[192,576]{1,0:T(8,128)(2,1)S(1)}, bf16[192,576]{1,0:T(8,128)(2,1)S(1)}, u32[]{:S(2)}, u32[]{:S(2)}) collective-permute-start(bf16[192,576]{1,0:T(8,128)(2,1)S(1)} %get-tuple-element.88), channel_id=1, source_target_pairs={{0,16},{8,24},{16,0},{24,8},{1,17},{9,25},{17,1},{25,9},{2,18},{10... | collective-permute-start | bytes 663560 | tf_op jit(solution)/shard_map/ppermute | solution.py:19
  9.8 13.4 %collective-permute-start.2 = (bf16[128,768]{1,0:T(8,128)(2,1)}, bf16[128,768]{1,0:T(8,128)(2,1)}, u32[]{:S(2)}, u32[]{:S(2)}) collective-permute-start(bf16[128,768]{1,0:T(8,128)(2,1)} %collective-permute-done.1), channel_id=1, source_target_pairs={{0,8},{8,0},{16,24},{24,16},{1,9},{9,1},{17,25},{25,17},{2,10},{10... | collective-permute-start | bytes 589832 | tf_op jit(solution)/shard_map/ppermute | solution.py:19
  14.7 6.5 %collective-permute-start.6 = (bf16[1,1536]{1,0:T(2,128)(2,1)S(1)}, bf16[1,1536]{1,0:T(2,128)(2,1)S(1)}, u32[]{:S(2)}, u32[]{:S(2)}) collective-permute-start(bf16[1,1536]{1,0:T(2,128)(2,1)S(1)} %reshape.205), channel_id=1, source_target_pairs={{0,16},{8,24},{16,0},{24,8},{1,17},{9,25},{17,1},{25,9},{2,18},{10... | collective-permute-start | bytes 9224 | tf_op jit(solution)/shard_map/ppermute | solution.py:19
  19.1 13.1 %collective-permute-start.10 = (bf16[192,768]{1,0:T(8,128)(2,1)}, bf16[192,768]{1,0:T(8,128)(2,1)}, u32[]{:S(2)}, u32[]{:S(2)}) collective-permute-start(bf16[192,768]{1,0:T(8,128)(2,1)} %get-tuple-element.190), channel_id=1, source_target_pairs={{0,16},{8,24},{16,0},{24,8},{1,17},{9,25},{17,1},{25,9},{2,18},{10... | collective-permute-start | bytes 884744 | tf_op jit(solution)/shard_map/ppermute | solution.py:19
  20.0 14.4 %collective-permute-start.11 = (bf16[192,768]{1,0:T(8,128)(2,1)}, bf16[192,768]{1,0:T(8,128)(2,1)}, u32[]{:S(2)}, u32[]{:S(2)}) collective-permute-start(bf16[192,768]{1,0:T(8,128)(2,1)} %get-tuple-element.189), channel_id=1, source_target_pairs={{0,24},{8,16},{16,8},{24,0},{1,25},{9,17},{17,9},{25,1},{2,26},{10... | collective-permute-start | bytes 884744 | tf_op jit(solution)/shard_map/ppermute | solution.py:19
  22.2 12.2 %collective-permute-start.9 = (bf16[192,768]{1,0:T(8,128)(2,1)}, bf16[192,768]{1,0:T(8,128)(2,1)}, u32[]{:S(2)}, u32[]{:S(2)}) collective-permute-start(bf16[192,768]{1,0:T(8,128)(2,1)} %get-tuple-element.191), channel_id=1, source_target_pairs={{0,8},{8,0},{16,24},{24,16},{1,9},{9,1},{17,25},{25,17},{2,10},{10... | collective-permute-start | bytes 884744 | tf_op jit(solution)/shard_map/ppermute | solution.py:19
  37.8 7.2 %collective-permute-start.14 = (bf16[128,768]{1,0:T(8,128)(2,1)S(1)}, bf16[128,768]{1,0:T(8,128)(2,1)S(1)}, u32[]{:S(2)}, u32[]{:S(2)}) collective-permute-start(bf16[128,768]{1,0:T(8,128)(2,1)S(1)} %add_convert_fusion.4), channel_id=1, source_target_pairs={{0,16},{8,24},{16,0},{24,8},{1,17},{9,25},{17,1},{25,9},{2,18},{10... | collective-permute-start | bytes 589832 | tf_op jit(solution)/shard_map/ppermute | solution.py:19
  46.6 6.4 %collective-permute-start.16 = (bf16[128,768]{1,0:T(8,128)(2,1)S(1)}, bf16[128,768]{1,0:T(8,128)(2,1)S(1)}, u32[]{:S(2)}, u32[]{:S(2)}) collective-permute-start(bf16[128,768]{1,0:T(8,128)(2,1)S(1)} %fusion.24.own), channel_id=1, source_target_pairs={{0,16},{8,24},{16,0},{24,8},{1,17},{9,25},{17,1},{25,9},{2,18},{10... | collective-permute-start | bytes 589832 | tf_op jit(solution)/shard_map/ppermute | solution.py:19
  46.9 6.1 %collective-permute-start.15 = (bf16[128,768]{1,0:T(8,128)(2,1)S(1)}, bf16[128,768]{1,0:T(8,128)(2,1)S(1)}, u32[]{:S(2)}, u32[]{:S(2)}) collective-permute-start(bf16[128,768]{1,0:T(8,128)(2,1)S(1)} %fusion.24.own), channel_id=1, source_target_pairs={{0,8},{8,0},{16,24},{24,16},{1,9},{9,1},{17,25},{25,17},{2,10},{10... | collective-permute-start | bytes 589832 | tf_op jit(solution)/shard_map/ppermute | solution.py:19
  64.2 7.0 %collective-permute-start.20 = (bf16[128,768]{1,0:T(8,128)(2,1)S(1)}, bf16[128,768]{1,0:T(8,128)(2,1)S(1)}, u32[]{:S(2)}, u32[]{:S(2)}) collective-permute-start(bf16[128,768]{1,0:T(8,128)(2,1)S(1)} %add_convert_fusion.3), channel_id=1, source_target_pairs={{0,16},{8,24},{16,0},{24,8},{1,17},{9,25},{17,1},{25,9},{2,18},{10... | collective-permute-start | bytes 589832 | tf_op jit(solution)/shard_map/ppermute | solution.py:19
  73.3 6.2 %collective-permute-start.22 = (bf16[128,768]{1,0:T(8,128)(2,1)S(1)}, bf16[128,768]{1,0:T(8,128)(2,1)S(1)}, u32[]{:S(2)}, u32[]{:S(2)}) collective-permute-start(bf16[128,768]{1,0:T(8,128)(2,1)S(1)} %get-tuple-element.176), channel_id=1, source_target_pairs={{0,16},{8,24},{16,0},{24,8},{1,17},{9,25},{17,1},{25,9},{2,18},{10... | collective-permute-start | bytes 589832 | tf_op jit(solution)/shard_map/ppermute | solution.py:19
  73.7 5.8 %collective-permute-start.21 = (bf16[128,768]{1,0:T(8,128)(2,1)S(1)}, bf16[128,768]{1,0:T(8,128)(2,1)S(1)}, u32[]{:S(2)}, u32[]{:S(2)}) collective-permute-start(bf16[128,768]{1,0:T(8,128)(2,1)S(1)} %get-tuple-element.176), channel_id=1, source_target_pairs={{0,8},{8,0},{16,24},{24,16},{1,9},{9,1},{17,25},{25,17},{2,10},{10... | collective-permute-start | bytes 589832 | tf_op jit(solution)/shard_map/ppermute | solution.py:19
  83.2 6.3 %collective-permute-start.24 = (bf16[128,768]{1,0:T(8,128)(2,1)S(1)}, bf16[128,768]{1,0:T(8,128)(2,1)S(1)}, u32[]{:S(2)}, u32[]{:S(2)}) collective-permute-start(bf16[128,768]{1,0:T(8,128)(2,1)S(1)} %get-tuple-element.197), channel_id=1, source_target_pairs={{0,8},{8,0},{16,24},{24,16},{1,9},{9,1},{17,25},{25,17},{2,10},{10... | collective-permute-start | bytes 589832 | tf_op jit(solution)/shard_map/ppermute | solution.py:19
  84.5 15.4 %collective-permute-start.30 = (bf16[1,384,768]{2,1,0:T(8,128)(2,1)S(1)}, bf16[1,384,768]{2,1,0:T(8,128)(2,1)S(1)}, u32[]{:S(2)}, u32[]{:S(2)}) collective-permute-start(bf16[1,384,768]{2,1,0:T(8,128)(2,1)S(1)} %dynamic-slice_bitcast_fusion), channel_id=1, source_target_pairs={{0,1},{1,0},{2,3},{3,2},{4,5},{5,4},{6,7},{7,6},{8,9},{9,8},{10,11... | collective-permute-start | bytes 1769480 | tf_op jit(solution)/shard_map/ppermute | solution.py:23
  86.2 6.7 %collective-permute-start.26 = (bf16[128,768]{1,0:T(8,128)(2,1)S(1)}, bf16[128,768]{1,0:T(8,128)(2,1)S(1)}, u32[]{:S(2)}, u32[]{:S(2)}) collective-permute-start(bf16[128,768]{1,0:T(8,128)(2,1)S(1)} %fusion.21), channel_id=1, source_target_pairs={{0,16},{8,24},{16,0},{24,8},{1,17},{9,25},{17,1},{25,9},{2,18},{10... | collective-permute-start | bytes 589832 | tf_op jit(solution)/shard_map/ppermute | solution.py:19
  87.9 15.2 %collective-permute-start.31 = (bf16[4,96,768]{2,1,0:T(8,128)(2,1)S(1)}, bf16[4,96,768]{2,1,0:T(8,128)(2,1)S(1)}, u32[]{:S(2)}, u32[]{:S(2)}) collective-permute-start(bf16[4,96,768]{2,1,0:T(8,128)(2,1)S(1)} %constant_dynamic-slice_fusion.2), channel_id=1, source_target_pairs={{0,2},{1,3},{2,0},{3,1},{4,6},{5,7},{6,4},{7,5},{8,10},{9,11},{10,... | collective-permute-start | bytes 1769480 | tf_op jit(solution)/shard_map/ppermute | solution.py:23
  94.9 5.8 %collective-permute-start.28 = (bf16[128,768]{1,0:T(8,128)(2,1)S(1)}, bf16[128,768]{1,0:T(8,128)(2,1)S(1)}, u32[]{:S(2)}, u32[]{:S(2)}) collective-permute-start(bf16[128,768]{1,0:T(8,128)(2,1)S(1)} %get-tuple-element.178), channel_id=1, source_target_pairs={{0,16},{8,24},{16,0},{24,8},{1,17},{9,25},{17,1},{25,9},{2,18},{10... | collective-permute-start | bytes 589832 | tf_op jit(solution)/shard_map/ppermute | solution.py:19
  96.6 8.3 %collective-permute-start.27 = (bf16[128,768]{1,0:T(8,128)(2,1)S(1)}, bf16[128,768]{1,0:T(8,128)(2,1)S(1)}, u32[]{:S(2)}, u32[]{:S(2)}) collective-permute-start(bf16[128,768]{1,0:T(8,128)(2,1)S(1)} %get-tuple-element.178), channel_id=1, source_target_pairs={{0,8},{8,0},{16,24},{24,16},{1,9},{9,1},{17,25},{25,17},{2,10},{10... | collective-permute-start | bytes 589832 | tf_op jit(solution)/shard_map/ppermute | solution.py:19
  101.5 11.3 %collective-permute-start.36 = (bf16[1,192,768]{2,1,0:T(8,128)(2,1)}, bf16[1,192,768]{2,1,0:T(8,128)(2,1)}, u32[]{:S(2)}, u32[]{:S(2)}) collective-permute-start(bf16[1,192,768]{2,1,0:T(8,128)(2,1)} %fusion.11), channel_id=1, source_target_pairs={{0,2},{1,3},{2,0},{3,1},{4,6},{5,7},{6,4},{7,5},{8,10},{9,11},{10,... | collective-permute-start | bytes 884744 | tf_op jit(solution)/shard_map/ppermute | solution.py:23
  104.0 10.6 %collective-permute-start.37 = (bf16[4,48,768]{2,1,0:T(8,128)(2,1)}, bf16[4,48,768]{2,1,0:T(8,128)(2,1)}, u32[]{:S(2)}, u32[]{:S(2)}) collective-permute-start(bf16[4,48,768]{2,1,0:T(8,128)(2,1)} %add_convert_fusion), channel_id=1, source_target_pairs={{0,1},{1,0},{2,3},{3,2},{4,5},{5,4},{6,7},{7,6},{8,9},{9,8},{10,11... | collective-permute-start | bytes 884744 | tf_op jit(solution)/shard_map/ppermute | solution.py:23
  110.5 10.6 %collective-permute-start.34 = (bf16[4,96,384]{2,1,0:T(8,128)(2,1)}, bf16[4,96,384]{2,1,0:T(8,128)(2,1)}, u32[]{:S(2)}, u32[]{:S(2)}) collective-permute-start(bf16[4,96,384]{2,1,0:T(8,128)(2,1)} %get-tuple-element.124), channel_id=1, source_target_pairs={{0,2},{1,3},{2,0},{3,1},{4,6},{5,7},{6,4},{7,5},{8,10},{9,11},{10,... | collective-permute-start | bytes 884744 | tf_op jit(solution)/shard_map/ppermute | solution.py:23
  112.1 9.0 %collective-permute-start.35 = (bf16[4,96,384]{2,1,0:T(8,128)(2,1)S(1)}, bf16[4,96,384]{2,1,0:T(8,128)(2,1)S(1)}, u32[]{:S(2)}, u32[]{:S(2)}) collective-permute-start(bf16[4,96,384]{2,1,0:T(8,128)(2,1)S(1)} %get-tuple-element.125), channel_id=1, source_target_pairs={{0,1},{1,0},{2,3},{3,2},{4,5},{5,4},{6,7},{7,6},{8,9},{9,8},{10,11... | collective-permute-start | bytes 884744 | tf_op jit(solution)/shard_map/ppermute | solution.py:23
  116.4 10.4 %collective-permute-start.56 = (bf16[4,24,768]{2,1,0:T(8,128)(2,1)}, bf16[4,24,768]{2,1,0:T(8,128)(2,1)S(1)}, u32[]{:S(2)}, u32[]{:S(2)}) collective-permute-start(bf16[4,24,768]{2,1,0:T(8,128)(2,1)} %add_convert_fusion.8), channel_id=1, source_target_pairs={{0,4},{1,5},{2,6},{3,7},{4,0},{5,1},{6,2},{7,3},{8,12},{9,13},{10,... | collective-permute-start | bytes 442376 | tf_op jit(solution)/shard_map/ppermute | solution.py:23
  122.2 7.0 %collective-permute-start.40 = (bf16[4,48,384]{2,1,0:T(8,128)(2,1)S(1)}, bf16[4,48,384]{2,1,0:T(8,128)(2,1)}, u32[]{:S(2)}, u32[]{:S(2)}) collective-permute-start(bf16[4,48,384]{2,1,0:T(8,128)(2,1)S(1)} %add_convert_fusion.6), channel_id=1, source_target_pairs={{0,1},{1,0},{2,3},{3,2},{4,5},{5,4},{6,7},{7,6},{8,9},{9,8},{10,11... | collective-permute-start | bytes 442376 | tf_op jit(solution)/shard_map/ppermute | solution.py:23
  126.3 6.0 %collective-permute-start.33 = (bf16[144,768]{1,0:T(8,128)(2,1)S(1)}, bf16[144,768]{1,0:T(8,128)(2,1)S(1)}, u32[]{:S(2)}, u32[]{:S(2)}) collective-permute-start(bf16[144,768]{1,0:T(8,128)(2,1)S(1)} %get-tuple-element.122), channel_id=1, source_target_pairs={{0,8},{8,0},{16,24},{24,16},{1,9},{9,1},{17,25},{25,17},{2,10},{10... | collective-permute-start | bytes 663560 | tf_op jit(solution)/shard_map/ppermute | solution.py:19
  126.3 65.1 %collective-permute-start.32 = (bf16[128,768]{1,0:T(8,128)(2,1)}, bf16[128,768]{1,0:T(8,128)(2,1)}, u32[]{:S(2)}, u32[]{:S(2)}) collective-permute-start(bf16[128,768]{1,0:T(8,128)(2,1)} %get-tuple-element.119), channel_id=1, source_target_pairs={{0,8},{8,0},{16,24},{24,16},{1,9},{9,1},{17,25},{25,17},{2,10},{10... | collective-permute-start | bytes 589832 | tf_op jit(solution)/shard_map/ppermute | solution.py:19
  126.8 9.9 %collective-permute-start.48 = (bf16[1,96,768]{2,1,0:T(8,128)(2,1)S(1)}, bf16[1,96,768]{2,1,0:T(8,128)(2,1)S(1)}, u32[]{:S(2)}, u32[]{:S(2)}) collective-permute-start(bf16[1,96,768]{2,1,0:T(8,128)(2,1)S(1)} %copy-done.47), channel_id=1, source_target_pairs={{0,4},{1,5},{2,6},{3,7},{4,0},{5,1},{6,2},{7,3},{8,12},{9,13},{10,... | collective-permute-start | bytes 442376 | tf_op jit(solution)/shard_map/ppermute | solution.py:23
  130.4 8.0 %collective-permute-start.57 = (bf16[24,768]{1,0:T(8,128)(2,1)S(1)}, bf16[24,768]{1,0:T(8,128)(2,1)S(1)}, u32[]{:S(2)}, u32[]{:S(2)}) collective-permute-start(bf16[24,768]{1,0:T(8,128)(2,1)S(1)} %get-tuple-element.221), channel_id=1, source_target_pairs={{0,8},{8,0},{16,24},{24,16},{1,9},{9,1},{17,25},{25,17},{2,10},{10... | collective-permute-start | bytes 110600 | tf_op jit(solution)/shard_map/ppermute | solution.py:19
  130.5 8.6 %collective-permute-start.58 = (bf16[24,768]{1,0:T(8,128)(2,1)S(1)}, bf16[24,768]{1,0:T(8,128)(2,1)S(1)}, u32[]{:S(2)}, u32[]{:S(2)}) collective-permute-start(bf16[24,768]{1,0:T(8,128)(2,1)S(1)} %get-tuple-element.220), channel_id=1, source_target_pairs={{0,16},{8,24},{16,0},{24,8},{1,17},{9,25},{17,1},{25,9},{2,18},{10... | collective-permute-start | bytes 110600 | tf_op jit(solution)/shard_map/ppermute | solution.py:19
  132.3 9.1 %collective-permute-start.59 = (bf16[24,768]{1,0:T(8,128)(2,1)S(1)}, bf16[24,768]{1,0:T(8,128)(2,1)S(1)}, u32[]{:S(2)}, u32[]{:S(2)}) collective-permute-start(bf16[24,768]{1,0:T(8,128)(2,1)S(1)} %get-tuple-element.219), channel_id=1, source_target_pairs={{0,24},{8,16},{16,8},{24,0},{1,25},{9,17},{17,9},{25,1},{2,26},{10... | collective-permute-start | bytes 110600 | tf_op jit(solution)/shard_map/ppermute | solution.py:19
  136.7 15.4 %collective-permute-start.39 = (bf16[144,768]{1,0:T(8,128)(2,1)S(1)}, bf16[144,768]{1,0:T(8,128)(2,1)S(1)}, u32[]{:S(2)}, u32[]{:S(2)}) collective-permute-start(bf16[144,768]{1,0:T(8,128)(2,1)S(1)} %get-tuple-element.130), channel_id=1, source_target_pairs={{0,16},{8,24},{16,0},{24,8},{1,17},{9,25},{17,1},{25,9},{2,18},{10... | collective-permute-start | bytes 663560 | tf_op jit(solution)/shard_map/ppermute | solution.py:19
  138.4 12.1 %collective-permute-start.42 = (bf16[4,24,384]{2,1,0:T(8,128)(2,1)S(1)}, bf16[4,24,384]{2,1,0:T(8,128)(2,1)S(1)}, u32[]{:S(2)}, u32[]{:S(2)}) collective-permute-start(bf16[4,24,384]{2,1,0:T(8,128)(2,1)S(1)} %add_convert_fusion.11), channel_id=1, source_target_pairs={{0,4},{1,5},{2,6},{3,7},{4,0},{5,1},{6,2},{7,3},{8,12},{9,13},{10,... | collective-permute-start | bytes 221192 | tf_op jit(solution)/shard_map/ppermute | solution.py:23
  139.1 13.0 %collective-permute-start.41 = (bf16[4,24,384]{2,1,0:T(8,128)(2,1)S(1)}, bf16[4,24,384]{2,1,0:T(8,128)(2,1)S(1)}, u32[]{:S(2)}, u32[]{:S(2)}) collective-permute-start(bf16[4,24,384]{2,1,0:T(8,128)(2,1)S(1)} %add_convert_fusion.12), channel_id=1, source_target_pairs={{0,4},{1,5},{2,6},{3,7},{4,0},{5,1},{6,2},{7,3},{8,12},{9,13},{10,... | collective-permute-start | bytes 221192 | tf_op jit(solution)/shard_map/ppermute | solution.py:23
  141.4 14.9 %collective-permute-start.49 = (bf16[1,96,768]{2,1,0:T(8,128)(2,1)S(1)}, bf16[1,96,768]{2,1,0:T(8,128)(2,1)S(1)}, u32[]{:S(2)}, u32[]{:S(2)}) collective-permute-start(bf16[1,96,768]{2,1,0:T(8,128)(2,1)S(1)} %fusion.27), channel_id=1, source_target_pairs={{0,4},{1,5},{2,6},{3,7},{4,0},{5,1},{6,2},{7,3},{8,12},{9,13},{10,... | collective-permute-start | bytes 442376 | tf_op jit(solution)/shard_map/ppermute | solution.py:23
  156.3 8.8 %collective-permute-start.60 = (bf16[4,24,768]{2,1,0:T(8,128)(2,1)S(1)}, bf16[4,24,768]{2,1,0:T(8,128)(2,1)S(1)}, u32[]{:S(2)}, u32[]{:S(2)}) collective-permute-start(bf16[4,24,768]{2,1,0:T(8,128)(2,1)S(1)} %pad_maximum_fusion.16), channel_id=1, source_target_pairs={{0,4},{1,5},{2,6},{3,7},{4,0},{5,1},{6,2},{7,3},{8,12},{9,13},{10,... | collective-permute-start | bytes 442376 | tf_op jit(solution)/shard_map/ppermute | solution.py:23
  156.4 16.2 %collective-permute-start.50 = (bf16[1,192,768]{2,1,0:T(8,128)(2,1)S(1)}, bf16[1,192,768]{2,1,0:T(8,128)(2,1)S(1)}, u32[]{:S(2)}, u32[]{:S(2)}) collective-permute-start(bf16[1,192,768]{2,1,0:T(8,128)(2,1)S(1)} %pad_maximum_fusion.8), channel_id=1, source_target_pairs={{0,2},{1,3},{2,0},{3,1},{4,6},{5,7},{6,4},{7,5},{8,10},{9,11},{10,... | collective-permute-start | bytes 884744 | tf_op jit(solution)/shard_map/ppermute | solution.py:23
  159.3 14.2 %collective-permute-start.47 = (bf16[128,384]{1,0:T(8,128)(2,1)S(1)}, bf16[128,384]{1,0:T(8,128)(2,1)S(1)}, u32[]{:S(2)}, u32[]{:S(2)}) collective-permute-start(bf16[128,384]{1,0:T(8,128)(2,1)S(1)} %pad_maximum_fusion.20), channel_id=1, source_target_pairs={{0,4},{1,5},{2,6},{3,7},{4,0},{5,1},{6,2},{7,3},{8,12},{9,13},{10,... | collective-permute-start | bytes 294920 | tf_op jit(solution)/shard_map/ppermute | solution.py:23
  159.8 13.7 %collective-permute-start.46 = (bf16[4,24,384]{2,1,0:T(8,128)(2,1)S(1)}, bf16[4,24,384]{2,1,0:T(8,128)(2,1)S(1)}, u32[]{:S(2)}, u32[]{:S(2)}) collective-permute-start(bf16[4,24,384]{2,1,0:T(8,128)(2,1)S(1)} %pad_maximum_fusion.21), channel_id=1, source_target_pairs={{0,4},{1,5},{2,6},{3,7},{4,0},{5,1},{6,2},{7,3},{8,12},{9,13},{10,... | collective-permute-start | bytes 221192 | tf_op jit(solution)/shard_map/ppermute | solution.py:23
  165.1 10.2 %collective-permute-start.61 = (bf16[4,48,768]{2,1,0:T(8,128)(2,1)S(1)}, bf16[4,48,768]{2,1,0:T(8,128)(2,1)S(1)}, u32[]{:S(2)}, u32[]{:S(2)}) collective-permute-start(bf16[4,48,768]{2,1,0:T(8,128)(2,1)S(1)} %pad_maximum_fusion.11), channel_id=1, source_target_pairs={{0,1},{1,0},{2,3},{3,2},{4,5},{5,4},{6,7},{7,6},{8,9},{9,8},{10,11... | collective-permute-start | bytes 884744 | tf_op jit(solution)/shard_map/ppermute | solution.py:23
  172.8 20.3 %collective-permute-start.55 = (bf16[1,384,768]{2,1,0:T(8,128)(2,1)S(1)}, bf16[1,384,768]{2,1,0:T(8,128)(2,1)S(1)}, u32[]{:S(2)}, u32[]{:S(2)}) collective-permute-start(bf16[1,384,768]{2,1,0:T(8,128)(2,1)S(1)} %get-tuple-element.204), channel_id=1, source_target_pairs={{0,1},{1,0},{2,3},{3,2},{4,5},{5,4},{6,7},{7,6},{8,9},{9,8},{10,11... | collective-permute-start | bytes 1769480 | tf_op jit(solution)/shard_map/ppermute | solution.py:23
  173.6 16.8 %collective-permute-start.51 = (bf16[4,48,384]{2,1,0:T(8,128)(2,1)S(1)}, bf16[4,48,384]{2,1,0:T(8,128)(2,1)S(1)}, u32[]{:S(2)}, u32[]{:S(2)}) collective-permute-start(bf16[4,48,384]{2,1,0:T(8,128)(2,1)S(1)} %pad_maximum_fusion.14), channel_id=1, source_target_pairs={{0,1},{1,0},{2,3},{3,2},{4,5},{5,4},{6,7},{7,6},{8,9},{9,8},{10,11... | collective-permute-start | bytes 442376 | tf_op jit(solution)/shard_map/ppermute | solution.py:23
  175.3 15.1 %collective-permute-start.53 = (bf16[224,384]{1,0:T(8,128)(2,1)S(1)}, bf16[224,384]{1,0:T(8,128)(2,1)S(1)}, u32[]{:S(2)}, u32[]{:S(2)}) collective-permute-start(bf16[224,384]{1,0:T(8,128)(2,1)S(1)} %pad_maximum_fusion.13), channel_id=1, source_target_pairs={{0,2},{1,3},{2,0},{3,1},{4,6},{5,7},{6,4},{7,5},{8,10},{9,11},{10,... | collective-permute-start | bytes 516104 | tf_op jit(solution)/shard_map/ppermute | solution.py:23
  175.5 19.7 %collective-permute-start.62 = (bf16[4,96,768]{2,1,0:T(8,128)(2,1)S(1)}, bf16[4,96,768]{2,1,0:T(8,128)(2,1)S(1)}, u32[]{:S(2)}, u32[]{:S(2)}) collective-permute-start(bf16[4,96,768]{2,1,0:T(8,128)(2,1)S(1)} %pad_maximum_fusion.6.held), channel_id=1, source_target_pairs={{0,2},{1,3},{2,0},{3,1},{4,6},{5,7},{6,4},{7,5},{8,10},{9,11},{10,... | collective-permute-start | bytes 1769480 | tf_op jit(solution)/shard_map/ppermute | solution.py:23
  190.6 8.5 %collective-permute-start.54 = (bf16[416,384]{1,0:T(8,128)(2,1)S(1)}, bf16[416,384]{1,0:T(8,128)(2,1)S(1)}, u32[]{:S(2)}, u32[]{:S(2)}) collective-permute-start(bf16[416,384]{1,0:T(8,128)(2,1)S(1)} %pad_maximum_fusion.7), channel_id=1, source_target_pairs={{0,1},{1,0},{2,3},{3,2},{4,5},{5,4},{6,7},{7,6},{8,9},{9,8},{10,11... | collective-permute-start | bytes 958472 | tf_op jit(solution)/shard_map/ppermute | solution.py:23
  191.3 7.8 %collective-permute-start.52 = (bf16[4,96,384]{2,1,0:T(8,128)(2,1)S(1)}, bf16[4,96,384]{2,1,0:T(8,128)(2,1)S(1)}, u32[]{:S(2)}, u32[]{:S(2)}) collective-permute-start(bf16[4,96,384]{2,1,0:T(8,128)(2,1)S(1)} %pad_maximum_fusion.9.held_one), channel_id=1, source_target_pairs={{0,2},{1,3},{2,0},{3,1},{4,6},{5,7},{6,4},{7,5},{8,10},{9,11},{10,... | collective-permute-start | bytes 884744 | tf_op jit(solution)/shard_map/ppermute | solution.py:23
  (64 other events, 279.2 us)
